TPU v7x, 32 devices: a whole 2x2x4 slice. The times are simulated.
32 devices in a mesh: dp: 8 (over y, x, core), fsdp: 4 (over z).
Axes of the slice: x: 2, y: 2, z: 4, core: 2. Of those that a mesh axis runs over, the one named last changes fastest.
Arguments:
- tokens: bfloat16 [64, 512, 768], P(('dp', 'fsdp')), may hold values from -6 to 6
- segment_ids: int32 [64, 512], P(('dp', 'fsdp')), may hold values from 0 to 3, never falling along the last dimension, each value on 1 to 256 neighbouring positions
- bucket_ids: int32 [64, 512, 8], P(('dp', 'fsdp')), may hold values from 0 to 16383
- cotangent: bfloat16 [64, 512, 768], P(('dp', 'fsdp')), may hold values from -6 to 6
- qkv_weight: bfloat16 [768, 2304], P(('dp', 'fsdp')), may hold values from -0.21875 to 0.21875
- out_weight: bfloat16 [768, 768], P(('dp', 'fsdp')), may hold values from -1.75 to 1.75
- up_weight: bfloat16 [768, 3072], P(('dp', 'fsdp')), may hold values from -0.21875 to 0.21875
- down_weight: bfloat16 [3072, 768], P(('dp', 'fsdp')), may hold values from -0.21875 to 0.21875
- attn_gain: bfloat16 [768], P(('dp', 'fsdp')), may hold values from 0.25 to 1.75
- attn_bias: bfloat16 [768], P(('dp', 'fsdp')), may hold values from -3 to 3
- ffn_gain: bfloat16 [768], P(('dp', 'fsdp')), may hold values from 0.25 to 1.75
- ffn_bias: bfloat16 [768], P(('dp', 'fsdp')), may hold values from -3 to 3
Outputs:
- layer_output: bfloat16 [64, 512, 768], P(('dp', 'fsdp'))
- tokens_grad: bfloat16 [64, 512, 768], P(('dp', 'fsdp'))
- qkv_grad: float32 [768, 2304], P(('dp', 'fsdp'))
- out_grad: float32 [768, 768], P(('dp', 'fsdp'))
- up_grad: float32 [768, 3072], P(('dp', 'fsdp'))
- down_grad: float32 [3072, 768], P(('dp', 'fsdp'))
- attn_gain_grad: float32 [768], P(('dp', 'fsdp'))
- attn_bias_grad: float32 [768], P(('dp', 'fsdp'))
- ffn_gain_grad: float32 [768], P(('dp', 'fsdp'))
- ffn_bias_grad: float32 [768], P(('dp', 'fsdp'))
- bucket_counts: int32 [8, 16384], replicated
Inputs may be any that keep to these rules, and one draw needn't show every extreme that they name: `segment_ids`: within each packed row the numbers never fall and start at 0; a document has at most 256 molecules.
All inputs are finite; a program needn't handle non-finite values.
Results may differ from a plain program's by a relative error of at most 0.014.
Values may be sent and summed in bfloat16 or wider, within the bound.
No kernel may reach another device: no remote copies, remote signals or barrier semaphores. Data moves between devices by JAX's collectives and lax.ppermute only.
A program may use at most 192 MiB of HBM per device.

v0:
```python
import functools

import jax
import jax.numpy as jnp
from jax import lax
from jax.experimental import pallas as pl
from jax.experimental.pallas import tpu as pltpu
from jax.sharding import PartitionSpec as P

H = 12
BUCKETS = 16384
LOW = 256
BLOCKS = 8
CORE, NEAR_X, NEAR_Y = 1, 2, 4
PLACES = (0, NEAR_X, NEAR_Y, NEAR_X + NEAR_Y)
BOTH = ("dp", "fsdp")


def swap(value, bit):
    return lax.ppermute(value, "dp", [(i, i ^ bit) for i in range(BLOCKS)])


def swap_inner(value, bit, size):
    return lax.ppermute(value, "fsdp", [(i, i ^ bit) for i in range(size)])


def by_bits(parts, index):
    bit = 1
    while bit < len(parts):
        odd = (index & bit) != 0
        parts = [jnp.where(odd, parts[j ^ bit], parts[j]) for j in range(len(parts))]
        bit *= 2
    return parts


def direct(ranks, inner):
    return ranks == BLOCKS and inner & (inner - 1) == 0


def gather_whole(shard):
    near = lax.all_gather(shard, "fsdp", axis=0, tiled=True)
    whole = lax.all_gather(near, "dp", axis=0, tiled=True)
    whole = whole.reshape(4, 2, -1, whole.shape[1])
    return [whole[:, 0], whole[:, 1]], [0, CORE]


def gather_inner(shard, inner):
    parts = [shard] + [swap_inner(shard, k, inner) for k in range(1, inner)]
    return jnp.concatenate(by_bits(parts, lax.axis_index("fsdp")), axis=0)


def gather_sides(own):
    return [own] + [swap(own, bits) for bits in PLACES[1:]]


def with_core(pieces):
    joined = jnp.stack(pieces)
    return [joined, swap(joined, CORE)], [0, CORE]


def after(value, *others):
    return lax.optimization_barrier((value, *others))[0]


def together(values, *others):
    return list(lax.optimization_barrier((*values, *others)))[: len(values)]


def gather_first(shards, inner, counts):
    own = gather_inner(shards[0], inner)
    own, second = together([own, shards[1]])
    sides = gather_sides(own)
    parts = [second] + [swap_inner(second, k, inner) for k in range(1, inner)]
    values = together([*sides, *parts])
    sides, parts = values[:4], values[4:]
    keep, other = halve_tables(counts, CORE)
    own_second = jnp.concatenate(by_bits(parts, lax.axis_index("fsdp")), axis=0)
    first = with_core(sides)
    own_second, third, other = together([own_second, shards[2], other], *first[0])
    parts = [swap_inner(third, k, inner) for k in range(1, inner - 1)]
    return first, gather_sides(own_second), [third] + parts, keep, other


def halve_tables(counts, bit):
    tables = counts.shape[0] // 2
    upper = (lax.axis_index("dp") & bit) != 0
    keep = jnp.where(upper, counts[tables:], counts[:tables])
    send = jnp.where(upper, counts[:tables], counts[tables:])
    return keep, swap(send, bit)


def double_tables(counts, other, bit):
    upper = (lax.axis_index("dp") & bit) != 0
    return jnp.concatenate(
        [jnp.where(upper, other, counts), jnp.where(upper, counts, other)], axis=0
    )


def add(*terms):
    total = terms[0].astype(jnp.float32)
    for term in terms[1:]:
        total = total + term.astype(jnp.float32)
    return total.astype(jnp.bfloat16)


def scatter_core(keep, send):
    other = swap(send, CORE)
    return [add(keep[place], other[place]) for place in range(4)]


def scatter_sides(parts):
    return [swap(part, bits) for part, bits in zip(parts[1:], PLACES[1:])]


def scatter_corner(parts):
    half = parts[3].shape[0] // 2
    return [swap(parts[3][:half], NEAR_Y), swap(parts[3][half:], NEAR_X)]


def scatter_rest(parts, corners):
    half = parts[3].shape[0] // 2
    first, second = corners
    to_x = jnp.concatenate([add(parts[1][:half], first), parts[1][half:]], axis=0)
    to_y = jnp.concatenate([parts[2][:half], add(parts[2][half:], second)], axis=0)
    return [swap(to_x, NEAR_X), swap(to_y, NEAR_Y)]


def scatter_inner(mine, inner):
    part = mine.shape[0] // inner
    parts = [mine[j * part : (j + 1) * part] for j in range(inner)]
    parts = by_bits(parts, lax.axis_index("fsdp"))
    return parts[:1] + [swap_inner(parts[k], k, inner) for k in range(1, inner)]


def sum_parts(parts):
    total = parts[0].astype(jnp.float32)
    for part in parts[1:]:
        total = total + part.astype(jnp.float32)
    return total


def scatter_whole(keep, send):
    whole = jnp.stack([keep, send], axis=1).reshape(-1, keep.shape[2])
    near = lax.psum_scatter(whole, "dp", scatter_dimension=0, tiled=True)
    return lax.psum_scatter(near, "fsdp", scatter_dimension=0, tiled=True).astype(jnp.float32)


def piece_pairs(refs, plan, me, block, target, sems, column=0):
    pairs = []
    for ref, first in zip(refs, plan):
        for place, bits in enumerate(PLACES):
            start = pl.multiple_of((me ^ first ^ bits) * block, 16)
            pairs.append(
                (
                    ref.at[place, :, column : column + target.shape[1]],
                    target.at[pl.ds(start, block), :],
                    sems.at[len(pairs)],
                )
            )
    return pairs


def load_pieces(*details):
    copies = [pltpu.make_async_copy(*pair) for pair in piece_pairs(*details)]
    for copy in copies:
        copy.start()
    return copies


def count_kernel(ids_ref, counts_ref):
    _, high_count, low_count = counts_ref.shape
    tables, length = ids_ref.shape
    high_at = lax.broadcasted_iota(jnp.int32, (high_count, length), 0)
    low_at = lax.broadcasted_iota(jnp.int32, (low_count, length), 0)
    for table in range(tables):
        ids = ids_ref[table : table + 1, :]
        upper = lax.shift_right_logical(ids, 8)
        lower = jnp.bitwise_and(ids, low_count - 1)
        counts_ref[table] = dot_nt(
            jnp.where(high_at == upper, 1.0, 0.0).astype(jnp.bfloat16),
            jnp.where(low_at == lower, 1.0, 0.0).astype(jnp.bfloat16),
        ).astype(jnp.int32)


def count_buckets(ids):
    tables = ids.shape[0]
    counts = pl.pallas_call(
        count_kernel,
        out_shape=jax.ShapeDtypeStruct((tables, BUCKETS // LOW, LOW), jnp.int32),
        cost_estimate=pl.CostEstimate(flops=3 * 10**9, bytes_accessed=10**6, transcendentals=0),
    )(ids)
    return counts.reshape(tables, BUCKETS)


def norm_parts(values):
    centered = values - jnp.mean(values, axis=-1, keepdims=True)
    spread = jnp.mean(centered * centered, axis=-1, keepdims=True)
    factor = lax.rsqrt(spread + 1e-12)
    return centered * factor, factor


def dot_nn(first, second):
    return jnp.dot(first, second, preferred_element_type=jnp.float32)


def dot_nt(first, second):
    return lax.dot_general(
        first, second, (((1,), (1,)), ((), ())), preferred_element_type=jnp.float32
    )


def flip_axes(matrix):
    return matrix.T


def attend_kernel(plan, count, me_ref, x_ref, seg_ref, *rest):
    pieces = rest[:count]
    qkv_ref, expo_ref, inv_ref, mixed_ref, ht_ref, o_ref, vec_ref, w_ref, sems = rest[count:]
    length, width = x_ref.shape[1:]
    head_dim = width // H

    @pl.when(pl.program_id(0) == 0)
    def _():
        for copy in load_pieces(pieces, plan, me_ref[0], width // BLOCKS, w_ref, sems):
            copy.wait()
        vec_ref[...] = w_ref[:, 3 * width :].astype(jnp.float32).T[:8]

    normed, _ = norm_parts(x_ref[0].astype(jnp.float32))
    h_one = (normed * vec_ref[0:1] + vec_ref[1:2]).astype(jnp.bfloat16)
    ht_ref[0] = flip_axes(h_one)
    qkv = dot_nn(h_one, w_ref[:, : 3 * width]).astype(jnp.bfloat16)
    qkv_ref[0, :, :width] = qkv[:, :width] * (1.0 / head_dim**0.5)
    qkv_ref[0, :, width:] = qkv[:, width:]
    lane = lax.broadcasted_iota(jnp.int32, (length, 128), 1)
    seg = seg_ref[0]
    key_seg = jnp.where(seg == lane, 1.0, 0.0).astype(jnp.bfloat16)
    query_seg = jnp.where(seg == lane, 0.0, -1e30).astype(jnp.bfloat16)
    for pair in range(H // 2):
        cols = slice(pair * 128, pair * 128 + 128)
        queries = qkv_ref[0, :, cols]
        keys = qkv_ref[0, :, width + pair * 128 : width + pair * 128 + 128]
        values = qkv_ref[0, :, 2 * width + pair * 128 : 2 * width + pair * 128 + 128]
        key_wide = jnp.concatenate([keys, key_seg], axis=1)
        values_t = flip_axes(values)
        parts = []
        for half in range(2):
            inside = (lane < head_dim) if half == 0 else (lane >= head_dim)
            query_half = jnp.where(inside, queries, jnp.zeros_like(queries))
            scores = dot_nt(key_wide, jnp.concatenate([query_half, query_seg], axis=1))
            top = jnp.max(scores, axis=0, keepdims=True)
            expo = jnp.exp(scores - top)
            inverse = 1.0 / jnp.sum(expo, axis=0, keepdims=True)
            expo = expo.astype(jnp.bfloat16)
            expo_ref[0, 2 * pair + half] = expo
            inv_ref[0, 2 * pair + half] = inverse
            out = dot_nn(values_t, expo)
            parts.append(out[half * head_dim : (half + 1) * head_dim] * inverse)
        mixed = jnp.concatenate(parts, axis=0)
        mixed_ref[0, cols, :] = mixed.astype(jnp.bfloat16)
        o_ref[0, :, cols] = mixed.T.astype(jnp.bfloat16)


def whole_spec(shape):
    zeros = (0,) * len(shape)
    return pl.BlockSpec(shape, lambda *_: zeros, pipeline_mode=pl.Buffered(1))


def row_spec(shape):
    rest = (0,) * (len(shape) - 1)
    return pl.BlockSpec((1,) + shape[1:], lambda r, *_: (r,) + rest)


def any_specs(pieces):
    return [pl.BlockSpec(memory_space=pl.ANY) for _ in pieces]


def kernel_params(mebibytes):
    return pltpu.CompilerParams(vmem_limit_bytes=mebibytes * 1024 * 1024)


def attend(tokens, segments, me, pieces, plan):
    rows, length, width = tokens.shape
    shapes = (
        jax.ShapeDtypeStruct((rows, length, 3 * width), jnp.bfloat16),
        jax.ShapeDtypeStruct((rows, H, length, length), jnp.bfloat16),
        jax.ShapeDtypeStruct((rows, H, 1, length), jnp.float32),
        jax.ShapeDtypeStruct((rows, width, length), jnp.bfloat16),
        jax.ShapeDtypeStruct((rows, width, length), jnp.bfloat16),
        jax.ShapeDtypeStruct((rows, length, width), jnp.bfloat16),
        jax.ShapeDtypeStruct((8, width), jnp.float32),
    )
    return list(pl.pallas_call(
        functools.partial(attend_kernel, plan, len(pieces)),
        grid=(rows,),
        in_specs=[
            pl.BlockSpec(memory_space=pltpu.SMEM),
            row_spec(tokens.shape),
            row_spec(segments.shape),
        ]
        + any_specs(pieces),
        out_specs=[row_spec(s.shape) for s in shapes[:-1]] + [whole_spec((8, width))],
        out_shape=shapes,
        scratch_shapes=[
            pltpu.VMEM((width, 3 * width + 128), jnp.bfloat16),
            pltpu.SemaphoreType.DMA((BLOCKS,)),
        ],
        compiler_params=kernel_params(58),
        cost_estimate=pl.CostEstimate(
            flops=10**9, bytes_accessed=10**6, transcendentals=0
        ),
    )(me, tokens, segments, *pieces))


def split_blocks(source, me, block, keep_ref, send_ref):
    for place, bits in enumerate(PLACES):
        start = pl.multiple_of((me ^ bits) * block, 16)
        keep_ref[place] = source[pl.ds(start, block), :].astype(jnp.bfloat16)
        start = pl.multiple_of((me ^ bits ^ CORE) * block, 16)
        send_ref[place] = source[pl.ds(start, block), :].astype(jnp.bfloat16)


def split_shapes(block, columns):
    return [jax.ShapeDtypeStruct((4, block, columns), jnp.bfloat16)] * 2


def forward_kernel(
    plan, count, me_ref, x_ref, o_ref, cot_ref, vec_ref, *rest
):
    pieces = rest[:count]
    (
        y_ref, ht_ref, keep_ref, send_ref, rise_ref, act_ref, h_ref, w_ref, sems,
    ) = rest[count:]
    step = pl.program_id(0)
    width = y_ref.shape[1]
    chunk = act_ref.shape[1]
    hidden = w_ref.shape[1] - width

    @pl.when(step == 0)
    def _():
        for copy in load_pieces(pieces, plan, me_ref[0], width // BLOCKS, w_ref, sems):
            copy.wait()
        y_ref[...] = x_ref[...].astype(jnp.float32) + dot_nn(o_ref[...], w_ref[:, hidden:])
        normed, _ = norm_parts(y_ref[...])
        h_ref[...] = (normed * vec_ref[2:3] + vec_ref[3:4]).astype(jnp.bfloat16)
        ht_ref[...] = flip_axes(h_ref[...])

    span = pl.ds(pl.multiple_of(step * chunk, chunk), chunk)
    slope = (2.0 / 3.141592653589793) ** 0.5
    upper = dot_nn(h_ref[...], w_ref[:, span])
    square = upper * upper
    half = 0.5 + 0.5 * jnp.tanh(upper * (slope + (slope * 0.044715) * square))
    active = upper * half
    inner = (2.0 * slope) + (6.0 * 0.044715 * slope) * square
    rise_ref[...] = (half + active * (1.0 - half) * inner).astype(jnp.bfloat16)
    active = active.astype(jnp.bfloat16)
    act_ref[...] = active
    down_grad = dot_nn(flip_axes(active), cot_ref[...]).astype(jnp.bfloat16)
    block = keep_ref.shape[1]
    for odd in range(2):

        @pl.when((me_ref[0] & 1) == odd)
        def _():
            keep_ref[0] = down_grad[odd * block : (odd + 1) * block]
            send_ref[0] = down_grad[(1 - odd) * block : (2 - odd) * block]


def feed_forward(tokens, mixed, cotangent, vec, me, pieces, plan):
    count, width = cotangent.shape
    hidden = pieces[0].shape[2] - width
    chunk = hidden // 4
    shapes = (
        jax.ShapeDtypeStruct((count, width), jnp.float32),
        jax.ShapeDtypeStruct((width, count), jnp.bfloat16),
        *split_shapes(hidden // BLOCKS, width),
        jax.ShapeDtypeStruct((count, hidden), jnp.bfloat16),
        jax.ShapeDtypeStruct((count, hidden), jnp.bfloat16),
    )
    half_spec = pl.BlockSpec((1, hidden // BLOCKS, width), lambda j, me: (j ^ (me[0] // 2), 0, 0))
    return pl.pallas_call(
        functools.partial(forward_kernel, plan, len(pieces)),
        grid_spec=pltpu.PrefetchScalarGridSpec(
            num_scalar_prefetch=1,
            grid=(hidden // chunk,),
            in_specs=[whole_spec((count, width))] * 3
            + [whole_spec(vec.shape)]
            + any_specs(pieces),
            out_specs=[whole_spec(s.shape) for s in shapes[:2]]
            + [half_spec] * 2
            + [pl.BlockSpec((count, chunk), lambda j, me: (0, j))] * 2,
            scratch_shapes=[
                pltpu.VMEM((count, width), jnp.bfloat16),
                pltpu.VMEM((width, hidden + width), jnp.bfloat16),
                pltpu.SemaphoreType.DMA((BLOCKS,)),
            ],
        ),
        out_shape=shapes,
        compiler_params=kernel_params(60),
        cost_estimate=pl.CostEstimate(flops=10**9, bytes_accessed=10**6, transcendentals=0),
    )(me, tokens, mixed, cotangent, vec, *pieces)


def norm_back(back, normed, factor, gain):
    scaled = back * gain
    inner = scaled - jnp.mean(scaled, axis=-1, keepdims=True)
    inner = inner - normed * jnp.mean(scaled * normed, axis=-1, keepdims=True)
    gain_grad = jnp.sum(back * normed, axis=0, keepdims=True)
    return factor * inner, gain_grad, jnp.sum(back, axis=0, keepdims=True)


def return_kernel(
    plan, count, plan_down, count_down, me_ref, y_ref, cot_ref, vec_ref, ht_ref, mixed_ref,
    rise_ref, act_ref, *rest
):
    pieces = rest[:count]
    down_pieces = rest[count : count + count_down]
    (
        grad_ref, out_ref, keep_ref, send_ref, sums_ref,
        acc_ref, du_ref, w_ref, wd_ref, part_ref, out_grad_ref, sems, down_sems,
    ) = rest[count + count_down :]
    step = pl.program_id(0)
    width = y_ref.shape[1]
    chunk = act_ref.shape[1]
    block = width // BLOCKS
    copies = [
        pltpu.make_async_copy(*pair)
        for pair in piece_pairs(pieces, plan, me_ref[0], block, w_ref, sems)
    ]

    @pl.when(step == 0)
    def _():
        down_copies = load_pieces(
            down_pieces, plan_down, me_ref[0], wd_ref.shape[0] // BLOCKS, wd_ref, down_sems
        )
        for copy in copies:
            copy.start()
        acc_ref[...] = y_ref[...]
        out_grad_ref[...] = jnp.zeros_like(out_grad_ref)
        sums_ref[...] = jnp.zeros_like(sums_ref)
        for copy in down_copies:
            copy.wait()

    @pl.when(step < pl.num_programs(0) - 1)
    def _():
        start = pl.multiple_of(step * chunk, chunk)
        down = wd_ref[pl.ds(start, chunk), :]
        grad_upper = (
            dot_nt(cot_ref[...], down) * rise_ref[...].astype(jnp.float32)
        ).astype(jnp.bfloat16)
        du_ref[:, pl.ds(start, chunk)] = grad_upper
        acc_ref[...] += dot_nn(act_ref[...], down)
        part_ref[...] = dot_nn(ht_ref[...], grad_upper)
        split_blocks(part_ref, me_ref[0], block, keep_ref, send_ref)

    @pl.when(step == pl.num_programs(0) - 1)
    def _():
        out_ref[...] = acc_ref[...].astype(jnp.bfloat16)
        for copy in copies:
            copy.wait()
        size = mixed_ref.shape[2]

        def body(place, carry):
            rows = pl.ds(pl.multiple_of(place * size, size), size)
            back = dot_nt(du_ref[rows, :], w_ref[...])
            normed, factor = norm_parts(y_ref[rows, :])
            through, gain_grad, bias_grad = norm_back(back, normed, factor, vec_ref[2:3])
            sums_ref[0:1] += gain_grad
            sums_ref[1:2] += bias_grad
            grad = cot_ref[rows, :].astype(jnp.float32) + through
            grad_ref[rows, :] = grad
            out_grad_ref[...] += dot_nn(mixed_ref[place], grad.astype(jnp.bfloat16))
            return carry

        lax.fori_loop(0, mixed_ref.shape[0], body, 0)
        split_blocks(out_grad_ref, me_ref[0], block, keep_ref, send_ref)


def feed_return(y_one, cotangent, vec, h_t, mixed, rise, active, me, pieces, plan, down_pieces, plan_down):
    count, width = cotangent.shape
    hidden = active.shape[1]
    chunk = hidden // 4
    shapes = (
        jax.ShapeDtypeStruct((count, width), jnp.float32),
        jax.ShapeDtypeStruct((count, width), jnp.bfloat16),
        *split_shapes(width // BLOCKS, hidden + width),
        jax.ShapeDtypeStruct((8, width), jnp.float32),
    )
    return pl.pallas_call(
        functools.partial(
            return_kernel, plan, len(pieces), plan_down, len(down_pieces)
        ),
        grid=(hidden // chunk + 1,),
        in_specs=[pl.BlockSpec(memory_space=pltpu.SMEM)]
        + [whole_spec(v.shape) for v in (y_one, cotangent, vec, h_t, mixed)]
        + [
            pl.BlockSpec((count, chunk), lambda j: (0, jnp.minimum(j, 3))),
            pl.BlockSpec((count, chunk), lambda j: (0, jnp.minimum(j, 3))),
        ]
        + any_specs(pieces)
        + any_specs(down_pieces),
        out_specs=[whole_spec(s.shape) for s in shapes[:2]]
        + [pl.BlockSpec((4, width // BLOCKS, width), lambda j: (0, 0, j))] * 2
        + [whole_spec((8, width))],
        out_shape=shapes,
        scratch_shapes=[
            pltpu.VMEM((count, width), jnp.float32),
            pltpu.VMEM((count, hidden), jnp.bfloat16),
            pltpu.VMEM((width, hidden), jnp.bfloat16),
            pltpu.VMEM((hidden, width), jnp.bfloat16),
            pltpu.VMEM((width, chunk), jnp.float32),
            pltpu.VMEM((width, width), jnp.float32),
            pltpu.SemaphoreType.DMA((BLOCKS,)),
            pltpu.SemaphoreType.DMA((BLOCKS,)),
        ],
        compiler_params=kernel_params(60),
        cost_estimate=pl.CostEstimate(
            flops=10**9, bytes_accessed=10**6, transcendentals=0
        ),
    )(me, y_one, cotangent, vec, h_t, mixed, rise, active, *pieces, *down_pieces)


def heads_back(queries, keys, values, grads_t, mixed_t, expos, inverses, head_dim):
    length = queries.shape[0]
    lane = lax.broadcasted_iota(jnp.int32, (length, 128), 1)
    inside = lane < head_dim
    one_lane = jnp.where(lane < 2, 1.0, 0.0).astype(jnp.bfloat16)
    pad_rows = jnp.zeros((126, length), jnp.bfloat16)
    gap_rows = jnp.zeros((head_dim, length), jnp.bfloat16)
    keys_t = flip_axes(keys)
    value_wide = jnp.concatenate([values, one_lane], axis=1)
    grad_pair = grads_t.astype(jnp.float32)
    product = grad_pair * mixed_t.astype(jnp.float32)
    spans = [slice(half * head_dim, (half + 1) * head_dim) for half in range(2)]
    scaled = [
        (grad_pair[span] * inverse).astype(jnp.bfloat16)
        for span, inverse in zip(spans, inverses)
    ]
    scaled_pair = jnp.concatenate(scaled, axis=0)
    dv = []
    dk = []
    dq = []
    for half, span in enumerate(spans):
        delta = -jnp.sum(product[span], axis=0, keepdims=True) * inverses[half]
        high = delta.astype(jnp.bfloat16)
        low = (delta - high.astype(jnp.float32)).astype(jnp.bfloat16)
        first = [scaled[0], gap_rows] if half == 0 else [gap_rows, scaled[1]]
        grad_wide = jnp.concatenate(first + [high, low, pad_rows], axis=0)
        expo = expos[half]
        grad_scores = (expo.astype(jnp.float32) * dot_nn(value_wide, grad_wide)).astype(
            jnp.bfloat16
        )
        dv.append(dot_nt(expo, scaled_pair))
        dk.append(dot_nn(grad_scores, queries))
        dq.append(dot_nn(keys_t, grad_scores)[span] * (1.0 / head_dim**0.5))
    return (
        jnp.concatenate(dq, axis=0).T.astype(jnp.bfloat16),
        jnp.where(inside, dk[0], dk[1]).astype(jnp.bfloat16),
        jnp.where(inside, dv[0], dv[1]).astype(jnp.bfloat16),
    )


def backward_kernel(
    plans, counts, groups, first_group, me_ref, grad_ref, q_ref, k_ref, v_ref, expo_ref, inv_ref,
    mixed_ref, ht_ref, *rest
):
    out_pieces, rest = rest[: counts[0]], rest[counts[0] :]
    last = first_group > 0
    if last:
        x_ref, vec_ref, early_ref, ffn_sums_ref, *rest = rest
        qkv_pieces, rest = rest[: counts[1]], rest[counts[1] :]
        tokens_grad_ref, *rest = rest
    else:
        dqkv_ref, *rest = rest
    keep_ref, send_ref, dot_ref, acc_ref, wout_ref, out_sems, *rest = rest
    if last:
        w_ref, vec_acc, sems = rest
    row = pl.program_id(0)
    group = pl.program_id(1)
    length, width = grad_ref.shape[1:]
    head_dim = width // H
    block = width // BLOCKS
    wide = q_ref.shape[2]
    part = wide * groups
    me = me_ref[0]

    @pl.when((row == 0) & (group == 0))
    def _():
        copies = load_pieces(
            out_pieces, plans[0], me, block, wout_ref, out_sems, out_pieces[0].shape[2] - width
        )
        if last:
            copies += load_pieces(qkv_pieces, plans[1], me, block, w_ref, sems)
            vec_acc[...] = jnp.zeros_like(vec_acc)
            vec_acc[2:4] = ffn_sums_ref[0:2]
        acc_ref[...] = jnp.zeros_like(acc_ref)
        for copy in copies:
            copy.wait()

    @pl.when(group == 0)
    def _():
        attn_in = grad_ref[0].astype(jnp.bfloat16)
        weights = wout_ref[first_group * wide : first_group * wide + part, :]
        dot_ref[...] = dot_nt(weights, attn_in).astype(jnp.bfloat16)

    results = []
    for pair in range(wide // 128):
        cols = slice(pair * 128, pair * 128 + 128)
        start = pl.multiple_of(group * wide + pair * 128, 128)
        results.append(
            heads_back(
                q_ref[0, :, cols], k_ref[0, :, cols], v_ref[0, :, cols],
                dot_ref[pl.ds(start, 128), :], mixed_ref[0, cols, :],
                [expo_ref[0, 2 * pair + half] for half in range(2)],
                [inv_ref[0, 2 * pair + half] for half in range(2)],
                head_dim,
            )
        )
    joined = [jnp.concatenate(list(values), axis=1) for values in zip(*results)]
    for place, value in enumerate(joined):
        start = pl.multiple_of(place * part + group * wide, 128)
        acc_ref[:, pl.ds(start, wide)] += dot_nn(ht_ref[0], value)
        if not last:
            dqkv_ref[0, :, pl.ds(start, wide)] = value
    if last:
        before = first_group * wide
        back = None
        for place, value in enumerate(joined):
            old = early_ref[0, :, place * before : (place + 1) * before]
            start = place * width
            term = dot_nt(old, w_ref[:, start : start + before])
            term = term + dot_nt(value, w_ref[:, start + before : start + width])
            back = term if back is None else back + term
        normed, factor = norm_parts(x_ref[0].astype(jnp.float32))
        through, gain_grad, bias_grad = norm_back(back, normed, factor, vec_ref[0:1])
        vec_acc[0:1] += gain_grad
        vec_acc[1:2] += bias_grad
        tokens_grad_ref[0] = (grad_ref[0] + through).astype(jnp.bfloat16)

    @pl.when((row == pl.num_programs(0) - 1) & (group == groups - 1))
    def _():
        if last:
            acc_ref[:, 3 * part :] = vec_acc[...].T
        split_blocks(acc_ref, me, block, keep_ref, send_ref)


def backward(grad_y, saved, me, groups, first_group, out_group, extra=None):
    rows, length, width = grad_y.shape
    qkv, expo, inverse, mixed, h_t = saved
    wide = 256
    heads = wide * H // width
    part = wide * groups
    per = width // wide

    def column_spec(kind):
        return pl.BlockSpec(
            (1, length, wide), lambda r, g: (r, 0, kind * per + first_group + g)
        )

    out_pieces, plan_out = out_group
    inputs = [me, grad_y, qkv, qkv, qkv, expo, inverse, mixed, h_t, *out_pieces]
    in_specs = [
        pl.BlockSpec(memory_space=pltpu.SMEM),
        row_spec(grad_y.shape),
        column_spec(0),
        column_spec(1),
        column_spec(2),
        pl.BlockSpec((1, heads, length, length), lambda r, g: (r, first_group + g, 0, 0)),
        pl.BlockSpec((1, heads, 1, length), lambda r, g: (r, first_group + g, 0, 0)),
        pl.BlockSpec((1, wide, length), lambda r, g: (r, first_group + g, 0)),
        row_spec(h_t.shape),
    ] + any_specs(out_pieces)
    plans = [plan_out]
    counts = [len(out_pieces)]
    if extra is None:
        columns = 3 * part
        shapes = [jax.ShapeDtypeStruct((rows, length, 3 * part), jnp.bfloat16)]
    else:
        columns = 3 * part + 128
        tokens, vec, early, ffn_sums, (pieces, plan) = extra
        inputs += [tokens, vec, early, ffn_sums, *pieces]
        in_specs += [row_spec(tokens.shape), whole_spec(vec.shape)]
        in_specs += [row_spec(early.shape), whole_spec(ffn_sums.shape)] + any_specs(pieces)
        shapes = [jax.ShapeDtypeStruct(tokens.shape, jnp.bfloat16)]
        plans += [plan]
        counts += [len(pieces)]
    out_specs = [row_spec(shapes[0].shape)]
    shapes += split_shapes(width // BLOCKS, columns)
    out_specs += [whole_spec(s.shape) for s in shapes[1:]]
    scratch = [
        pltpu.VMEM((part, length), jnp.bfloat16),
        pltpu.VMEM((width, columns), jnp.float32),
        pltpu.VMEM((width, width), jnp.bfloat16),
        pltpu.SemaphoreType.DMA((BLOCKS,)),
    ]
    if extra is not None:
        scratch += [
            pltpu.VMEM((width, 3 * width), jnp.bfloat16),
            pltpu.VMEM((128, width), jnp.float32),
            pltpu.SemaphoreType.DMA((BLOCKS,)),
        ]
    return pl.pallas_call(
        functools.partial(backward_kernel, plans, counts, groups, first_group),
        grid=(rows, groups),
        in_specs=in_specs,
        out_specs=out_specs,
        out_shape=shapes,
        scratch_shapes=scratch,
        compiler_params=kernel_params(58),
        cost_estimate=pl.CostEstimate(flops=10**9, bytes_accessed=10**6, transcendentals=0),
    )(*inputs)


def layer(ranks, inner, tokens, segment_ids, cotangent, me, front, counts):
    rows, length, width = tokens.shape
    flat_shape = (rows * length, width)
    flat_cot = cotangent.reshape(flat_shape)
    first = front[0]
    near = direct(ranks, inner)
    *saved, o, vec = attend(tokens, segment_ids[:, :, None], me, *first)
    if near:
        _, sides, parts, keep, other = front
        *values, o, other = together([*sides, *parts, o, other])
        sides, parts = values[:4], values[4:]
        parts.append(swap_inner(parts[0], inner - 1, inner))
        own_third = jnp.concatenate(by_bits(parts, lax.axis_index("fsdp")), axis=0)
        second = with_core(sides)
        keep, other = halve_tables(keep + other, NEAR_X)
        own_third, second[0][1] = together([own_third, second[0][1]])
        sides = gather_sides(own_third)
    else:
        second, third = front[1:]
    y_one, h_t, *down_parts, rise, active = feed_forward(
        tokens.reshape(flat_shape), o.reshape(flat_shape), flat_cot, vec, me, *second
    )
    if near:
        *sides, y_one, down_parts[1], other = together([*sides, y_one, down_parts[1], other])
        keep, other = halve_tables(keep + other, NEAR_Y)
        third = with_core(sides)
        down_parts = scatter_core(*down_parts)
        y_one, *down_parts = together([y_one, *down_parts])
        down_received = scatter_sides(down_parts)
    grad_y, layer_output, *up_parts, ffn_sums = feed_return(
        y_one, flat_cot, vec, h_t, saved[3], rise, active, me, *second, *third
    )
    groups = 2
    if near:
        *down_received, up_parts[1], grad_y, other = together(
            [*down_received, up_parts[1], grad_y, other]
        )
        counts = keep + other
        others = [swap_inner(counts, k, inner) for k in range(1, inner)]
        parts = scatter_core(*up_parts)
        down_mine = add(down_parts[0], *down_received)
        *values, grad_y = together([*parts, *others, grad_y])
        parts, others = values[:4], values[4:]
        received = scatter_sides(parts)
        down_inner = scatter_inner(down_mine, inner)
    grad_y = grad_y.reshape(tokens.shape)
    dqkv, *early = backward(grad_y, saved, me, groups, 0, second)
    if near:
        received[0], received[1], dqkv, early[1], *down_inner = together(
            [received[0], received[1], dqkv, early[1], *down_inner]
        )
        counts = sum(others, counts)
        other = swap(counts, NEAR_Y)
        early_parts = scatter_core(*early)
        dqkv, *early_parts = together([dqkv, *early_parts])
        early_received = scatter_sides(early_parts)
    tokens_grad, *late = backward(
        grad_y, saved, me, 1, groups, second, (tokens, vec, dqkv, ffn_sums, first)
    )
    if near:
        *values, tokens_grad, late[1], other = together(
            [*received, *early_received, tokens_grad, late[1], other]
        )
        received, early_received = values[:3], values[3:]
        late_parts = scatter_core(*late)
        up_mine = add(parts[0], *received)
        early_mine = add(early_parts[0], *early_received)
        joined = jnp.concatenate([up_mine, early_mine], axis=1)
        late_received = scatter_sides(late_parts)
        *joined, late_mine = together(
            [*scatter_inner(joined, inner), add(late_parts[0], *late_received)]
        )
        joined_sum = sum_parts(joined)
        up_sum, early_sum = joined_sum[:, : up_mine.shape[1]], joined_sum[:, up_mine.shape[1] :]
        down_sum = sum_parts(down_inner)
        late_sum = sum_parts(scatter_inner(late_mine, inner))
        for bit, following in ((NEAR_Y, NEAR_X), (NEAR_X, CORE), (CORE, None)):
            counts = double_tables(counts, other, bit)
            if following is not None:
                other = swap(counts, following)
    else:
        up_sum, down_sum, early_sum, late_sum = [
            scatter_whole(*v) for v in (up_parts, down_parts, early, late)
        ]
    part = width * groups // 3
    grads = []
    for place in range(3):
        grads.append(early_sum[:, place * part : (place + 1) * part])
        grads.append(late_sum[:, place * (width - part) : (place + 1) * (width - part)])
    hidden = active.shape[1]
    return (
        layer_output.reshape(tokens.shape),
        tokens_grad,
        jnp.concatenate(grads, axis=1),
        up_sum[:, hidden:],
        up_sum[:, :hidden],
        down_sum,
        late_sum[:, 3 * (width - part) :],
        counts,
    )


def per_device(
    ranks,
    inner,
    tokens,
    segment_ids,
    bucket_ids,
    cotangent,
    qkv_weight,
    out_weight,
    up_weight,
    down_weight,
    attn_gain,
    attn_bias,
    ffn_gain,
    ffn_bias,
):
    vectors = jnp.stack([attn_gain, attn_bias, ffn_gain, ffn_bias], axis=1)
    vectors = jnp.pad(vectors, ((0, 0), (0, 124)))
    ids = bucket_ids.reshape(-1, bucket_ids.shape[2]).T
    counts = count_buckets(ids)
    shards = (
        jnp.concatenate([qkv_weight, vectors], axis=1),
        jnp.concatenate([up_weight, out_weight], axis=1),
        down_weight,
    )
    if direct(ranks, inner):
        me = lax.axis_index("dp").reshape(1).astype(jnp.int32)
        front = gather_first(shards, inner, counts)
    else:
        me = jnp.zeros((1,), jnp.int32)
        front = [gather_whole(shard) for shard in shards]
        counts = lax.psum(counts, BOTH)
    *results, vec_sums, counts = layer(
        ranks, inner, tokens, segment_ids, cotangent, me, front, counts
    )
    return (*results, *[vec_sums[:, place] for place in range(4)], counts)


def solution(mesh):
    placed = (
        P(("dp", "fsdp"), None, None),
        P(("dp", "fsdp"), None),
        P(("dp", "fsdp"), None, None),
        P(("dp", "fsdp"), None, None),
        P(("dp", "fsdp"), None),
        P(("dp", "fsdp"), None),
        P(("dp", "fsdp"), None),
        P(("dp", "fsdp"), None),
        P(("dp", "fsdp")),
        P(("dp", "fsdp")),
        P(("dp", "fsdp")),
        P(("dp", "fsdp")),
    )
    return jax.shard_map(
        functools.partial(per_device, mesh.shape["dp"], mesh.shape["fsdp"]),
        mesh=mesh,
        in_specs=placed,
        out_specs=(
            P(("dp", "fsdp"), None, None),
            P(("dp", "fsdp"), None, None),
            P(("dp", "fsdp"), None),
            P(("dp", "fsdp"), None),
            P(("dp", "fsdp"), None),
            P(("dp", "fsdp"), None),
            P(("dp", "fsdp")),
            P(("dp", "fsdp")),
            P(("dp", "fsdp")),
            P(("dp", "fsdp")),
            P(),
        ),
        check_vma=False,
    )
```

profile of v0, /device:TPU:0, one launch (start us, length us, event | category | flops | bytes accessed | tf_op | source)
XLA Modules:
  0.0 292.8 jit_solution(17697052078963788630)
XLA Ops:
  2.4 3.1 %collective-permute-start.2 = (bf16[24,2432]{1,0:T(8,128)(2,1)S(1)}, bf16[24,2432]{1,0:T(8,128)(2,1)S(1)}, u32[]{:S(2)}, u32[]{:S(2)}) collective-permute-start(bf16[24,2432]{1,0:T(8,128)(2,1)S(1)} %fusion.23), channel_id=1, source_target_pairs={{0,1},{1,0},{2,3},{3,2},{4,5},{5,4},{6,7},{7,6},{8,9},{9,8},{10,11... | collective-permute-start | bytes 350216 | tf_op jit(solution)/shard_map/ppermute | solution.py:24
  5.5 2.6 collective-permute-start.1
  9.9 7.4 %collective-permute-done.1 = bf16[24,2432]{1,0:T(8,128)(2,1)S(1)} collective-permute-done((bf16[24,2432]{1,0:T(8,128)(2,1)S(1)}, bf16[24,2432]{1,0:T(8,128)(2,1)S(1)}, u32[]{:S(2)}, u32[]{:S(2)}) %collective-permute-start.1) | collective-permute-done | bytes 116768 | tf_op jit(solution)/shard_map/ppermute | solution.py:24
  17.3 1.0 broadcast_select_fusion.48
  18.4 2.5 collective-permute-start.5
  21.9 2.5 collective-permute-start.8
  25.2 4.8 %collective-permute-done.8 = bf16[24,3840]{1,0:T(8,128)(2,1)S(1)} collective-permute-done((bf16[24,3840]{1,0:T(8,128)(2,1)S(1)}, bf16[24,3840]{1,0:T(8,128)(2,1)S(1)}, u32[]{:S(2)}, u32[]{:S(2)}) %collective-permute-start.8) | collective-permute-done | bytes 184352 | tf_op jit(solution)/shard_map/ppermute | solution.py:24
  30.0 6.5 %collective-permute-start.6 = (bf16[24,3840]{1,0:T(8,128)(2,1)S(1)}, bf16[24,3840]{1,0:T(8,128)(2,1)S(1)}, u32[]{:S(2)}, u32[]{:S(2)}) collective-permute-start(bf16[24,3840]{1,0:T(8,128)(2,1)S(1)} %pad_maximum_fusion.7), channel_id=1, source_target_pairs={{0,1},{1,0},{2,3},{3,2},{4,5},{5,4},{6,7},{7,6},{8,9},{9,8},{10,11... | collective-permute-start | bytes 552968 | tf_op jit(solution)/shard_map/ppermute | solution.py:24
  36.6 2.3 collective-permute-done.7
  38.9 3.4 %collective-permute-done.6 = bf16[24,3840]{1,0:T(8,128)(2,1)S(1)} collective-permute-done((bf16[24,3840]{1,0:T(8,128)(2,1)S(1)}, bf16[24,3840]{1,0:T(8,128)(2,1)S(1)}, u32[]{:S(2)}, u32[]{:S(2)}) %collective-permute-start.6) | collective-permute-done | bytes 184352 | tf_op jit(solution)/shard_map/ppermute | solution.py:24
  43.2 1.3 pad_maximum_fusion.2.rest_0_.rest_6_
  44.6 3.0 %shard_map.203 = s32[8,64,256]{2,1,0:T(8,128)} custom-call(s32[8,1024]{1,0:T(8,128)} %bitcast.92), custom_call_target="tpu_custom_call" | custom-call | flops 3000000000 | bytes 1000000 | tf_op jit(solution)/shard_map/pallas_call | solution.py:187
  47.6 1.1 select_bitcast_fusion
  50.6 2.5 collective-permute-start.13
  54.4 1.1 collective-permute-start.15
  56.3 1.0 copy.33.seg_ref
  57.3 24.4 %shard_map.204 = (bf16[2,512,2304]{2,1,0:T(8,128)(2,1)}, bf16[2,12,512,512]{3,2,1,0:T(8,128)(2,1)}, f32[2,12,1,512]{3,2,1,0:T(1,128)}, bf16[2,768,512]{2,1,0:T(8...) custom-call(s32[1]{0:T(128)} %bitcast.me_ref, ...), custom_call_target="tpu_custom_call" | custom-call | flops 1000000000 | bytes 1000000 | tf_op jit(solution)/shard_map/pallas_call | solution.py:292
  81.8 4.3 %collective-permute-done.12 = bf16[96,3840]{1,0:T(8,128)(2,1)S(1)} collective-permute-done((bf16[96,3840]{1,0:T(8,128)(2,1)S(1)}, bf16[96,3840]{1,0:T(8,128)(2,1)S(1)}, u32[]{:S(2)}, u32[]{:S(2)}) %collective-permute-start.12) | collective-permute-done | bytes 737312 | tf_op jit(solution)/shard_map/ppermute | solution.py:20
  87.0 2.0 pad_maximum_fusion.rest_0_
  89.2 1.4 collective-permute-start.16
  90.8 1.0 add.147
  91.8 5.5 %collective-permute-done.16 = bf16[96,768]{1,0:T(8,128)(2,1)} collective-permute-done((bf16[96,768]{1,0:T(8,128)(2,1)S(1)}, bf16[96,768]{1,0:T(8,128)(2,1)}, u32[]{:S(2)}, u32[]{:S(2)}) %collective-permute-start.16) | collective-permute-done | bytes 147488 | tf_op jit(solution)/shard_map/ppermute | solution.py:24
  97.3 1.1 broadcast_select_fusion.31
  98.5 2.3 collective-permute-start.20
  102.1 1.5 collective-permute-start.21
  103.7 26.8 %shard_map.205 = (f32[1024,768]{1,0:T(8,128)}, bf16[768,1024]{1,0:T(8,128)(2,1)}, bf16[4,384,768]{2,1,0:T(8,128)(2,1)}, bf16[4,384,768]{2,1,0:T(8,128)(2,1)}, bf...) custom-call(s32[1]{0:T(128)} %bitcast.me_ref, bf16[1024,768]{1,0:T(8,128)(2,1)} %bitcast.67, ...), custom_call_target="tpu_custom_call" | custom-call | flops 1000000000 | bytes 1000000 | tf_op jit(solution)/shard_map/pallas_call | solution.py:379
  131.6 7.5 %collective-permute-done.22 = bf16[4,384,768]{2,1,0:T(8,128)(2,1)S(1)} collective-permute-done((bf16[4,384,768]{2,1,0:T(8,128)(2,1)}, bf16[4,384,768]{2,1,0:T(8,128)(2,1)S(1)}, u32[]{:S(2)}, u32[]{:S(2)}) %collective-permute-start.22) | collective-permute-done | bytes 2359328 | tf_op jit(solution)/shard_map/ppermute | solution.py:20
  139.1 1.6 fusion.7
  141.3 1.5 collective-permute-start.25
  142.8 1.4 collective-permute-start.26
  144.3 1.3 collective-permute-start.27
  145.6 1.4 copy-done.4
  147.0 37.5 %shard_map.206 = (f32[1024,768]{1,0:T(8,128)}, bf16[1024,768]{1,0:T(8,128)(2,1)}, bf16[4,96,3840]{2,1,0:T(8,128)(2,1)}, bf16[4,96,3840]{2,1,0:T(8,128)(2,1)}, f32[8,768]{1,0:T(8,128)}) custom-call(s32[1]{0:T(128)} %bitcast.me_ref, f32[1024,768]{1,0:T(8,128)} %get-tuple-element.143.y_ref, bf16[1024,768]{1,0:T(8,128)(2,1)} %bitcast.71, ...), custom_call_target="tpu_custom_call" | custom-call | flops 1000000000 | bytes 1000000 | tf_op jit(solution)/shard_map/pallas_call | solution.py:487
  184.7 1.4 collective-permute-start.31
  186.2 1.1 collective-permute-start.30
  187.3 1.9 collective-permute-start.29
  189.2 1.0 collective-permute-done.28
  190.2 2.6 fusion.3
  192.8 1.2 collective-permute-done.30
  194.0 1.2 collective-permute-start.32
  195.6 1.7 add_convert_fusion.5
  197.4 2.5 collective-permute-start.36
  199.9 2.0 collective-permute-start.35
  201.8 20.3 %shard_map.207 = (bf16[2,512,1536]{2,1,0:T(8,128)(2,1)}, bf16[4,96,1536]{2,1,0:T(8,128)(2,1)}, bf16[4,96,1536]{2,1,0:T(8,128)(2,1)}) custom-call(s32[1]{0:T(128)} %bitcast.me_ref, f32[2,512,768]{2,1,0:T(8,128)} %bitcast.68, bf16[2,512,2304]{2,1,0:T(8,128)(2,1)} %get-tuple-element.166.q_ref.k_ref.v_ref, ...), custom_call_target="tpu_custom_call" | custom-call | flops 1000000000 | bytes 1000000 | tf_op jit(solution)/shard_map/pallas_call | solution.py:700
  222.8 1.5 collective-permute-start.42
  224.4 1.5 collective-permute-start.37
  225.9 1.6 fusion.14
  227.4 1.1 collective-permute-start.39
  228.5 1.0 collective-permute-start.40
  229.5 1.5 collective-permute-start.41
  231.8 25.2 %shard_map.208 = (bf16[2,512,768]{2,1,0:T(8,128)(2,1)}, bf16[4,96,896]{2,1,0:T(8,128)(2,1)}, bf16[4,96,896]{2,1,0:T(8,128)(2,1)}) custom-call(s32[1]{0:T(128)} %bitcast.me_ref, f32[2,512,768]{2,1,0:T(8,128)} %bitcast.69, bf16[2,512,2304]{2,1,0:T(8,128)(2,1)} %get-tuple-element.166.q_ref.k_ref.v_ref, ...), custom_call_target="tpu_custom_call" | custom-call | flops 1000000000 | bytes 1000000 | tf_op jit(solution)/shard_map/pallas_call | solution.py:700
  257.2 1.1 collective-permute-start.53
  259.0 2.4 collective-permute-start.45
  263.6 2.0 collective-permute-start.43
  265.8 1.1 collective-permute-start.47
  267.0 1.6 collective-permute-start.49
  268.6 4.5 %collective-permute-done.47 = bf16[96,896]{1,0:T(8,128)(2,1)S(1)} collective-permute-done((bf16[96,896]{1,0:T(8,128)(2,1)S(1)}, bf16[96,896]{1,0:T(8,128)(2,1)S(1)}, u32[]{:S(2)}, u32[]{:S(2)}) %collective-permute-start.47) | collective-permute-done | bytes 172064 | tf_op jit(solution)/shard_map/ppermute | solution.py:20
  273.1 1.1 collective-permute-start.48
  275.1 1.3 collective-permute-done.49
  276.4 3.6 %collective-permute-done.48 = bf16[96,896]{1,0:T(8,128)(2,1)S(1)} collective-permute-done((bf16[96,896]{1,0:T(8,128)(2,1)S(1)}, bf16[96,896]{1,0:T(8,128)(2,1)S(1)}, u32[]{:S(2)}, u32[]{:S(2)}) %collective-permute-start.48) | collective-permute-done | bytes 172064 | tf_op jit(solution)/shard_map/ppermute | solution.py:20
  280.1 2.1 collective-permute-done.44
  282.3 2.9 collective-permute-start.51
  285.2 1.5 collective-permute-start.52
  288.2 2.8 collective-permute-done.52
  (165 shorter events, 24.3 us)
Async XLA Ops:
  2.4 7.5 %collective-permute-start.2 = (bf16[24,2432]{1,0:T(8,128)(2,1)S(1)}, bf16[24,2432]{1,0:T(8,128)(2,1)S(1)}, u32[]{:S(2)}, u32[]{:S(2)}) collective-permute-start(bf16[24,2432]{1,0:T(8,128)(2,1)S(1)} %fusion.23), channel_id=1, source_target_pairs={{0,1},{1,0},{2,3},{3,2},{4,5},{5,4},{6,7},{7,6},{8,9},{9,8},{10,11... | collective-permute-start | bytes 350216 | tf_op jit(solution)/shard_map/ppermute | solution.py:24
  5.5 11.9 %collective-permute-start.1 = (bf16[24,2432]{1,0:T(8,128)(2,1)S(1)}, bf16[24,2432]{1,0:T(8,128)(2,1)S(1)}, u32[]{:S(2)}, u32[]{:S(2)}) collective-permute-start(bf16[24,2432]{1,0:T(8,128)(2,1)S(1)} %fusion.23), channel_id=1, source_target_pairs={{0,2},{1,3},{2,0},{3,1},{4,6},{5,7},{6,4},{7,5},{8,10},{9,11},{10,... | collective-permute-start | bytes 350216 | tf_op jit(solution)/shard_map/ppermute | solution.py:24
  8.0 9.3 %collective-permute-start = (bf16[24,2432]{1,0:T(8,128)(2,1)S(1)}, bf16[24,2432]{1,0:T(8,128)(2,1)S(1)}, u32[]{:S(2)}, u32[]{:S(2)}) collective-permute-start(bf16[24,2432]{1,0:T(8,128)(2,1)S(1)} %fusion.23), channel_id=1, source_target_pairs={{0,3},{1,2},{2,1},{3,0},{4,7},{5,6},{6,5},{7,4},{8,11},{9,10},{10,... | collective-permute-start | bytes 350216 | tf_op jit(solution)/shard_map/ppermute | solution.py:24
  18.4 24.0 %collective-permute-start.5 = (bf16[96,2432]{1,0:T(8,128)(2,1)S(1)}, bf16[96,2432]{1,0:T(8,128)(2,1)S(1)}, u32[]{:S(2)}, u32[]{:S(2)}) collective-permute-start(bf16[96,2432]{1,0:T(8,128)(2,1)S(1)} %pad_maximum_fusion.5), channel_id=1, source_target_pairs={{0,24},{4,28},{8,16},{12,20},{16,8},{20,12},{24,0},{28,4},{1,25},{... | collective-permute-start | bytes 1400840 | tf_op jit(solution)/shard_map/ppermute | solution.py:20
  20.9 21.5 %collective-permute-start.4 = (bf16[96,2432]{1,0:T(8,128)(2,1)S(1)}, bf16[96,2432]{1,0:T(8,128)(2,1)S(1)}, u32[]{:S(2)}, u32[]{:S(2)}) collective-permute-start(bf16[96,2432]{1,0:T(8,128)(2,1)S(1)} %pad_maximum_fusion.5), channel_id=1, source_target_pairs={{0,16},{4,20},{8,24},{12,28},{16,0},{20,4},{24,8},{28,12},{1,17},{... | collective-permute-start | bytes 1400840 | tf_op jit(solution)/shard_map/ppermute | solution.py:20
  21.4 21.0 %collective-permute-start.3 = (bf16[96,2432]{1,0:T(8,128)(2,1)S(1)}, bf16[96,2432]{1,0:T(8,128)(2,1)S(1)}, u32[]{:S(2)}, u32[]{:S(2)}) collective-permute-start(bf16[96,2432]{1,0:T(8,128)(2,1)S(1)} %pad_maximum_fusion.5), channel_id=1, source_target_pairs={{0,8},{4,12},{8,0},{12,4},{16,24},{20,28},{24,16},{28,20},{1,9},{5... | collective-permute-start | bytes 1400840 | tf_op jit(solution)/shard_map/ppermute | solution.py:20
  21.9 8.1 %collective-permute-start.8 = (bf16[24,3840]{1,0:T(8,128)(2,1)S(1)}, bf16[24,3840]{1,0:T(8,128)(2,1)S(1)}, u32[]{:S(2)}, u32[]{:S(2)}) collective-permute-start(bf16[24,3840]{1,0:T(8,128)(2,1)S(1)} %pad_maximum_fusion.7), channel_id=1, source_target_pairs={{0,3},{1,2},{2,1},{3,0},{4,7},{5,6},{6,5},{7,4},{8,11},{9,10},{10,... | collective-permute-start | bytes 552968 | tf_op jit(solution)/shard_map/ppermute | solution.py:24
  24.4 14.5 %collective-permute-start.7 = (bf16[24,3840]{1,0:T(8,128)(2,1)S(1)}, bf16[24,3840]{1,0:T(8,128)(2,1)S(1)}, u32[]{:S(2)}, u32[]{:S(2)}) collective-permute-start(bf16[24,3840]{1,0:T(8,128)(2,1)S(1)} %pad_maximum_fusion.7), channel_id=1, source_target_pairs={{0,2},{1,3},{2,0},{3,1},{4,6},{5,7},{6,4},{7,5},{8,10},{9,11},{10,... | collective-permute-start | bytes 552968 | tf_op jit(solution)/shard_map/ppermute | solution.py:24
  30.0 12.4 %copy-start.13 = (bf16[24,3840]{1,0:T(8,128)(2,1)}, bf16[24,3840]{1,0:T(8,128)(2,1)S(1)}, u32[]{:S(2)}) copy-start(bf16[24,3840]{1,0:T(8,128)(2,1)S(1)} %collective-permute-done.8) | copy-start | bytes 552964
  30.0 12.3 %collective-permute-start.6 = (bf16[24,3840]{1,0:T(8,128)(2,1)S(1)}, bf16[24,3840]{1,0:T(8,128)(2,1)S(1)}, u32[]{:S(2)}, u32[]{:S(2)}) collective-permute-start(bf16[24,3840]{1,0:T(8,128)(2,1)S(1)} %pad_maximum_fusion.7), channel_id=1, source_target_pairs={{0,1},{1,0},{2,3},{3,2},{4,5},{5,4},{6,7},{7,6},{8,9},{9,8},{10,11... | collective-permute-start | bytes 552968 | tf_op jit(solution)/shard_map/ppermute | solution.py:24
  44.5 6.1 %collective-permute-start.10 = (bf16[4,96,2432]{2,1,0:T(8,128)(2,1)S(1)}, bf16[4,96,2432]{2,1,0:T(8,128)(2,1)}, u32[]{:S(2)}, u32[]{:S(2)}) collective-permute-start(bf16[4,96,2432]{2,1,0:T(8,128)(2,1)S(1)} %pad_maximum_fusion.2.rest_0_.rest_6_), channel_id=1, source_target_pairs={{0,4},{4,0},{8,12},{12,8},{16,20},{20,16},{24,28},{28,24},{1,5},{5... | collective-permute-start | bytes 5603336 | tf_op jit(solution)/shard_map/ppermute | solution.py:20
  48.9 5.4 %copy-start.23 = (bf16[96,768]{1,0:T(8,128)(2,1)S(1)}, bf16[96,768]{1,0:T(8,128)(2,1)}, u32[]{:S(2)}) copy-start(bf16[96,768]{1,0:T(8,128)(2,1)} %param.19) | copy-start | bytes 442372
  48.9 7.4 %copy-start.28 = (s32[2,512]{1,0:T(2,128)S(1)}, s32[2,512]{1,0:T(2,128)}, u32[]{:S(2)}) copy-start(s32[2,512]{1,0:T(2,128)} %param.13) | copy-start | bytes 12292
  48.9 1.7 collective-permute-start.9
  49.6 32.1 %copy-start.3 = (bf16[96,3840]{1,0:T(8,128)(2,1)}, bf16[96,3840]{1,0:T(8,128)(2,1)S(1)}, u32[]{:S(2)}) copy-start(bf16[96,3840]{1,0:T(8,128)(2,1)S(1)} %pad_maximum_fusion.3) | copy-start | bytes 2211844
  50.6 31.1 %collective-permute-start.13 = (bf16[96,3840]{1,0:T(8,128)(2,1)S(1)}, bf16[96,3840]{1,0:T(8,128)(2,1)S(1)}, u32[]{:S(2)}, u32[]{:S(2)}) collective-permute-start(bf16[96,3840]{1,0:T(8,128)(2,1)S(1)} %pad_maximum_fusion.3), channel_id=1, source_target_pairs={{0,24},{4,28},{8,16},{12,20},{16,8},{20,12},{24,0},{28,4},{1,25},{... | collective-permute-start | bytes 2211848 | tf_op jit(solution)/shard_map/ppermute | solution.py:20
  53.1 33.0 %collective-permute-start.12 = (bf16[96,3840]{1,0:T(8,128)(2,1)S(1)}, bf16[96,3840]{1,0:T(8,128)(2,1)S(1)}, u32[]{:S(2)}, u32[]{:S(2)}) collective-permute-start(bf16[96,3840]{1,0:T(8,128)(2,1)S(1)} %pad_maximum_fusion.3), channel_id=1, source_target_pairs={{0,16},{4,20},{8,24},{12,28},{16,0},{20,4},{24,8},{28,12},{1,17},{... | collective-permute-start | bytes 2211848 | tf_op jit(solution)/shard_map/ppermute | solution.py:20
  53.6 32.7 %collective-permute-start.11 = (bf16[96,3840]{1,0:T(8,128)(2,1)S(1)}, bf16[96,3840]{1,0:T(8,128)(2,1)}, u32[]{:S(2)}, u32[]{:S(2)}) collective-permute-start(bf16[96,3840]{1,0:T(8,128)(2,1)S(1)} %pad_maximum_fusion.3), channel_id=1, source_target_pairs={{0,8},{4,12},{8,0},{12,4},{16,24},{20,28},{24,16},{28,20},{1,9},{5... | collective-permute-start | bytes 2211848 | tf_op jit(solution)/shard_map/ppermute | solution.py:20
  54.4 27.3 %collective-permute-start.15 = (bf16[96,768]{1,0:T(8,128)(2,1)S(1)}, bf16[96,768]{1,0:T(8,128)(2,1)S(1)}, u32[]{:S(2)}, u32[]{:S(2)}) collective-permute-start(bf16[96,768]{1,0:T(8,128)(2,1)S(1)} %copy-done.23), channel_id=1, source_target_pairs={{0,2},{1,3},{2,0},{3,1},{4,6},{5,7},{6,4},{7,5},{8,10},{9,11},{10,... | collective-permute-start | bytes 442376 | tf_op jit(solution)/shard_map/ppermute | solution.py:24
  55.4 26.3 %collective-permute-start.14 = (bf16[96,768]{1,0:T(8,128)(2,1)S(1)}, bf16[96,768]{1,0:T(8,128)(2,1)S(1)}, u32[]{:S(2)}, u32[]{:S(2)}) collective-permute-start(bf16[96,768]{1,0:T(8,128)(2,1)S(1)} %copy-done.23), channel_id=1, source_target_pairs={{0,1},{1,0},{2,3},{3,2},{4,5},{5,4},{6,7},{7,6},{8,9},{9,8},{10,11... | collective-permute-start | bytes 442376 | tf_op jit(solution)/shard_map/ppermute | solution.py:24
  89.0 9.5 %copy-start = (bf16[4,96,3840]{2,1,0:T(8,128)(2,1)}, bf16[4,96,3840]{2,1,0:T(8,128)(2,1)S(1)}, u32[]{:S(2)}) copy-start(bf16[4,96,3840]{2,1,0:T(8,128)(2,1)S(1)} %pad_maximum_fusion.rest_0_) | copy-start | bytes 8847364
  89.0 9.5 %collective-permute-start.17 = (bf16[4,96,3840]{2,1,0:T(8,128)(2,1)S(1)}, bf16[4,96,3840]{2,1,0:T(8,128)(2,1)}, u32[]{:S(2)}, u32[]{:S(2)}) collective-permute-start(bf16[4,96,3840]{2,1,0:T(8,128)(2,1)S(1)} %pad_maximum_fusion.rest_0_), channel_id=1, source_target_pairs={{0,4},{4,0},{8,12},{12,8},{16,20},{20,16},{24,28},{28,24},{1,5},{5... | collective-permute-start | bytes 8847368 | tf_op jit(solution)/shard_map/ppermute | solution.py:20
  89.2 8.1 %collective-permute-start.16 = (bf16[96,768]{1,0:T(8,128)(2,1)S(1)}, bf16[96,768]{1,0:T(8,128)(2,1)}, u32[]{:S(2)}, u32[]{:S(2)}) collective-permute-start(bf16[96,768]{1,0:T(8,128)(2,1)S(1)} %copy-done.24), channel_id=1, source_target_pairs={{0,3},{1,2},{2,1},{3,0},{4,7},{5,6},{6,5},{7,4},{8,11},{9,10},{10,... | collective-permute-start | bytes 442376 | tf_op jit(solution)/shard_map/ppermute | solution.py:24
  91.8 10.3 %copy-start.6 = (s32[4,16384]{1,0:T(4,128)}, s32[4,16384]{1,0:T(4,128)S(1)}, u32[]{:S(2)}) copy-start(s32[4,16384]{1,0:T(4,128)S(1)} %add.147) | copy-start | bytes 786436
  98.5 32.0 %collective-permute-start.20 = (bf16[384,768]{1,0:T(8,128)(2,1)S(1)}, bf16[384,768]{1,0:T(8,128)(2,1)S(1)}, u32[]{:S(2)}, u32[]{:S(2)}) collective-permute-start(bf16[384,768]{1,0:T(8,128)(2,1)S(1)} %pad_maximum_fusion.4), channel_id=1, source_target_pairs={{0,24},{4,28},{8,16},{12,20},{16,8},{20,12},{24,0},{28,4},{1,25},{... | collective-permute-start | bytes 1769480 | tf_op jit(solution)/shard_map/ppermute | solution.py:20
  100.8 29.7 %collective-permute-start.19 = (bf16[384,768]{1,0:T(8,128)(2,1)S(1)}, bf16[384,768]{1,0:T(8,128)(2,1)S(1)}, u32[]{:S(2)}, u32[]{:S(2)}) collective-permute-start(bf16[384,768]{1,0:T(8,128)(2,1)S(1)} %pad_maximum_fusion.4), channel_id=1, source_target_pairs={{0,16},{4,20},{8,24},{12,28},{16,0},{20,4},{24,8},{28,12},{1,17},{... | collective-permute-start | bytes 1769480 | tf_op jit(solution)/shard_map/ppermute | solution.py:20
  101.5 29.1 %collective-permute-start.18 = (bf16[384,768]{1,0:T(8,128)(2,1)S(1)}, bf16[384,768]{1,0:T(8,128)(2,1)S(1)}, u32[]{:S(2)}, u32[]{:S(2)}) collective-permute-start(bf16[384,768]{1,0:T(8,128)(2,1)S(1)} %pad_maximum_fusion.4), channel_id=1, source_target_pairs={{0,8},{4,12},{8,0},{12,4},{16,24},{20,28},{24,16},{28,20},{1,9},{5... | collective-permute-start | bytes 1769480 | tf_op jit(solution)/shard_map/ppermute | solution.py:20
  102.1 28.4 %collective-permute-start.21 = (s32[2,16384]{1,0:T(2,128)S(1)}, s32[2,16384]{1,0:T(2,128)S(1)}, u32[]{:S(2)}, u32[]{:S(2)}) collective-permute-start(s32[2,16384]{1,0:T(2,128)S(1)} %broadcast_select_fusion.40), channel_id=1, source_target_pairs={{0,8},{4,12},{8,0},{12,4},{16,24},{20,28},{24,16},{28,20},{1,9},{5... | collective-permute-start | bytes 393224 | tf_op jit(solution)/shard_map/ppermute | solution.py:20
  130.6 8.5 %copy-start.5 = (bf16[4,384,768]{2,1,0:T(8,128)(2,1)S(1)}, bf16[4,384,768]{2,1,0:T(8,128)(2,1)}, u32[]{:S(2)}) copy-start(bf16[4,384,768]{2,1,0:T(8,128)(2,1)} %get-tuple-element.141) | copy-start | bytes 7077892
  130.9 9.8 %copy-start.2 = (bf16[4,384,768]{2,1,0:T(8,128)(2,1)}, bf16[4,384,768]{2,1,0:T(8,128)(2,1)S(1)}, u32[]{:S(2)}) copy-start(bf16[4,384,768]{2,1,0:T(8,128)(2,1)S(1)} %pad_maximum_fusion.1.rest_2_) | copy-start | bytes 7077892
  130.9 14.7 %collective-permute-start.23 = (bf16[4,384,768]{2,1,0:T(8,128)(2,1)S(1)}, bf16[4,384,768]{2,1,0:T(8,128)(2,1)S(1)}, u32[]{:S(2)}, u32[]{:S(2)}) collective-permute-start(bf16[4,384,768]{2,1,0:T(8,128)(2,1)S(1)} %pad_maximum_fusion.1.rest_2_), channel_id=1, source_target_pairs={{0,4},{4,0},{8,12},{12,8},{16,20},{20,16},{24,28},{28,24},{1,5},{5... | collective-permute-start | bytes 7077896 | tf_op jit(solution)/shard_map/ppermute | solution.py:20
  131.0 8.1 %collective-permute-start.22 = (bf16[4,384,768]{2,1,0:T(8,128)(2,1)}, bf16[4,384,768]{2,1,0:T(8,128)(2,1)S(1)}, u32[]{:S(2)}, u32[]{:S(2)}) collective-permute-start(bf16[4,384,768]{2,1,0:T(8,128)(2,1)} %get-tuple-element.142), channel_id=1, source_target_pairs={{0,4},{4,0},{8,12},{12,8},{16,20},{20,16},{24,28},{28,24},{1,5},{5... | collective-permute-start | bytes 7077896 | tf_op jit(solution)/shard_map/ppermute | solution.py:20
  140.7 43.8 %collective-permute-start.24 = (bf16[384,768]{1,0:T(8,128)(2,1)}, bf16[384,768]{1,0:T(8,128)(2,1)}, u32[]{:S(2)}, u32[]{:S(2)}) collective-permute-start(bf16[384,768]{1,0:T(8,128)(2,1)} %get-tuple-element.154), channel_id=1, source_target_pairs={{0,8},{4,12},{8,0},{12,4},{16,24},{20,28},{24,16},{28,20},{1,9},{5... | collective-permute-start | bytes 1769480 | tf_op jit(solution)/shard_map/ppermute | solution.py:20
  141.3 43.2 %collective-permute-start.25 = (bf16[384,768]{1,0:T(8,128)(2,1)}, bf16[384,768]{1,0:T(8,128)(2,1)}, u32[]{:S(2)}, u32[]{:S(2)}) collective-permute-start(bf16[384,768]{1,0:T(8,128)(2,1)} %get-tuple-element.155), channel_id=1, source_target_pairs={{0,16},{4,20},{8,24},{12,28},{16,0},{20,4},{24,8},{28,12},{1,17},{... | collective-permute-start | bytes 1769480 | tf_op jit(solution)/shard_map/ppermute | solution.py:20
  142.8 41.7 %collective-permute-start.26 = (bf16[384,768]{1,0:T(8,128)(2,1)S(1)}, bf16[384,768]{1,0:T(8,128)(2,1)}, u32[]{:S(2)}, u32[]{:S(2)}) collective-permute-start(bf16[384,768]{1,0:T(8,128)(2,1)S(1)} %get-tuple-element.156), channel_id=1, source_target_pairs={{0,24},{4,28},{8,16},{12,20},{16,8},{20,12},{24,0},{28,4},{1,25},{... | collective-permute-start | bytes 1769480 | tf_op jit(solution)/shard_map/ppermute | solution.py:20
  144.3 40.2 %collective-permute-start.27 = (s32[1,16384]{1,0:T(1,128)S(1)}, s32[1,16384]{1,0:T(1,128)S(1)}, u32[]{:S(2)}, u32[]{:S(2)}) collective-permute-start(s32[1,16384]{1,0:T(1,128)S(1)} %broadcast_select_fusion.37), channel_id=1, source_target_pairs={{0,16},{4,20},{8,24},{12,28},{16,0},{20,4},{24,8},{28,12},{1,17},{... | collective-permute-start | bytes 196616 | tf_op jit(solution)/shard_map/ppermute | solution.py:20
  184.5 5.7 %collective-permute-start.28 = (bf16[4,96,3840]{2,1,0:T(8,128)(2,1)}, bf16[4,96,3840]{2,1,0:T(8,128)(2,1)S(1)}, u32[]{:S(2)}, u32[]{:S(2)}) collective-permute-start(bf16[4,96,3840]{2,1,0:T(8,128)(2,1)} %get-tuple-element.160), channel_id=1, source_target_pairs={{0,4},{4,0},{8,12},{12,8},{16,20},{20,16},{24,28},{28,24},{1,5},{5... | collective-permute-start | bytes 8847368 | tf_op jit(solution)/shard_map/ppermute | solution.py:20
  184.7 8.0 %collective-permute-start.31 = (s32[1,16384]{1,0:T(1,128)S(1)}, s32[1,16384]{1,0:T(1,128)S(1)}, u32[]{:S(2)}, u32[]{:S(2)}) collective-permute-start(s32[1,16384]{1,0:T(1,128)S(1)} %fusion.24), channel_id=1, source_target_pairs={{0,3},{1,2},{2,1},{3,0},{4,7},{5,6},{6,5},{7,4},{8,11},{9,10},{10,... | collective-permute-start | bytes 196616 | tf_op jit(solution)/shard_map/ppermute | solution.py:24
  186.2 7.8 %collective-permute-start.30 = (s32[1,16384]{1,0:T(1,128)S(1)}, s32[1,16384]{1,0:T(1,128)S(1)}, u32[]{:S(2)}, u32[]{:S(2)}) collective-permute-start(s32[1,16384]{1,0:T(1,128)S(1)} %fusion.24), channel_id=1, source_target_pairs={{0,2},{1,3},{2,0},{3,1},{4,6},{5,7},{6,4},{7,5},{8,10},{9,11},{10,... | collective-permute-start | bytes 196616 | tf_op jit(solution)/shard_map/ppermute | solution.py:24
  187.3 6.7 %collective-permute-start.29 = (s32[1,16384]{1,0:T(1,128)S(1)}, s32[1,16384]{1,0:T(1,128)S(1)}, u32[]{:S(2)}, u32[]{:S(2)}) collective-permute-start(s32[1,16384]{1,0:T(1,128)S(1)} %fusion.24), channel_id=1, source_target_pairs={{0,1},{1,0},{2,3},{3,2},{4,5},{5,4},{6,7},{7,6},{8,9},{9,8},{10,11... | collective-permute-start | bytes 196616 | tf_op jit(solution)/shard_map/ppermute | solution.py:24
  194.0 28.2 %collective-permute-start.32 = (bf16[96,3840]{1,0:T(8,128)(2,1)S(1)}, bf16[96,3840]{1,0:T(8,128)(2,1)S(1)}, u32[]{:S(2)}, u32[]{:S(2)}) collective-permute-start(bf16[96,3840]{1,0:T(8,128)(2,1)S(1)} %get-tuple-element.163), channel_id=1, source_target_pairs={{0,8},{4,12},{8,0},{12,4},{16,24},{20,28},{24,16},{28,20},{1,9},{5... | collective-permute-start | bytes 2211848 | tf_op jit(solution)/shard_map/ppermute | solution.py:20
  195.1 27.1 %collective-permute-start.33 = (bf16[96,3840]{1,0:T(8,128)(2,1)S(1)}, bf16[96,3840]{1,0:T(8,128)(2,1)S(1)}, u32[]{:S(2)}, u32[]{:S(2)}) collective-permute-start(bf16[96,3840]{1,0:T(8,128)(2,1)S(1)} %get-tuple-element.164), channel_id=1, source_target_pairs={{0,16},{4,20},{8,24},{12,28},{16,0},{20,4},{24,8},{28,12},{1,17},{... | collective-permute-start | bytes 2211848 | tf_op jit(solution)/shard_map/ppermute | solution.py:20
  197.4 24.7 %collective-permute-start.36 = (bf16[96,768]{1,0:T(8,128)(2,1)S(1)}, bf16[96,768]{1,0:T(8,128)(2,1)S(1)}, u32[]{:S(2)}, u32[]{:S(2)}) collective-permute-start(bf16[96,768]{1,0:T(8,128)(2,1)S(1)} %get-tuple-element.244), channel_id=1, source_target_pairs={{0,3},{1,2},{2,1},{3,0},{4,7},{5,6},{6,5},{7,4},{8,11},{9,10},{10,... | collective-permute-start | bytes 442376 | tf_op jit(solution)/shard_map/ppermute | solution.py:24
  199.9 22.2 %collective-permute-start.34 = (bf16[96,768]{1,0:T(8,128)(2,1)S(1)}, bf16[96,768]{1,0:T(8,128)(2,1)S(1)}, u32[]{:S(2)}, u32[]{:S(2)}) collective-permute-start(bf16[96,768]{1,0:T(8,128)(2,1)S(1)} %get-tuple-element.246), channel_id=1, source_target_pairs={{0,1},{1,0},{2,3},{3,2},{4,5},{5,4},{6,7},{7,6},{8,9},{9,8},{10,11... | collective-permute-start | bytes 442376 | tf_op jit(solution)/shard_map/ppermute | solution.py:24
  199.9 22.3 %collective-permute-start.35 = (bf16[96,768]{1,0:T(8,128)(2,1)S(1)}, bf16[96,768]{1,0:T(8,128)(2,1)S(1)}, u32[]{:S(2)}, u32[]{:S(2)}) collective-permute-start(bf16[96,768]{1,0:T(8,128)(2,1)S(1)} %get-tuple-element.247), channel_id=1, source_target_pairs={{0,2},{1,3},{2,0},{3,1},{4,6},{5,7},{6,4},{7,5},{8,10},{9,11},{10,... | collective-permute-start | bytes 442376 | tf_op jit(solution)/shard_map/ppermute | solution.py:24
  222.2 3.7 %collective-permute-start.38 = (bf16[4,96,1536]{2,1,0:T(8,128)(2,1)}, bf16[4,96,1536]{2,1,0:T(8,128)(2,1)S(1)}, u32[]{:S(2)}, u32[]{:S(2)}) collective-permute-start(bf16[4,96,1536]{2,1,0:T(8,128)(2,1)} %get-tuple-element.181), channel_id=1, source_target_pairs={{0,4},{4,0},{8,12},{12,8},{16,20},{20,16},{24,28},{28,24},{1,5},{5... | collective-permute-start | bytes 3538952 | tf_op jit(solution)/shard_map/ppermute | solution.py:20
  222.8 34.1 %collective-permute-start.42 = (s32[1,16384]{1,0:T(1,128)S(1)}, s32[1,16384]{1,0:T(1,128)S(1)}, u32[]{:S(2)}, u32[]{:S(2)}) collective-permute-start(s32[1,16384]{1,0:T(1,128)S(1)} %add_add_fusion), channel_id=1, source_target_pairs={{0,16},{4,20},{8,24},{12,28},{16,0},{20,4},{24,8},{28,12},{1,17},{... | collective-permute-start | bytes 196616 | tf_op jit(solution)/shard_map/ppermute | solution.py:20
  224.4 32.6 %collective-permute-start.37 = (bf16[96,3840]{1,0:T(8,128)(2,1)S(1)}, bf16[96,3840]{1,0:T(8,128)(2,1)S(1)}, u32[]{:S(2)}, u32[]{:S(2)}) collective-permute-start(bf16[96,3840]{1,0:T(8,128)(2,1)S(1)} %get-tuple-element.178), channel_id=1, source_target_pairs={{0,24},{4,28},{8,16},{12,20},{16,8},{20,12},{24,0},{28,4},{1,25},{... | collective-permute-start | bytes 2211848 | tf_op jit(solution)/shard_map/ppermute | solution.py:20
  227.4 29.6 %collective-permute-start.39 = (bf16[96,1536]{1,0:T(8,128)(2,1)S(1)}, bf16[96,1536]{1,0:T(8,128)(2,1)S(1)}, u32[]{:S(2)}, u32[]{:S(2)}) collective-permute-start(bf16[96,1536]{1,0:T(8,128)(2,1)S(1)} %get-tuple-element.182), channel_id=1, source_target_pairs={{0,8},{4,12},{8,0},{12,4},{16,24},{20,28},{24,16},{28,20},{1,9},{5... | collective-permute-start | bytes 884744 | tf_op jit(solution)/shard_map/ppermute | solution.py:20
  228.5 28.5 %collective-permute-start.40 = (bf16[96,1536]{1,0:T(8,128)(2,1)S(1)}, bf16[96,1536]{1,0:T(8,128)(2,1)S(1)}, u32[]{:S(2)}, u32[]{:S(2)}) collective-permute-start(bf16[96,1536]{1,0:T(8,128)(2,1)S(1)} %get-tuple-element.183), channel_id=1, source_target_pairs={{0,16},{4,20},{8,24},{12,28},{16,0},{20,4},{24,8},{28,12},{1,17},{... | collective-permute-start | bytes 884744 | tf_op jit(solution)/shard_map/ppermute | solution.py:20
  229.5 27.5 %collective-permute-start.41 = (bf16[96,1536]{1,0:T(8,128)(2,1)S(1)}, bf16[96,1536]{1,0:T(8,128)(2,1)S(1)}, u32[]{:S(2)}, u32[]{:S(2)}) collective-permute-start(bf16[96,1536]{1,0:T(8,128)(2,1)S(1)} %get-tuple-element.184), channel_id=1, source_target_pairs={{0,24},{4,28},{8,16},{12,20},{16,8},{20,12},{24,0},{28,4},{1,25},{... | collective-permute-start | bytes 884744 | tf_op jit(solution)/shard_map/ppermute | solution.py:20
  257.2 5.0 %collective-permute-start.53 = (s32[2,16384]{1,0:T(2,128)S(1)}, s32[2,16384]{1,0:T(2,128)S(1)}, u32[]{:S(2)}, u32[]{:S(2)}) collective-permute-start(s32[2,16384]{1,0:T(2,128)S(1)} %pad_add_fusion.2), channel_id=1, source_target_pairs={{0,8},{4,12},{8,0},{12,4},{16,24},{20,28},{24,16},{28,20},{1,9},{5... | collective-permute-start | bytes 393224 | tf_op jit(solution)/shard_map/ppermute | solution.py:20
  259.0 6.7 %copy-start.10 = (bf16[4,96,896]{2,1,0:T(8,128)(2,1)S(1)}, bf16[4,96,896]{2,1,0:T(8,128)(2,1)}, u32[]{:S(2)}) copy-start(bf16[4,96,896]{2,1,0:T(8,128)(2,1)} %get-tuple-element.201) | copy-start | bytes 2064388
  259.0 21.1 %collective-permute-start.45 = (bf16[24,5376]{1,0:T(8,128)(2,1)S(1)}, bf16[24,5376]{1,0:T(8,128)(2,1)S(1)}, u32[]{:S(2)}, u32[]{:S(2)}) collective-permute-start(bf16[24,5376]{1,0:T(8,128)(2,1)S(1)} %get-tuple-element.217), channel_id=1, source_target_pairs={{0,3},{1,2},{2,1},{3,0},{4,7},{5,6},{6,5},{7,4},{8,11},{9,10},{10,... | collective-permute-start | bytes 774152 | tf_op jit(solution)/shard_map/ppermute | solution.py:24
  261.4 4.3 %collective-permute-start.46 = (bf16[4,96,896]{2,1,0:T(8,128)(2,1)S(1)}, bf16[4,96,896]{2,1,0:T(8,128)(2,1)S(1)}, u32[]{:S(2)}, u32[]{:S(2)}) collective-permute-start(bf16[4,96,896]{2,1,0:T(8,128)(2,1)S(1)} %copy-done.29), channel_id=1, source_target_pairs={{0,4},{4,0},{8,12},{12,8},{16,20},{20,16},{24,28},{28,24},{1,5},{5... | collective-permute-start | bytes 2064392 | tf_op jit(solution)/shard_map/ppermute | solution.py:20
  262.5 4.3 %collective-permute-start.54 = (s32[4,16384]{1,0:T(4,128)S(1)}, s32[4,16384]{1,0:T(4,128)S(1)}, u32[]{:S(2)}, u32[]{:S(2)}) collective-permute-start(s32[4,16384]{1,0:T(4,128)S(1)} %pad_add_fusion.1), channel_id=1, source_target_pairs={{0,4},{4,0},{8,12},{12,8},{16,20},{20,16},{24,28},{28,24},{1,5},{5... | collective-permute-start | bytes 786440 | tf_op jit(solution)/shard_map/ppermute | solution.py:20
  262.7 19.5 %collective-permute-start.44 = (bf16[24,5376]{1,0:T(8,128)(2,1)S(1)}, bf16[24,5376]{1,0:T(8,128)(2,1)S(1)}, u32[]{:S(2)}, u32[]{:S(2)}) collective-permute-start(bf16[24,5376]{1,0:T(8,128)(2,1)S(1)} %get-tuple-element.237), channel_id=1, source_target_pairs={{0,2},{1,3},{2,0},{3,1},{4,6},{5,7},{6,4},{7,5},{8,10},{9,11},{10,... | collective-permute-start | bytes 774152 | tf_op jit(solution)/shard_map/ppermute | solution.py:24
  263.6 18.6 %collective-permute-start.43 = (bf16[24,5376]{1,0:T(8,128)(2,1)S(1)}, bf16[24,5376]{1,0:T(8,128)(2,1)S(1)}, u32[]{:S(2)}, u32[]{:S(2)}) collective-permute-start(bf16[24,5376]{1,0:T(8,128)(2,1)S(1)} %get-tuple-element.238), channel_id=1, source_target_pairs={{0,1},{1,0},{2,3},{3,2},{4,5},{5,4},{6,7},{7,6},{8,9},{9,8},{10,11... | collective-permute-start | bytes 774152 | tf_op jit(solution)/shard_map/ppermute | solution.py:24
  265.8 7.3 %collective-permute-start.47 = (bf16[96,896]{1,0:T(8,128)(2,1)S(1)}, bf16[96,896]{1,0:T(8,128)(2,1)S(1)}, u32[]{:S(2)}, u32[]{:S(2)}) collective-permute-start(bf16[96,896]{1,0:T(8,128)(2,1)S(1)} %get-tuple-element.234), channel_id=1, source_target_pairs={{0,8},{4,12},{8,0},{12,4},{16,24},{20,28},{24,16},{28,20},{1,9},{5... | collective-permute-start | bytes 516104 | tf_op jit(solution)/shard_map/ppermute | solution.py:20
  267.0 9.3 %collective-permute-start.49 = (bf16[96,896]{1,0:T(8,128)(2,1)S(1)}, bf16[96,896]{1,0:T(8,128)(2,1)S(1)}, u32[]{:S(2)}, u32[]{:S(2)}) collective-permute-start(bf16[96,896]{1,0:T(8,128)(2,1)S(1)} %get-tuple-element.235), channel_id=1, source_target_pairs={{0,24},{4,28},{8,16},{12,20},{16,8},{20,12},{24,0},{28,4},{1,25},{... | collective-permute-start | bytes 516104 | tf_op jit(solution)/shard_map/ppermute | solution.py:20
  273.1 6.8 %collective-permute-start.48 = (bf16[96,896]{1,0:T(8,128)(2,1)S(1)}, bf16[96,896]{1,0:T(8,128)(2,1)S(1)}, u32[]{:S(2)}, u32[]{:S(2)}) collective-permute-start(bf16[96,896]{1,0:T(8,128)(2,1)S(1)} %get-tuple-element.236), channel_id=1, source_target_pairs={{0,16},{4,20},{8,24},{12,28},{16,0},{20,4},{24,8},{28,12},{1,17},{... | collective-permute-start | bytes 516104 | tf_op jit(solution)/shard_map/ppermute | solution.py:20
  282.3 6.0 %collective-permute-start.50 = (bf16[24,896]{1,0:T(8,128)(2,1)S(1)}, bf16[24,896]{1,0:T(8,128)(2,1)S(1)}, u32[]{:S(2)}, u32[]{:S(2)}) collective-permute-start(bf16[24,896]{1,0:T(8,128)(2,1)S(1)} %get-tuple-element.262), channel_id=1, source_target_pairs={{0,1},{1,0},{2,3},{3,2},{4,5},{5,4},{6,7},{7,6},{8,9},{9,8},{10,11... | collective-permute-start | bytes 129032 | tf_op jit(solution)/shard_map/ppermute | solution.py:24
  282.3 5.9 %collective-permute-start.51 = (bf16[24,896]{1,0:T(8,128)(2,1)S(1)}, bf16[24,896]{1,0:T(8,128)(2,1)S(1)}, u32[]{:S(2)}, u32[]{:S(2)}) collective-permute-start(bf16[24,896]{1,0:T(8,128)(2,1)S(1)} %get-tuple-element.263), channel_id=1, source_target_pairs={{0,2},{1,3},{2,0},{3,1},{4,6},{5,7},{6,4},{7,5},{8,10},{9,11},{10,... | collective-permute-start | bytes 129032 | tf_op jit(solution)/shard_map/ppermute | solution.py:24
  285.2 5.8 %collective-permute-start.52 = (bf16[24,896]{1,0:T(8,128)(2,1)S(1)}, bf16[24,896]{1,0:T(8,128)(2,1)S(1)}, u32[]{:S(2)}, u32[]{:S(2)}) collective-permute-start(bf16[24,896]{1,0:T(8,128)(2,1)S(1)} %get-tuple-element.264), channel_id=1, source_target_pairs={{0,3},{1,2},{2,1},{3,0},{4,7},{5,6},{6,5},{7,4},{8,11},{9,10},{10,... | collective-permute-start | bytes 129032 | tf_op jit(solution)/shard_map/ppermute | solution.py:24
  (21 other events, 50.2 us)
where the time goes:
time: 296 us; the launch traced here: 293 us
  Pallas kernels  137 us (46%)
  starting transfers between devices  69.3 us (23%)
  waiting for transfers between devices  54.9 us (19%)
  other arithmetic  22.1 us (7%)
  local copies, waits for them, and re-layouts  7.75 us (3%)
    pallas_call x2, Pallas kernels, backward(): pl.pallas_call(functools.partial(backward_kernel, plans, counts, groups,...  45.4 us
    ppermute x21, starting transfers between devices, swap_inner(): return lax.ppermute(value, 'fsdp', [(i, i ^ bit) for i in range(size)])  37.5 us
    pallas_call x1, Pallas kernels, feed_return(): pl.pallas_call(functools.partial(return_kernel, plan, len(pieces), plan_d...  37.5 us
    ppermute x34, starting transfers between devices, swap(): return lax.ppermute(value, 'dp', [(i, i ^ bit) for i in range(BLOCKS)])  31.7 us
    ppermute x21, waiting for transfers between devices, swap_inner(): return lax.ppermute(value, 'fsdp', [(i, i ^ bit) for i in range(size)])  30.6 us
    pallas_call x1, Pallas kernels, feed_forward(): pl.pallas_call(functools.partial(forward_kernel, plan, len(pieces)), grid...  26.8 us
    pallas_call x1, Pallas kernels, attend(): pl.pallas_call(functools.partial(attend_kernel, plan, len(pieces)), grid=...  24.4 us
    ppermute x34, waiting for transfers between devices, swap(): return lax.ppermute(value, 'dp', [(i, i ^ bit) for i in range(BLOCKS)])  24.3 us
  transfers between devices with their start and end apart: 55, of which 18 were waited for; matrix products, arithmetic and copies ran while one was open for 6% of the time, Pallas kernels for 47%

commit v1 on v0

--- a/solution.py
+++ b/solution.py
@@ -66,9 +66,9 @@
     return list(lax.optimization_barrier((*values, *others)))[: len(values)]
 
 
-def gather_first(shards, inner, counts):
+def gather_first(shards, inner, counts, segments):
     own = gather_inner(shards[0], inner)
-    own, second = together([own, shards[1]])
+    own, second, counts, segments = together([own, shards[1], counts, segments])
     sides = gather_sides(own)
     parts = [second] + [swap_inner(second, k, inner) for k in range(1, inner)]
     values = together([*sides, *parts])
@@ -78,7 +78,7 @@
     first = with_core(sides)
     own_second, third, other = together([own_second, shards[2], other], *first[0])
     parts = [swap_inner(third, k, inner) for k in range(1, inner - 1)]
-    return first, gather_sides(own_second), [third] + parts, keep, other
+    return first, gather_sides(own_second), [third] + parts, keep, other, segments
 
 
 def halve_tables(counts, bit):
@@ -559,38 +559,24 @@
 
 
 def backward_kernel(
-    plans, counts, groups, first_group, me_ref, grad_ref, q_ref, k_ref, v_ref, expo_ref, inv_ref,
-    mixed_ref, ht_ref, *rest
+    plan, count, groups, me_ref, grad_ref, q_ref, k_ref, v_ref, expo_ref, inv_ref, mixed_ref, ht_ref,
+    *rest
 ):
-    out_pieces, rest = rest[: counts[0]], rest[counts[0] :]
-    last = first_group > 0
-    if last:
-        x_ref, vec_ref, early_ref, ffn_sums_ref, *rest = rest
-        qkv_pieces, rest = rest[: counts[1]], rest[counts[1] :]
-        tokens_grad_ref, *rest = rest
-    else:
-        dqkv_ref, *rest = rest
-    keep_ref, send_ref, dot_ref, acc_ref, wout_ref, out_sems, *rest = rest
-    if last:
-        w_ref, vec_acc, sems = rest
+    pieces = rest[:count]
+    dqkv_ref, keep_ref, send_ref, dot_ref, acc_ref, wout_ref, sems = rest[count:]
     row = pl.program_id(0)
     group = pl.program_id(1)
     length, width = grad_ref.shape[1:]
     head_dim = width // H
     block = width // BLOCKS
     wide = q_ref.shape[2]
-    part = wide * groups
     me = me_ref[0]
 
     @pl.when((row == 0) & (group == 0))
     def _():
         copies = load_pieces(
-            out_pieces, plans[0], me, block, wout_ref, out_sems, out_pieces[0].shape[2] - width
+            pieces, plan, me, block, wout_ref, sems, pieces[0].shape[2] - width
         )
-        if last:
-            copies += load_pieces(qkv_pieces, plans[1], me, block, w_ref, sems)
-            vec_acc[...] = jnp.zeros_like(vec_acc)
-            vec_acc[2:4] = ffn_sums_ref[0:2]
         acc_ref[...] = jnp.zeros_like(acc_ref)
         for copy in copies:
             copy.wait()
@@ -598,8 +584,7 @@
     @pl.when(group == 0)
     def _():
         attn_in = grad_ref[0].astype(jnp.bfloat16)
-        weights = wout_ref[first_group * wide : first_group * wide + part, :]
-        dot_ref[...] = dot_nt(weights, attn_in).astype(jnp.bfloat16)
+        dot_ref[...] = dot_nt(wout_ref[...], attn_in).astype(jnp.bfloat16)
 
     results = []
     for pair in range(wide // 128):
@@ -616,106 +601,121 @@
         )
     joined = [jnp.concatenate(list(values), axis=1) for values in zip(*results)]
     for place, value in enumerate(joined):
-        start = pl.multiple_of(place * part + group * wide, 128)
+        start = pl.multiple_of(place * width + group * wide, 128)
         acc_ref[:, pl.ds(start, wide)] += dot_nn(ht_ref[0], value)
-        if not last:
-            dqkv_ref[0, :, pl.ds(start, wide)] = value
-    if last:
-        before = first_group * wide
-        back = None
-        for place, value in enumerate(joined):
-            old = early_ref[0, :, place * before : (place + 1) * before]
-            start = place * width
-            term = dot_nt(old, w_ref[:, start : start + before])
-            term = term + dot_nt(value, w_ref[:, start + before : start + width])
-            back = term if back is None else back + term
-        normed, factor = norm_parts(x_ref[0].astype(jnp.float32))
-        through, gain_grad, bias_grad = norm_back(back, normed, factor, vec_ref[0:1])
-        vec_acc[0:1] += gain_grad
-        vec_acc[1:2] += bias_grad
-        tokens_grad_ref[0] = (grad_ref[0] + through).astype(jnp.bfloat16)
+        dqkv_ref[0, :, pl.ds(start, wide)] = value
 
     @pl.when((row == pl.num_programs(0) - 1) & (group == groups - 1))
     def _():
-        if last:
-            acc_ref[:, 3 * part :] = vec_acc[...].T
         split_blocks(acc_ref, me, block, keep_ref, send_ref)
 
 
-def backward(grad_y, saved, me, groups, first_group, out_group, extra=None):
+def backward(grad_y, saved, me, pieces, plan):
     rows, length, width = grad_y.shape
     qkv, expo, inverse, mixed, h_t = saved
     wide = 256
     heads = wide * H // width
-    part = wide * groups
-    per = width // wide
+    groups = width // wide
 
     def column_spec(kind):
-        return pl.BlockSpec(
-            (1, length, wide), lambda r, g: (r, 0, kind * per + first_group + g)
-        )
-
-    out_pieces, plan_out = out_group
-    inputs = [me, grad_y, qkv, qkv, qkv, expo, inverse, mixed, h_t, *out_pieces]
+        return pl.BlockSpec((1, length, wide), lambda r, g: (r, 0, kind * groups + g))
+
+    inputs = [me, grad_y, qkv, qkv, qkv, expo, inverse, mixed, h_t, *pieces]
     in_specs = [
         pl.BlockSpec(memory_space=pltpu.SMEM),
         row_spec(grad_y.shape),
         column_spec(0),
         column_spec(1),
         column_spec(2),
-        pl.BlockSpec((1, heads, length, length), lambda r, g: (r, first_group + g, 0, 0)),
-        pl.BlockSpec((1, heads, 1, length), lambda r, g: (r, first_group + g, 0, 0)),
-        pl.BlockSpec((1, wide, length), lambda r, g: (r, first_group + g, 0)),
+        pl.BlockSpec((1, heads, length, length), lambda r, g: (r, g, 0, 0)),
+        pl.BlockSpec((1, heads, 1, length), lambda r, g: (r, g, 0, 0)),
+        pl.BlockSpec((1, wide, length), lambda r, g: (r, g, 0)),
         row_spec(h_t.shape),
-    ] + any_specs(out_pieces)
-    plans = [plan_out]
-    counts = [len(out_pieces)]
-    if extra is None:
-        columns = 3 * part
-        shapes = [jax.ShapeDtypeStruct((rows, length, 3 * part), jnp.bfloat16)]
-    else:
-        columns = 3 * part + 128
-        tokens, vec, early, ffn_sums, (pieces, plan) = extra
-        inputs += [tokens, vec, early, ffn_sums, *pieces]
-        in_specs += [row_spec(tokens.shape), whole_spec(vec.shape)]
-        in_specs += [row_spec(early.shape), whole_spec(ffn_sums.shape)] + any_specs(pieces)
-        shapes = [jax.ShapeDtypeStruct(tokens.shape, jnp.bfloat16)]
-        plans += [plan]
-        counts += [len(pieces)]
-    out_specs = [row_spec(shapes[0].shape)]
-    shapes += split_shapes(width // BLOCKS, columns)
-    out_specs += [whole_spec(s.shape) for s in shapes[1:]]
-    scratch = [
-        pltpu.VMEM((part, length), jnp.bfloat16),
-        pltpu.VMEM((width, columns), jnp.float32),
-        pltpu.VMEM((width, width), jnp.bfloat16),
-        pltpu.SemaphoreType.DMA((BLOCKS,)),
-    ]
-    if extra is not None:
-        scratch += [
+    ] + any_specs(pieces)
+    shapes = [jax.ShapeDtypeStruct((rows, length, 3 * width), jnp.bfloat16)]
+    shapes += split_shapes(width // BLOCKS, 3 * width)
+    return pl.pallas_call(
+        functools.partial(backward_kernel, plan, len(pieces), groups),
+        grid=(rows, groups),
+        in_specs=in_specs,
+        out_specs=[row_spec(shapes[0].shape)] + [whole_spec(s.shape) for s in shapes[1:]],
+        out_shape=shapes,
+        scratch_shapes=[
+            pltpu.VMEM((width, length), jnp.bfloat16),
+            pltpu.VMEM((width, 3 * width), jnp.float32),
+            pltpu.VMEM((width, width), jnp.bfloat16),
+            pltpu.SemaphoreType.DMA((BLOCKS,)),
+        ],
+        compiler_params=kernel_params(58),
+        cost_estimate=pl.CostEstimate(flops=10**9, bytes_accessed=10**6, transcendentals=0),
+    )(*inputs)
+
+
+def finish_kernel(
+    plan, count, me_ref, grad_ref, x_ref, dqkv_ref, vec_ref, ffn_sums_ref, *rest
+):
+    pieces = rest[:count]
+    tokens_grad_ref, keep_ref, send_ref, w_ref, vec_acc, sems = rest[count:]
+    row = pl.program_id(0)
+    block = w_ref.shape[0] // BLOCKS
+    normed, factor = norm_parts(x_ref[0].astype(jnp.float32))
+
+    @pl.when(row == 0)
+    def _():
+        copies = load_pieces(pieces, plan, me_ref[0], block, w_ref, sems)
+        vec_acc[...] = jnp.zeros_like(vec_acc)
+        vec_acc[2:4] = ffn_sums_ref[0:2]
+        for copy in copies:
+            copy.wait()
+
+    back = dot_nt(dqkv_ref[0], w_ref[...])
+    through, gain_grad, bias_grad = norm_back(back, normed, factor, vec_ref[0:1])
+    vec_acc[0:1] += gain_grad
+    vec_acc[1:2] += bias_grad
+    tokens_grad_ref[0] = (grad_ref[0] + through).astype(jnp.bfloat16)
+
+    @pl.when(row == pl.num_programs(0) - 1)
+    def _():
+        vec_t = vec_acc[...].T
+        vec_acc[...] = jnp.zeros_like(vec_acc)
+        w_ref[:, :128] = vec_t.astype(jnp.bfloat16)
+        for place, bits in enumerate(PLACES):
+            start = pl.multiple_of((me_ref[0] ^ bits) * block, 16)
+            keep_ref[place] = w_ref[pl.ds(start, block), :128]
+            start = pl.multiple_of((me_ref[0] ^ bits ^ CORE) * block, 16)
+            send_ref[place] = w_ref[pl.ds(start, block), :128]
+
+
+def finish(grad_y, tokens, dqkv, vec, ffn_sums, me, pieces, plan):
+    rows, length, width = tokens.shape
+    shapes = [jax.ShapeDtypeStruct(tokens.shape, jnp.bfloat16)]
+    shapes += split_shapes(width // BLOCKS, 128)
+    return pl.pallas_call(
+        functools.partial(finish_kernel, plan, len(pieces)),
+        grid=(rows,),
+        in_specs=[pl.BlockSpec(memory_space=pltpu.SMEM)]
+        + [row_spec(v.shape) for v in (grad_y, tokens, dqkv)]
+        + [whole_spec(vec.shape), whole_spec(ffn_sums.shape)]
+        + any_specs(pieces),
+        out_specs=[row_spec(tokens.shape)] + [whole_spec(s.shape) for s in shapes[1:]],
+        out_shape=shapes,
+        scratch_shapes=[
             pltpu.VMEM((width, 3 * width), jnp.bfloat16),
             pltpu.VMEM((128, width), jnp.float32),
             pltpu.SemaphoreType.DMA((BLOCKS,)),
-        ]
-    return pl.pallas_call(
-        functools.partial(backward_kernel, plans, counts, groups, first_group),
-        grid=(rows, groups),
-        in_specs=in_specs,
-        out_specs=out_specs,
-        out_shape=shapes,
-        scratch_shapes=scratch,
+        ],
         compiler_params=kernel_params(58),
         cost_estimate=pl.CostEstimate(flops=10**9, bytes_accessed=10**6, transcendentals=0),
-    )(*inputs)
-
-
-def layer(ranks, inner, tokens, segment_ids, cotangent, me, front, counts):
+    )(me, grad_y, tokens, dqkv, vec, ffn_sums, *pieces)
+
+
+def layer(ranks, inner, tokens, segments, cotangent, me, front, counts):
     rows, length, width = tokens.shape
     flat_shape = (rows * length, width)
     flat_cot = cotangent.reshape(flat_shape)
     first = front[0]
     near = direct(ranks, inner)
-    *saved, o, vec = attend(tokens, segment_ids[:, :, None], me, *first)
+    *saved, o, vec = attend(tokens, segments, me, *first)
     if near:
         _, sides, parts, keep, other = front
         *values, o, other = together([*sides, *parts, o, other])
@@ -741,7 +741,6 @@
     grad_y, layer_output, *up_parts, ffn_sums = feed_return(
         y_one, flat_cot, vec, h_t, saved[3], rise, active, me, *second, *third
     )
-    groups = 2
     if near:
         *down_received, up_parts[1], grad_y, other = together(
             [*down_received, up_parts[1], grad_y, other]
@@ -750,63 +749,67 @@
         others = [swap_inner(counts, k, inner) for k in range(1, inner)]
         parts = scatter_core(*up_parts)
         down_mine = add(down_parts[0], *down_received)
-        *values, grad_y = together([*parts, *others, grad_y])
+        *values, grad_y, down_mine = together([*parts, *others, grad_y, down_mine])
         parts, others = values[:4], values[4:]
+        counts = sum(others, counts)
         received = scatter_sides(parts)
-        down_inner = scatter_inner(down_mine, inner)
+        size = down_mine.shape[0] // inner
+        pieces = [down_mine[k * size : (k + 1) * size] for k in range(inner)]
+        pieces = by_bits(pieces, lax.axis_index("fsdp"))
+        down_inner = [swap_inner(pieces[k], k, inner) for k in range(1, inner - 1)]
     grad_y = grad_y.reshape(tokens.shape)
-    dqkv, *early = backward(grad_y, saved, me, groups, 0, second)
+    dqkv, *early = backward(grad_y, saved, me, *second)
     if near:
-        received[0], received[1], dqkv, early[1], *down_inner = together(
-            [received[0], received[1], dqkv, early[1], *down_inner]
+        *values, dqkv, early[1], piece, counts = together(
+            [*received, *down_inner, dqkv, early[1], pieces[-1], counts]
         )
-        counts = sum(others, counts)
+        received, down_inner = values[:3], values[3:]
         other = swap(counts, NEAR_Y)
+        down_inner.append(swap_inner(piece, inner - 1, inner))
         early_parts = scatter_core(*early)
-        dqkv, *early_parts = together([dqkv, *early_parts])
+        up_mine = add(parts[0], *received)
+        size = up_mine.shape[0] // inner
+        up_pieces = [up_mine[k * size : (k + 1) * size] for k in range(inner)]
+        up_pieces = by_bits(up_pieces, lax.axis_index("fsdp"))
+        *values, dqkv, other = together([*early_parts, *down_inner, *up_pieces, dqkv, other])
+        early_parts, down_inner = values[:4], values[4 : 3 + inner]
+        up_pieces = values[3 + inner :]
+        counts = double_tables(counts, other, NEAR_Y)
+        down_sum = sum_parts(pieces[:1] + down_inner)
         early_received = scatter_sides(early_parts)
-    tokens_grad, *late = backward(
-        grad_y, saved, me, 1, groups, second, (tokens, vec, dqkv, ffn_sums, first)
-    )
+        up_inner = [swap_inner(up_pieces[k], k, inner) for k in range(1, inner - 1)]
+    tokens_grad, *late = finish(grad_y, tokens, dqkv, vec, ffn_sums, me, *first)
     if near:
-        *values, tokens_grad, late[1], other = together(
-            [*received, *early_received, tokens_grad, late[1], other]
+        *values, tokens_grad, late[1], piece, counts = together(
+            [*early_received, *up_inner, tokens_grad, late[1], up_pieces[-1], counts]
         )
-        received, early_received = values[:3], values[3:]
+        early_received, up_inner = values[:3], values[3:]
         late_parts = scatter_core(*late)
-        up_mine = add(parts[0], *received)
+        other = swap(counts, NEAR_X)
+        *late_parts, other = together([*late_parts, other])
+        counts = double_tables(counts, other, NEAR_X)
+        other = swap(counts, CORE)
+        up_inner.append(swap_inner(piece, inner - 1, inner))
         early_mine = add(early_parts[0], *early_received)
-        joined = jnp.concatenate([up_mine, early_mine], axis=1)
+        early_sum = sum_parts(scatter_inner(early_mine, inner))
         late_received = scatter_sides(late_parts)
-        *joined, late_mine = together(
-            [*scatter_inner(joined, inner), add(late_parts[0], *late_received)]
-        )
-        joined_sum = sum_parts(joined)
-        up_sum, early_sum = joined_sum[:, : up_mine.shape[1]], joined_sum[:, up_mine.shape[1] :]
-        down_sum = sum_parts(down_inner)
+        up_sum = sum_parts(up_pieces[:1] + up_inner)
+        late_mine, other = together([add(late_parts[0], *late_received), other])
         late_sum = sum_parts(scatter_inner(late_mine, inner))
-        for bit, following in ((NEAR_Y, NEAR_X), (NEAR_X, CORE), (CORE, None)):
-            counts = double_tables(counts, other, bit)
-            if following is not None:
-                other = swap(counts, following)
+        counts = double_tables(counts, other, CORE)
     else:
         up_sum, down_sum, early_sum, late_sum = [
             scatter_whole(*v) for v in (up_parts, down_parts, early, late)
         ]
-    part = width * groups // 3
-    grads = []
-    for place in range(3):
-        grads.append(early_sum[:, place * part : (place + 1) * part])
-        grads.append(late_sum[:, place * (width - part) : (place + 1) * (width - part)])
     hidden = active.shape[1]
     return (
         layer_output.reshape(tokens.shape),
         tokens_grad,
-        jnp.concatenate(grads, axis=1),
+        early_sum,
         up_sum[:, hidden:],
         up_sum[:, :hidden],
         down_sum,
-        late_sum[:, 3 * (width - part) :],
+        late_sum,
         counts,
     )
 
@@ -831,6 +834,7 @@
     vectors = jnp.pad(vectors, ((0, 0), (0, 124)))
     ids = bucket_ids.reshape(-1, bucket_ids.shape[2]).T
     counts = count_buckets(ids)
+    segments = segment_ids[:, :, None]
     shards = (
         jnp.concatenate([qkv_weight, vectors], axis=1),
         jnp.concatenate([up_weight, out_weight], axis=1),
@@ -838,13 +842,13 @@
     )
     if direct(ranks, inner):
         me = lax.axis_index("dp").reshape(1).astype(jnp.int32)
-        front = gather_first(shards, inner, counts)
+        *front, segments = gather_first(shards, inner, counts, segments)
     else:
         me = jnp.zeros((1,), jnp.int32)
         front = [gather_whole(shard) for shard in shards]
         counts = lax.psum(counts, BOTH)
     *results, vec_sums, counts = layer(
-        ranks, inner, tokens, segment_ids, cotangent, me, front, counts
+        ranks, inner, tokens, segments, cotangent, me, front, counts
     )
     return (*results, *[vec_sums[:, place] for place in range(4)], counts)
 

time: 296 us -> 299 us (1.010)
  waiting for transfers between devices: 54.9 us -> 68.9 us
  other arithmetic: 22.1 us -> 14.9 us
  Pallas kernels: 137 us -> 131 us
  local copies, waits for them, and re-layouts: 7.75 us -> 11.8 us
    ppermute x21 -> x24, waiting for transfers between devices: 30.6 us -> 39.6 us  [swap_inner(): return lax.ppermute(value, 'fsdp', [(i, i ^ bit) for i in range(size)])]
    pallas_call x2, Pallas kernels: 45.4 us -> 39.2 us  [the longest x1 27.6 us: backward(): pl.pallas_call(functools.partial(backward_kernel, plan, len(pieces), grou...]
    ppermute x34, waiting for transfers between devices: 24.3 us -> 29.3 us  [swap(): return lax.ppermute(value, 'dp', [(i, i ^ bit) for i in range(BLOCKS)])]
    unnamed x67 -> x31, local copies, waits for them, and re-layouts: 4.51 us -> 8.58 us
    ppermute x34, starting transfers between devices: 31.7 us -> 28.3 us  [swap(): return lax.ppermute(value, 'dp', [(i, i ^ bit) for i in range(BLOCKS)])]
    convert_element_type x8, other arithmetic: 8.22 us -> 5.16 us  [add(): return total.astype(jnp.bfloat16)]
    ppermute x21 -> x24, starting transfers between devices: 37.5 us -> 38.9 us  [swap_inner(): return lax.ppermute(value, 'fsdp', [(i, i ^ bit) for i in range(size)])]
  transfers between devices with their start and end apart: 55 -> 58, of which waited for: 18 -> 21; matrix products, arithmetic and copies ran while one was open for 6% -> 5% of each run, Pallas kernels for 47% -> 44%
where the time goes in v1:
time: 299 us; the launch traced here: 295 us
  Pallas kernels  131 us (44%)
  waiting for transfers between devices  68.9 us (23%)
  starting transfers between devices  67.2 us (22%)
  other arithmetic  14.9 us (5%)
  local copies, waits for them, and re-layouts  11.8 us (4%)
    ppermute x24, waiting for transfers between devices, swap_inner(): return lax.ppermute(value, 'fsdp', [(i, i ^ bit) for i in range(size)])  39.6 us
    ppermute x24, starting transfers between devices, swap_inner(): return lax.ppermute(value, 'fsdp', [(i, i ^ bit) for i in range(size)])  38.9 us
    pallas_call x1, Pallas kernels, feed_return(): pl.pallas_call(functools.partial(return_kernel, plan, len(pieces), plan_d...  37.1 us
    ppermute x34, waiting for transfers between devices, swap(): return lax.ppermute(value, 'dp', [(i, i ^ bit) for i in range(BLOCKS)])  29.3 us
    ppermute x34, starting transfers between devices, swap(): return lax.ppermute(value, 'dp', [(i, i ^ bit) for i in range(BLOCKS)])  28.3 us
    pallas_call x1, Pallas kernels, backward(): pl.pallas_call(functools.partial(backward_kernel, plan, len(pieces), grou...  27.6 us
    pallas_call x1, Pallas kernels, feed_forward(): pl.pallas_call(functools.partial(forward_kernel, plan, len(pieces)), grid...  26.7 us
    pallas_call x1, Pallas kernels, attend(): pl.pallas_call(functools.partial(attend_kernel, plan, len(pieces)), grid=...  24.7 us
  transfers between devices with their start and end apart: 58, of which 21 were waited for; matrix products, arithmetic and copies ran while one was open for 5% of the time, Pallas kernels for 44%

profile of v1, /device:TPU:0, one launch (start us, length us, event | category | flops | bytes accessed | tf_op | source)
XLA Modules:
  0.0 295.0 jit_solution(17122242259515451657)
XLA Ops:
  1.5 0.9 fusion.13
  2.4 3.1 %collective-permute-start.2 = (bf16[24,2432]{1,0:T(8,128)(2,1)S(1)}, bf16[24,2432]{1,0:T(8,128)(2,1)S(1)}, u32[]{:S(2)}, u32[]{:S(2)}) collective-permute-start(bf16[24,2432]{1,0:T(8,128)(2,1)S(1)} %fusion.13), channel_id=1, source_target_pairs={{0,1},{1,0},{2,3},{3,2},{4,5},{5,4},{6,7},{7,6},{8,9},{9,8},{10,11... | collective-permute-start | bytes 350216 | tf_op jit(solution)/shard_map/ppermute | solution.py:24
  5.5 2.6 collective-permute-start.1
  8.1 0.9 pad_maximum_fusion.6
  9.0 3.0 %shard_map.203 = s32[8,64,256]{2,1,0:T(8,128)} custom-call(s32[8,1024]{1,0:T(8,128)} %bitcast.87), custom_call_target="tpu_custom_call" | custom-call | flops 3000000000 | bytes 1000000 | tf_op jit(solution)/shard_map/pallas_call | solution.py:187
  12.0 1.3 copy.34
  13.4 3.9 %collective-permute-done.1 = bf16[24,2432]{1,0:T(8,128)(2,1)S(1)} collective-permute-done((bf16[24,2432]{1,0:T(8,128)(2,1)S(1)}, bf16[24,2432]{1,0:T(8,128)(2,1)S(1)}, u32[]{:S(2)}, u32[]{:S(2)}) %collective-permute-start.1) | collective-permute-done | bytes 116768 | tf_op jit(solution)/shard_map/ppermute | solution.py:24
  17.5 2.5 collective-permute-start.5
  21.0 2.5 collective-permute-start.8
  24.3 4.8 %collective-permute-done.8 = bf16[24,3840]{1,0:T(8,128)(2,1)S(1)} collective-permute-done((bf16[24,3840]{1,0:T(8,128)(2,1)S(1)}, bf16[24,3840]{1,0:T(8,128)(2,1)S(1)}, u32[]{:S(2)}, u32[]{:S(2)}) %collective-permute-start.8) | collective-permute-done | bytes 184352 | tf_op jit(solution)/shard_map/ppermute | solution.py:24
  29.1 6.5 %collective-permute-start.6 = (bf16[24,3840]{1,0:T(8,128)(2,1)S(1)}, bf16[24,3840]{1,0:T(8,128)(2,1)S(1)}, u32[]{:S(2)}, u32[]{:S(2)}) collective-permute-start(bf16[24,3840]{1,0:T(8,128)(2,1)S(1)} %pad_maximum_fusion.6), channel_id=1, source_target_pairs={{0,1},{1,0},{2,3},{3,2},{4,5},{5,4},{6,7},{7,6},{8,9},{9,8},{10,11... | collective-permute-start | bytes 552968 | tf_op jit(solution)/shard_map/ppermute | solution.py:24
  35.7 2.3 collective-permute-done.7
  38.0 3.4 %collective-permute-done.6 = bf16[24,3840]{1,0:T(8,128)(2,1)S(1)} collective-permute-done((bf16[24,3840]{1,0:T(8,128)(2,1)S(1)}, bf16[24,3840]{1,0:T(8,128)(2,1)S(1)}, u32[]{:S(2)}, u32[]{:S(2)}) %collective-permute-start.6) | collective-permute-done | bytes 184352 | tf_op jit(solution)/shard_map/ppermute | solution.py:24
  43.0 3.0 %collective-permute-done.9 = s32[4,16384]{1,0:T(4,128)S(1)} collective-permute-done((s32[4,16384]{1,0:T(4,128)S(1)}, s32[4,16384]{1,0:T(4,128)S(1)}, u32[]{:S(2)}, u32[]{:S(2)}) %collective-permute-start.9) | collective-permute-done | bytes 262176 | tf_op jit(solution)/shard_map/ppermute | solution.py:20
  46.1 1.3 copy-done.4
  47.3 2.4 collective-permute-start.13
  50.8 1.3 collective-permute-start.15
  52.9 1.0 copy.33.seg_ref
  54.0 24.7 %shard_map.204 = (bf16[2,512,2304]{2,1,0:T(8,128)(2,1)}, bf16[2,12,512,512]{3,2,1,0:T(8,128)(2,1)}, f32[2,12,1,512]{3,2,1,0:T(1,128)}, bf16[2,768,512]{2,1,0:T(8...) custom-call(s32[1]{0:T(128)} %bitcast.me_ref, ...), custom_call_target="tpu_custom_call" | custom-call | flops 1000000000 | bytes 1000000 | tf_op jit(solution)/shard_map/pallas_call | solution.py:292
  78.7 3.9 %collective-permute-done.12 = bf16[96,3840]{1,0:T(8,128)(2,1)S(1)} collective-permute-done((bf16[96,3840]{1,0:T(8,128)(2,1)S(1)}, bf16[96,3840]{1,0:T(8,128)(2,1)S(1)}, u32[]{:S(2)}, u32[]{:S(2)}) %collective-permute-start.12) | collective-permute-done | bytes 737312 | tf_op jit(solution)/shard_map/ppermute | solution.py:20
  82.7 1.5 collective-permute-start.16
  85.2 5.2 %collective-permute-done.16 = bf16[96,768]{1,0:T(8,128)(2,1)S(1)} collective-permute-done((bf16[96,768]{1,0:T(8,128)(2,1)}, bf16[96,768]{1,0:T(8,128)(2,1)S(1)}, u32[]{:S(2)}, u32[]{:S(2)}) %collective-permute-start.16) | collective-permute-done | bytes 147488 | tf_op jit(solution)/shard_map/ppermute | solution.py:24
  90.4 1.1 broadcast_select_fusion.30
  91.6 1.6 copy-done.1
  93.2 1.1 collective-permute-start.20
  94.3 1.9 collective-permute-start.19
  96.8 1.6 collective-permute-start.21
  98.3 26.7 %shard_map.205 = (f32[1024,768]{1,0:T(8,128)}, bf16[768,1024]{1,0:T(8,128)(2,1)}, bf16[4,384,768]{2,1,0:T(8,128)(2,1)}, bf16[4,384,768]{2,1,0:T(8,128)(2,1)}, bf...) custom-call(s32[1]{0:T(128)} %bitcast.me_ref, bf16[1024,768]{1,0:T(8,128)(2,1)} %bitcast.60, ...), custom_call_target="tpu_custom_call" | custom-call | flops 1000000000 | bytes 1000000 | tf_op jit(solution)/shard_map/pallas_call | solution.py:379
  125.5 2.1 copy-done.14
  127.7 5.7 %collective-permute-done.22 = bf16[4,384,768]{2,1,0:T(8,128)(2,1)S(1)} collective-permute-done((bf16[4,384,768]{2,1,0:T(8,128)(2,1)S(1)}, bf16[4,384,768]{2,1,0:T(8,128)(2,1)S(1)}, u32[]{:S(2)}, u32[]{:S(2)}) %collective-permute-start.22) | collective-permute-done | bytes 2359328 | tf_op jit(solution)/shard_map/ppermute | solution.py:20
  133.4 1.6 fusion.7
  135.6 1.6 collective-permute-start.25
  137.2 1.3 collective-permute-start.26
  138.9 1.4 copy-done.6
  140.3 37.1 %shard_map.206 = (f32[1024,768]{1,0:T(8,128)}, bf16[1024,768]{1,0:T(8,128)(2,1)}, bf16[4,96,3840]{2,1,0:T(8,128)(2,1)}, bf16[4,96,3840]{2,1,0:T(8,128)(2,1)}, f32[8,768]{1,0:T(8,128)}) custom-call(s32[1]{0:T(128)} %bitcast.me_ref, f32[1024,768]{1,0:T(8,128)} %get-tuple-element.159.y_ref, bf16[1024,768]{1,0:T(8,128)(2,1)} %bitcast.64, ...), custom_call_target="tpu_custom_call" | custom-call | flops 1000000000 | bytes 1000000 | tf_op jit(solution)/shard_map/pallas_call | solution.py:487
  177.7 1.6 collective-permute-start.31
  179.3 1.9 collective-permute-start.30
  181.2 0.9 collective-permute-start.29
  182.2 1.7 add_convert_fusion.5
  184.6 3.3 %collective-permute-done.30 = s32[1,16384]{1,0:T(1,128)S(1)} collective-permute-done((s32[1,16384]{1,0:T(1,128)S(1)}, s32[1,16384]{1,0:T(1,128)S(1)}, u32[]{:S(2)}, u32[]{:S(2)}) %collective-permute-start.30) | collective-permute-done | bytes 65568 | tf_op jit(solution)/shard_map/ppermute | solution.py:24
  188.7 2.5 collective-permute-start.36
  191.2 2.0 collective-permute-start.32
  193.5 1.1 collective-permute-start.34
  194.8 27.6 %shard_map.207 = (bf16[2,512,2304]{2,1,0:T(8,128)(2,1)}, bf16[4,96,2304]{2,1,0:T(8,128)(2,1)}, bf16[4,96,2304]{2,1,0:T(8,128)(2,1)}) custom-call(s32[1]{0:T(128)} %bitcast.me_ref, f32[2,512,768]{2,1,0:T(8,128)} %bitcast.61, bf16[2,512,2304]{2,1,0:T(8,128)(2,1)} %get-tuple-element.184.q_ref.k_ref.v_ref, ...), custom_call_target="tpu_custom_call" | custom-call | flops 1000000000 | bytes 1000000 | tf_op jit(solution)/shard_map/pallas_call | solution.py:637
  222.5 4.1 %collective-permute-done.33 = bf16[96,3840]{1,0:T(8,128)(2,1)S(1)} collective-permute-done((bf16[96,3840]{1,0:T(8,128)(2,1)S(1)}, bf16[96,3840]{1,0:T(8,128)(2,1)S(1)}, u32[]{:S(2)}, u32[]{:S(2)}) %collective-permute-start.33) | collective-permute-done | bytes 737312 | tf_op jit(solution)/shard_map/ppermute | solution.py:20
  227.0 1.0 collective-permute-start.38
  228.4 3.5 %collective-permute-done.37 = bf16[4,96,2304]{2,1,0:T(8,128)(2,1)S(1)} collective-permute-done((bf16[4,96,2304]{2,1,0:T(8,128)(2,1)}, bf16[4,96,2304]{2,1,0:T(8,128)(2,1)S(1)}, u32[]{:S(2)}, u32[]{:S(2)}) %collective-permute-start.37) | collective-permute-done | bytes 1769504 | tf_op jit(solution)/shard_map/ppermute | solution.py:20
  232.4 1.9 collective-permute-done.38
  236.0 1.5 collective-permute-start.40
  238.2 1.2 collective-permute-start.42
  239.6 11.6 %shard_map.208 = (bf16[2,512,768]{2,1,0:T(8,128)(2,1)}, bf16[4,96,128]{2,1,0:T(8,128)(2,1)}, bf16[4,96,128]{2,1,0:T(8,128)(2,1)}) custom-call(s32[1]{0:T(128)} %bitcast.me_ref, f32[2,512,768]{2,1,0:T(8,128)} %bitcast.62, bf16[2,512,768]{2,1,0:T(8,128)(2,1)} %x_ref.3, bf16[2,512,2304]{2,1,0:T(8,128)(2,1)} %get-tuple-element.213.dqkv_ref, ...), custom_call_target="tpu_custom_call" | custom-call | flops 1000000000 | bytes 1000000 | tf_op jit(solution)/shard_map/pallas_call | solution.py:693
  252.0 6.2 %collective-permute-done.42 = bf16[96,2304]{1,0:T(8,128)(2,1)S(1)} collective-permute-done((bf16[96,2304]{1,0:T(8,128)(2,1)S(1)}, bf16[96,2304]{1,0:T(8,128)(2,1)S(1)}, u32[]{:S(2)}, u32[]{:S(2)}) %collective-permute-start.42) | collective-permute-done | bytes 442400 | tf_op jit(solution)/shard_map/ppermute | solution.py:20
  258.8 1.0 collective-permute-start.48
  260.2 3.4 %collective-permute-start.46 = (bf16[24,2304]{1,0:T(8,128)(2,1)S(1)}, bf16[24,2304]{1,0:T(8,128)(2,1)S(1)}, u32[]{:S(2)}, u32[]{:S(2)}) collective-permute-start(bf16[24,2304]{1,0:T(8,128)(2,1)S(1)} %get-tuple-element.279), channel_id=1, source_target_pairs={{0,2},{1,3},{2,0},{3,1},{4,6},{5,7},{6,4},{7,5},{8,10},{9,11},{10,... | collective-permute-start | bytes 331784 | tf_op jit(solution)/shard_map/ppermute | solution.py:24
  263.6 1.0 collective-permute-start.47
  264.6 4.7 %collective-permute-done.45 = bf16[24,2304]{1,0:T(8,128)(2,1)S(1)} collective-permute-done((bf16[24,2304]{1,0:T(8,128)(2,1)S(1)}, bf16[24,2304]{1,0:T(8,128)(2,1)S(1)}, u32[]{:S(2)}, u32[]{:S(2)}) %collective-permute-start.45) | collective-permute-done | bytes 110624 | tf_op jit(solution)/shard_map/ppermute | solution.py:24
  269.3 7.8 %collective-permute-done.46 = bf16[24,2304]{1,0:T(8,128)(2,1)S(1)} collective-permute-done((bf16[24,2304]{1,0:T(8,128)(2,1)S(1)}, bf16[24,2304]{1,0:T(8,128)(2,1)S(1)}, u32[]{:S(2)}, u32[]{:S(2)}) %collective-permute-start.46) | collective-permute-done | bytes 110624 | tf_op jit(solution)/shard_map/ppermute | solution.py:24
  277.9 1.4 collective-permute-start.51
  279.8 1.6 collective-permute-start.53
  281.9 1.2 collective-permute-done.52
  283.2 1.4 collective-permute-done.53
  286.2 2.3 collective-permute-start.55
  288.5 2.4 collective-permute-start.57
  291.9 1.2 collective-permute-done.56
  (135 shorter events, 23.4 us)
Async XLA Ops:
  2.4 11.0 %collective-permute-start.2 = (bf16[24,2432]{1,0:T(8,128)(2,1)S(1)}, bf16[24,2432]{1,0:T(8,128)(2,1)S(1)}, u32[]{:S(2)}, u32[]{:S(2)}) collective-permute-start(bf16[24,2432]{1,0:T(8,128)(2,1)S(1)} %fusion.13), channel_id=1, source_target_pairs={{0,1},{1,0},{2,3},{3,2},{4,5},{5,4},{6,7},{7,6},{8,9},{9,8},{10,11... | collective-permute-start | bytes 350216 | tf_op jit(solution)/shard_map/ppermute | solution.py:24
  5.5 11.9 %collective-permute-start.1 = (bf16[24,2432]{1,0:T(8,128)(2,1)S(1)}, bf16[24,2432]{1,0:T(8,128)(2,1)S(1)}, u32[]{:S(2)}, u32[]{:S(2)}) collective-permute-start(bf16[24,2432]{1,0:T(8,128)(2,1)S(1)} %fusion.13), channel_id=1, source_target_pairs={{0,2},{1,3},{2,0},{3,1},{4,6},{5,7},{6,4},{7,5},{8,10},{9,11},{10,... | collective-permute-start | bytes 350216 | tf_op jit(solution)/shard_map/ppermute | solution.py:24
  8.0 9.3 %collective-permute-start = (bf16[24,2432]{1,0:T(8,128)(2,1)S(1)}, bf16[24,2432]{1,0:T(8,128)(2,1)S(1)}, u32[]{:S(2)}, u32[]{:S(2)}) collective-permute-start(bf16[24,2432]{1,0:T(8,128)(2,1)S(1)} %fusion.13), channel_id=1, source_target_pairs={{0,3},{1,2},{2,1},{3,0},{4,7},{5,6},{6,5},{7,4},{8,11},{9,10},{10,... | collective-permute-start | bytes 350216 | tf_op jit(solution)/shard_map/ppermute | solution.py:24
  9.0 8.3 %copy-start.9 = (bf16[24,2304]{1,0:T(8,128)(2,1)S(1)}, bf16[24,2304]{1,0:T(8,128)(2,1)}, u32[]{:S(2)}) copy-start(bf16[24,2304]{1,0:T(8,128)(2,1)} %param.16) | copy-start | bytes 331780
  17.5 24.0 %collective-permute-start.5 = (bf16[96,2432]{1,0:T(8,128)(2,1)S(1)}, bf16[96,2432]{1,0:T(8,128)(2,1)S(1)}, u32[]{:S(2)}, u32[]{:S(2)}) collective-permute-start(bf16[96,2432]{1,0:T(8,128)(2,1)S(1)} %pad_maximum_fusion.5), channel_id=1, source_target_pairs={{0,24},{4,28},{8,16},{12,20},{16,8},{20,12},{24,0},{28,4},{1,25},{... | collective-permute-start | bytes 1400840 | tf_op jit(solution)/shard_map/ppermute | solution.py:20
  20.0 21.5 %collective-permute-start.4 = (bf16[96,2432]{1,0:T(8,128)(2,1)S(1)}, bf16[96,2432]{1,0:T(8,128)(2,1)S(1)}, u32[]{:S(2)}, u32[]{:S(2)}) collective-permute-start(bf16[96,2432]{1,0:T(8,128)(2,1)S(1)} %pad_maximum_fusion.5), channel_id=1, source_target_pairs={{0,16},{4,20},{8,24},{12,28},{16,0},{20,4},{24,8},{28,12},{1,17},{... | collective-permute-start | bytes 1400840 | tf_op jit(solution)/shard_map/ppermute | solution.py:20
  20.5 21.0 %collective-permute-start.3 = (bf16[96,2432]{1,0:T(8,128)(2,1)S(1)}, bf16[96,2432]{1,0:T(8,128)(2,1)S(1)}, u32[]{:S(2)}, u32[]{:S(2)}) collective-permute-start(bf16[96,2432]{1,0:T(8,128)(2,1)S(1)} %pad_maximum_fusion.5), channel_id=1, source_target_pairs={{0,8},{4,12},{8,0},{12,4},{16,24},{20,28},{24,16},{28,20},{1,9},{5... | collective-permute-start | bytes 1400840 | tf_op jit(solution)/shard_map/ppermute | solution.py:20
  21.0 8.1 %collective-permute-start.8 = (bf16[24,3840]{1,0:T(8,128)(2,1)S(1)}, bf16[24,3840]{1,0:T(8,128)(2,1)S(1)}, u32[]{:S(2)}, u32[]{:S(2)}) collective-permute-start(bf16[24,3840]{1,0:T(8,128)(2,1)S(1)} %pad_maximum_fusion.6), channel_id=1, source_target_pairs={{0,3},{1,2},{2,1},{3,0},{4,7},{5,6},{6,5},{7,4},{8,11},{9,10},{10,... | collective-permute-start | bytes 552968 | tf_op jit(solution)/shard_map/ppermute | solution.py:24
  23.5 14.5 %collective-permute-start.7 = (bf16[24,3840]{1,0:T(8,128)(2,1)S(1)}, bf16[24,3840]{1,0:T(8,128)(2,1)S(1)}, u32[]{:S(2)}, u32[]{:S(2)}) collective-permute-start(bf16[24,3840]{1,0:T(8,128)(2,1)S(1)} %pad_maximum_fusion.6), channel_id=1, source_target_pairs={{0,2},{1,3},{2,0},{3,1},{4,6},{5,7},{6,4},{7,5},{8,10},{9,11},{10,... | collective-permute-start | bytes 552968 | tf_op jit(solution)/shard_map/ppermute | solution.py:24
  29.1 12.3 %collective-permute-start.6 = (bf16[24,3840]{1,0:T(8,128)(2,1)S(1)}, bf16[24,3840]{1,0:T(8,128)(2,1)S(1)}, u32[]{:S(2)}, u32[]{:S(2)}) collective-permute-start(bf16[24,3840]{1,0:T(8,128)(2,1)S(1)} %pad_maximum_fusion.6), channel_id=1, source_target_pairs={{0,1},{1,0},{2,3},{3,2},{4,5},{5,4},{6,7},{7,6},{8,9},{9,8},{10,11... | collective-permute-start | bytes 552968 | tf_op jit(solution)/shard_map/ppermute | solution.py:24
  41.8 4.3 %collective-permute-start.10 = (bf16[4,96,2432]{2,1,0:T(8,128)(2,1)S(1)}, bf16[4,96,2432]{2,1,0:T(8,128)(2,1)S(1)}, u32[]{:S(2)}, u32[]{:S(2)}) collective-permute-start(bf16[4,96,2432]{2,1,0:T(8,128)(2,1)S(1)} %pad_maximum_fusion.2.rest_0_), channel_id=1, source_target_pairs={{0,4},{4,0},{8,12},{12,8},{16,20},{20,16},{24,28},{28,24},{1,5},{5... | collective-permute-start | bytes 5603336 | tf_op jit(solution)/shard_map/ppermute | solution.py:20
  41.9 11.0 %copy-start.13 = (s32[2,512]{1,0:T(2,128)S(1)}, s32[2,512]{1,0:T(2,128)}, u32[]{:S(2)}) copy-start(s32[2,512]{1,0:T(2,128)} %param.13) | copy-start | bytes 12292
  42.0 4.1 %collective-permute-start.9 = (s32[4,16384]{1,0:T(4,128)S(1)}, s32[4,16384]{1,0:T(4,128)S(1)}, u32[]{:S(2)}, u32[]{:S(2)}) collective-permute-start(s32[4,16384]{1,0:T(4,128)S(1)} %slice_select_fusion), channel_id=1, source_target_pairs={{0,4},{4,0},{8,12},{12,8},{16,20},{20,16},{24,28},{28,24},{1,5},{5... | collective-permute-start | bytes 786440 | tf_op jit(solution)/shard_map/ppermute | solution.py:20
  47.3 31.4 %collective-permute-start.13 = (bf16[96,3840]{1,0:T(8,128)(2,1)S(1)}, bf16[96,3840]{1,0:T(8,128)(2,1)S(1)}, u32[]{:S(2)}, u32[]{:S(2)}) collective-permute-start(bf16[96,3840]{1,0:T(8,128)(2,1)S(1)} %pad_maximum_fusion.3), channel_id=1, source_target_pairs={{0,24},{4,28},{8,16},{12,20},{16,8},{20,12},{24,0},{28,4},{1,25},{... | collective-permute-start | bytes 2211848 | tf_op jit(solution)/shard_map/ppermute | solution.py:20
  49.8 32.8 %collective-permute-start.12 = (bf16[96,3840]{1,0:T(8,128)(2,1)S(1)}, bf16[96,3840]{1,0:T(8,128)(2,1)S(1)}, u32[]{:S(2)}, u32[]{:S(2)}) collective-permute-start(bf16[96,3840]{1,0:T(8,128)(2,1)S(1)} %pad_maximum_fusion.3), channel_id=1, source_target_pairs={{0,16},{4,20},{8,24},{12,28},{16,0},{20,4},{24,8},{28,12},{1,17},{... | collective-permute-start | bytes 2211848 | tf_op jit(solution)/shard_map/ppermute | solution.py:20
  50.3 32.4 %collective-permute-start.11 = (bf16[96,3840]{1,0:T(8,128)(2,1)S(1)}, bf16[96,3840]{1,0:T(8,128)(2,1)S(1)}, u32[]{:S(2)}, u32[]{:S(2)}) collective-permute-start(bf16[96,3840]{1,0:T(8,128)(2,1)S(1)} %pad_maximum_fusion.3), channel_id=1, source_target_pairs={{0,8},{4,12},{8,0},{12,4},{16,24},{20,28},{24,16},{28,20},{1,9},{5... | collective-permute-start | bytes 2211848 | tf_op jit(solution)/shard_map/ppermute | solution.py:20
  50.8 27.8 %collective-permute-start.15 = (bf16[96,768]{1,0:T(8,128)(2,1)}, bf16[96,768]{1,0:T(8,128)(2,1)}, u32[]{:S(2)}, u32[]{:S(2)}) collective-permute-start(bf16[96,768]{1,0:T(8,128)(2,1)} %param.19), channel_id=1, source_target_pairs={{0,2},{1,3},{2,0},{3,1},{4,6},{5,7},{6,4},{7,5},{8,10},{9,11},{10,... | collective-permute-start | bytes 442376 | tf_op jit(solution)/shard_map/ppermute | solution.py:24
  52.2 26.5 %collective-permute-start.14 = (bf16[96,768]{1,0:T(8,128)(2,1)}, bf16[96,768]{1,0:T(8,128)(2,1)}, u32[]{:S(2)}, u32[]{:S(2)}) collective-permute-start(bf16[96,768]{1,0:T(8,128)(2,1)} %param.19), channel_id=1, source_target_pairs={{0,1},{1,0},{2,3},{3,2},{4,5},{5,4},{6,7},{7,6},{8,9},{9,8},{10,11... | collective-permute-start | bytes 442376 | tf_op jit(solution)/shard_map/ppermute | solution.py:24
  82.7 7.8 %collective-permute-start.16 = (bf16[96,768]{1,0:T(8,128)(2,1)}, bf16[96,768]{1,0:T(8,128)(2,1)S(1)}, u32[]{:S(2)}, u32[]{:S(2)}) collective-permute-start(bf16[96,768]{1,0:T(8,128)(2,1)} %param.19), channel_id=1, source_target_pairs={{0,3},{1,2},{2,1},{3,0},{4,7},{5,6},{6,5},{7,4},{8,11},{9,10},{10,... | collective-permute-start | bytes 442376 | tf_op jit(solution)/shard_map/ppermute | solution.py:24
  84.6 7.0 %copy-start = (bf16[4,96,3840]{2,1,0:T(8,128)(2,1)}, bf16[4,96,3840]{2,1,0:T(8,128)(2,1)S(1)}, u32[]{:S(2)}) copy-start(bf16[4,96,3840]{2,1,0:T(8,128)(2,1)S(1)} %pad_maximum_fusion.rest_0_) | copy-start | bytes 8847364
  84.6 7.0 %collective-permute-start.17 = (bf16[4,96,3840]{2,1,0:T(8,128)(2,1)S(1)}, bf16[4,96,3840]{2,1,0:T(8,128)(2,1)S(1)}, u32[]{:S(2)}, u32[]{:S(2)}) collective-permute-start(bf16[4,96,3840]{2,1,0:T(8,128)(2,1)S(1)} %pad_maximum_fusion.rest_0_), channel_id=1, source_target_pairs={{0,4},{4,0},{8,12},{12,8},{16,20},{20,16},{24,28},{28,24},{1,5},{5... | collective-permute-start | bytes 8847368 | tf_op jit(solution)/shard_map/ppermute | solution.py:20
  93.2 31.8 %collective-permute-start.20 = (bf16[384,768]{1,0:T(8,128)(2,1)S(1)}, bf16[384,768]{1,0:T(8,128)(2,1)S(1)}, u32[]{:S(2)}, u32[]{:S(2)}) collective-permute-start(bf16[384,768]{1,0:T(8,128)(2,1)S(1)} %pad_maximum_fusion.4), channel_id=1, source_target_pairs={{0,24},{4,28},{8,16},{12,20},{16,8},{20,12},{24,0},{28,4},{1,25},{... | collective-permute-start | bytes 1769480 | tf_op jit(solution)/shard_map/ppermute | solution.py:20
  94.3 30.8 %collective-permute-start.19 = (bf16[384,768]{1,0:T(8,128)(2,1)S(1)}, bf16[384,768]{1,0:T(8,128)(2,1)S(1)}, u32[]{:S(2)}, u32[]{:S(2)}) collective-permute-start(bf16[384,768]{1,0:T(8,128)(2,1)S(1)} %pad_maximum_fusion.4), channel_id=1, source_target_pairs={{0,16},{4,20},{8,24},{12,28},{16,0},{20,4},{24,8},{28,12},{1,17},{... | collective-permute-start | bytes 1769480 | tf_op jit(solution)/shard_map/ppermute | solution.py:20
  96.2 28.9 %collective-permute-start.18 = (bf16[384,768]{1,0:T(8,128)(2,1)S(1)}, bf16[384,768]{1,0:T(8,128)(2,1)S(1)}, u32[]{:S(2)}, u32[]{:S(2)}) collective-permute-start(bf16[384,768]{1,0:T(8,128)(2,1)S(1)} %pad_maximum_fusion.4), channel_id=1, source_target_pairs={{0,8},{4,12},{8,0},{12,4},{16,24},{20,28},{24,16},{28,20},{1,9},{5... | collective-permute-start | bytes 1769480 | tf_op jit(solution)/shard_map/ppermute | solution.py:20
  96.8 28.3 %collective-permute-start.21 = (s32[2,16384]{1,0:T(2,128)S(1)}, s32[2,16384]{1,0:T(2,128)S(1)}, u32[]{:S(2)}, u32[]{:S(2)}) collective-permute-start(s32[2,16384]{1,0:T(2,128)S(1)} %broadcast_select_fusion.37), channel_id=1, source_target_pairs={{0,8},{4,12},{8,0},{12,4},{16,24},{20,28},{24,16},{28,20},{1,9},{5... | collective-permute-start | bytes 393224 | tf_op jit(solution)/shard_map/ppermute | solution.py:20
  125.1 8.3 %copy-start.7 = (bf16[4,384,768]{2,1,0:T(8,128)(2,1)S(1)}, bf16[4,384,768]{2,1,0:T(8,128)(2,1)}, u32[]{:S(2)}) copy-start(bf16[4,384,768]{2,1,0:T(8,128)(2,1)} %get-tuple-element.157) | copy-start | bytes 7077892
  125.4 9.6 %copy-start.3 = (bf16[4,384,768]{2,1,0:T(8,128)(2,1)}, bf16[4,384,768]{2,1,0:T(8,128)(2,1)S(1)}, u32[]{:S(2)}) copy-start(bf16[4,384,768]{2,1,0:T(8,128)(2,1)S(1)} %pad_maximum_fusion.1.rest_2_) | copy-start | bytes 7077892
  125.4 13.5 %collective-permute-start.23 = (bf16[4,384,768]{2,1,0:T(8,128)(2,1)S(1)}, bf16[4,384,768]{2,1,0:T(8,128)(2,1)S(1)}, u32[]{:S(2)}, u32[]{:S(2)}) collective-permute-start(bf16[4,384,768]{2,1,0:T(8,128)(2,1)S(1)} %pad_maximum_fusion.1.rest_2_), channel_id=1, source_target_pairs={{0,4},{4,0},{8,12},{12,8},{16,20},{20,16},{24,28},{28,24},{1,5},{5... | collective-permute-start | bytes 7077896 | tf_op jit(solution)/shard_map/ppermute | solution.py:20
  127.6 5.8 %collective-permute-start.22 = (bf16[4,384,768]{2,1,0:T(8,128)(2,1)S(1)}, bf16[4,384,768]{2,1,0:T(8,128)(2,1)S(1)}, u32[]{:S(2)}, u32[]{:S(2)}) collective-permute-start(bf16[4,384,768]{2,1,0:T(8,128)(2,1)S(1)} %copy-done.14), channel_id=1, source_target_pairs={{0,4},{4,0},{8,12},{12,8},{16,20},{20,16},{24,28},{28,24},{1,5},{5... | collective-permute-start | bytes 7077896 | tf_op jit(solution)/shard_map/ppermute | solution.py:20
  135.0 42.5 %collective-permute-start.24 = (bf16[384,768]{1,0:T(8,128)(2,1)}, bf16[384,768]{1,0:T(8,128)(2,1)}, u32[]{:S(2)}, u32[]{:S(2)}) collective-permute-start(bf16[384,768]{1,0:T(8,128)(2,1)} %get-tuple-element.170), channel_id=1, source_target_pairs={{0,8},{4,12},{8,0},{12,4},{16,24},{20,28},{24,16},{28,20},{1,9},{5... | collective-permute-start | bytes 1769480 | tf_op jit(solution)/shard_map/ppermute | solution.py:20
  135.6 41.9 %collective-permute-start.25 = (bf16[384,768]{1,0:T(8,128)(2,1)}, bf16[384,768]{1,0:T(8,128)(2,1)}, u32[]{:S(2)}, u32[]{:S(2)}) collective-permute-start(bf16[384,768]{1,0:T(8,128)(2,1)} %get-tuple-element.171), channel_id=1, source_target_pairs={{0,16},{4,20},{8,24},{12,28},{16,0},{20,4},{24,8},{28,12},{1,17},{... | collective-permute-start | bytes 1769480 | tf_op jit(solution)/shard_map/ppermute | solution.py:20
  137.2 40.3 %collective-permute-start.26 = (bf16[384,768]{1,0:T(8,128)(2,1)S(1)}, bf16[384,768]{1,0:T(8,128)(2,1)}, u32[]{:S(2)}, u32[]{:S(2)}) collective-permute-start(bf16[384,768]{1,0:T(8,128)(2,1)S(1)} %get-tuple-element.172), channel_id=1, source_target_pairs={{0,24},{4,28},{8,16},{12,20},{16,8},{20,12},{24,0},{28,4},{1,25},{... | collective-permute-start | bytes 1769480 | tf_op jit(solution)/shard_map/ppermute | solution.py:20
  138.6 38.9 %collective-permute-start.27 = (s32[1,16384]{1,0:T(1,128)S(1)}, s32[1,16384]{1,0:T(1,128)S(1)}, u32[]{:S(2)}, u32[]{:S(2)}) collective-permute-start(s32[1,16384]{1,0:T(1,128)S(1)} %broadcast_select_fusion.34), channel_id=1, source_target_pairs={{0,16},{4,20},{8,24},{12,28},{16,0},{20,4},{24,8},{28,12},{1,17},{... | collective-permute-start | bytes 196616 | tf_op jit(solution)/shard_map/ppermute | solution.py:20
  177.5 6.4 %collective-permute-start.28 = (bf16[4,96,3840]{2,1,0:T(8,128)(2,1)}, bf16[4,96,3840]{2,1,0:T(8,128)(2,1)S(1)}, u32[]{:S(2)}, u32[]{:S(2)}) collective-permute-start(bf16[4,96,3840]{2,1,0:T(8,128)(2,1)} %get-tuple-element.176), channel_id=1, source_target_pairs={{0,4},{4,0},{8,12},{12,8},{16,20},{20,16},{24,28},{28,24},{1,5},{5... | collective-permute-start | bytes 8847368 | tf_op jit(solution)/shard_map/ppermute | solution.py:20
  177.7 6.9 %collective-permute-start.31 = (s32[1,16384]{1,0:T(1,128)S(1)}, s32[1,16384]{1,0:T(1,128)S(1)}, u32[]{:S(2)}, u32[]{:S(2)}) collective-permute-start(s32[1,16384]{1,0:T(1,128)S(1)} %fusion.14), channel_id=1, source_target_pairs={{0,3},{1,2},{2,1},{3,0},{4,7},{5,6},{6,5},{7,4},{8,11},{9,10},{10,... | collective-permute-start | bytes 196616 | tf_op jit(solution)/shard_map/ppermute | solution.py:24
  179.3 8.6 %collective-permute-start.30 = (s32[1,16384]{1,0:T(1,128)S(1)}, s32[1,16384]{1,0:T(1,128)S(1)}, u32[]{:S(2)}, u32[]{:S(2)}) collective-permute-start(s32[1,16384]{1,0:T(1,128)S(1)} %fusion.14), channel_id=1, source_target_pairs={{0,2},{1,3},{2,0},{3,1},{4,6},{5,7},{6,4},{7,5},{8,10},{9,11},{10,... | collective-permute-start | bytes 196616 | tf_op jit(solution)/shard_map/ppermute | solution.py:24
  181.2 6.7 %collective-permute-start.29 = (s32[1,16384]{1,0:T(1,128)S(1)}, s32[1,16384]{1,0:T(1,128)S(1)}, u32[]{:S(2)}, u32[]{:S(2)}) collective-permute-start(s32[1,16384]{1,0:T(1,128)S(1)} %fusion.14), channel_id=1, source_target_pairs={{0,1},{1,0},{2,3},{3,2},{4,5},{5,4},{6,7},{7,6},{8,9},{9,8},{10,11... | collective-permute-start | bytes 196616 | tf_op jit(solution)/shard_map/ppermute | solution.py:24
  188.7 33.7 %collective-permute-start.35 = (bf16[96,768]{1,0:T(8,128)(2,1)}, bf16[96,768]{1,0:T(8,128)(2,1)S(1)}, u32[]{:S(2)}, u32[]{:S(2)}) collective-permute-start(bf16[96,768]{1,0:T(8,128)(2,1)} %get-tuple-element.266), channel_id=1, source_target_pairs={{0,1},{1,0},{2,3},{3,2},{4,5},{5,4},{6,7},{7,6},{8,9},{9,8},{10,11... | collective-permute-start | bytes 442376 | tf_op jit(solution)/shard_map/ppermute | solution.py:24
  188.7 33.7 %collective-permute-start.36 = (bf16[96,768]{1,0:T(8,128)(2,1)}, bf16[96,768]{1,0:T(8,128)(2,1)S(1)}, u32[]{:S(2)}, u32[]{:S(2)}) collective-permute-start(bf16[96,768]{1,0:T(8,128)(2,1)} %get-tuple-element.267), channel_id=1, source_target_pairs={{0,2},{1,3},{2,0},{3,1},{4,6},{5,7},{6,4},{7,5},{8,10},{9,11},{10,... | collective-permute-start | bytes 442376 | tf_op jit(solution)/shard_map/ppermute | solution.py:24
  191.2 31.3 %collective-permute-start.32 = (bf16[96,3840]{1,0:T(8,128)(2,1)S(1)}, bf16[96,3840]{1,0:T(8,128)(2,1)S(1)}, u32[]{:S(2)}, u32[]{:S(2)}) collective-permute-start(bf16[96,3840]{1,0:T(8,128)(2,1)S(1)} %get-tuple-element.189), channel_id=1, source_target_pairs={{0,8},{4,12},{8,0},{12,4},{16,24},{20,28},{24,16},{28,20},{1,9},{5... | collective-permute-start | bytes 2211848 | tf_op jit(solution)/shard_map/ppermute | solution.py:20
  193.1 33.4 %collective-permute-start.33 = (bf16[96,3840]{1,0:T(8,128)(2,1)S(1)}, bf16[96,3840]{1,0:T(8,128)(2,1)S(1)}, u32[]{:S(2)}, u32[]{:S(2)}) collective-permute-start(bf16[96,3840]{1,0:T(8,128)(2,1)S(1)} %get-tuple-element.190), channel_id=1, source_target_pairs={{0,16},{4,20},{8,24},{12,28},{16,0},{20,4},{24,8},{28,12},{1,17},{... | collective-permute-start | bytes 2211848 | tf_op jit(solution)/shard_map/ppermute | solution.py:20
  193.5 33.0 %collective-permute-start.34 = (bf16[96,3840]{1,0:T(8,128)(2,1)S(1)}, bf16[96,3840]{1,0:T(8,128)(2,1)S(1)}, u32[]{:S(2)}, u32[]{:S(2)}) collective-permute-start(bf16[96,3840]{1,0:T(8,128)(2,1)S(1)} %get-tuple-element.191), channel_id=1, source_target_pairs={{0,24},{4,28},{8,16},{12,20},{16,8},{20,12},{24,0},{28,4},{1,25},{... | collective-permute-start | bytes 2211848 | tf_op jit(solution)/shard_map/ppermute | solution.py:20
  226.6 5.8 %collective-permute-start.39 = (s32[1,16384]{1,0:T(1,128)S(1)}, s32[1,16384]{1,0:T(1,128)S(1)}, u32[]{:S(2)}, u32[]{:S(2)}) collective-permute-start(s32[1,16384]{1,0:T(1,128)S(1)} %add_add_fusion), channel_id=1, source_target_pairs={{0,16},{4,20},{8,24},{12,28},{16,0},{20,4},{24,8},{28,12},{1,17},{... | collective-permute-start | bytes 196616 | tf_op jit(solution)/shard_map/ppermute | solution.py:20
  227.0 7.3 %collective-permute-start.38 = (bf16[96,768]{1,0:T(8,128)(2,1)}, bf16[96,768]{1,0:T(8,128)(2,1)S(1)}, u32[]{:S(2)}, u32[]{:S(2)}) collective-permute-start(bf16[96,768]{1,0:T(8,128)(2,1)} %get-tuple-element.201), channel_id=1, source_target_pairs={{0,3},{1,2},{2,1},{3,0},{4,7},{5,6},{6,5},{7,4},{8,11},{9,10},{10,... | collective-permute-start | bytes 442376 | tf_op jit(solution)/shard_map/ppermute | solution.py:24
  228.0 3.9 %collective-permute-start.37 = (bf16[4,96,2304]{2,1,0:T(8,128)(2,1)}, bf16[4,96,2304]{2,1,0:T(8,128)(2,1)S(1)}, u32[]{:S(2)}, u32[]{:S(2)}) collective-permute-start(bf16[4,96,2304]{2,1,0:T(8,128)(2,1)} %get-tuple-element.198), channel_id=1, source_target_pairs={{0,4},{4,0},{8,12},{12,8},{16,20},{20,16},{24,28},{28,24},{1,5},{5... | collective-permute-start | bytes 5308424 | tf_op jit(solution)/shard_map/ppermute | solution.py:20
  234.3 17.7 %collective-permute-start.43 = (bf16[24,3840]{1,0:T(8,128)(2,1)S(1)}, bf16[24,3840]{1,0:T(8,128)(2,1)S(1)}, u32[]{:S(2)}, u32[]{:S(2)}) collective-permute-start(bf16[24,3840]{1,0:T(8,128)(2,1)S(1)} %get-tuple-element.211), channel_id=1, source_target_pairs={{0,1},{1,0},{2,3},{3,2},{4,5},{5,4},{6,7},{7,6},{8,9},{9,8},{10,11... | collective-permute-start | bytes 552968 | tf_op jit(solution)/shard_map/ppermute | solution.py:24
  235.2 16.8 %collective-permute-start.44 = (bf16[24,3840]{1,0:T(8,128)(2,1)S(1)}, bf16[24,3840]{1,0:T(8,128)(2,1)S(1)}, u32[]{:S(2)}, u32[]{:S(2)}) collective-permute-start(bf16[24,3840]{1,0:T(8,128)(2,1)S(1)} %get-tuple-element.212), channel_id=1, source_target_pairs={{0,2},{1,3},{2,0},{3,1},{4,6},{5,7},{6,4},{7,5},{8,10},{9,11},{10,... | collective-permute-start | bytes 552968 | tf_op jit(solution)/shard_map/ppermute | solution.py:24
  236.0 16.1 %collective-permute-start.40 = (bf16[96,2304]{1,0:T(8,128)(2,1)S(1)}, bf16[96,2304]{1,0:T(8,128)(2,1)S(1)}, u32[]{:S(2)}, u32[]{:S(2)}) collective-permute-start(bf16[96,2304]{1,0:T(8,128)(2,1)S(1)} %get-tuple-element.208), channel_id=1, source_target_pairs={{0,8},{4,12},{8,0},{12,4},{16,24},{20,28},{24,16},{28,20},{1,9},{5... | collective-permute-start | bytes 1327112 | tf_op jit(solution)/shard_map/ppermute | solution.py:20
  237.4 14.6 %collective-permute-start.41 = (bf16[96,2304]{1,0:T(8,128)(2,1)S(1)}, bf16[96,2304]{1,0:T(8,128)(2,1)S(1)}, u32[]{:S(2)}, u32[]{:S(2)}) collective-permute-start(bf16[96,2304]{1,0:T(8,128)(2,1)S(1)} %get-tuple-element.209), channel_id=1, source_target_pairs={{0,16},{4,20},{8,24},{12,28},{16,0},{20,4},{24,8},{28,12},{1,17},{... | collective-permute-start | bytes 1327112 | tf_op jit(solution)/shard_map/ppermute | solution.py:20
  238.2 20.0 %collective-permute-start.42 = (bf16[96,2304]{1,0:T(8,128)(2,1)S(1)}, bf16[96,2304]{1,0:T(8,128)(2,1)S(1)}, u32[]{:S(2)}, u32[]{:S(2)}) collective-permute-start(bf16[96,2304]{1,0:T(8,128)(2,1)S(1)} %get-tuple-element.210), channel_id=1, source_target_pairs={{0,24},{4,28},{8,16},{12,20},{16,8},{20,12},{24,0},{28,4},{1,25},{... | collective-permute-start | bytes 1327112 | tf_op jit(solution)/shard_map/ppermute | solution.py:20
  252.0 12.5 %copy-start.12 = (bf16[4,96,128]{2,1,0:T(8,128)(2,1)S(1)}, bf16[4,96,128]{2,1,0:T(8,128)(2,1)}, u32[]{:S(2)}) copy-start(bf16[4,96,128]{2,1,0:T(8,128)(2,1)} %get-tuple-element.231) | copy-start | bytes 294916
  258.2 5.4 %collective-permute-start.49 = (bf16[4,96,128]{2,1,0:T(8,128)(2,1)}, bf16[4,96,128]{2,1,0:T(8,128)(2,1)S(1)}, u32[]{:S(2)}, u32[]{:S(2)}) collective-permute-start(bf16[4,96,128]{2,1,0:T(8,128)(2,1)} %get-tuple-element.232), channel_id=1, source_target_pairs={{0,4},{4,0},{8,12},{12,8},{16,20},{20,16},{24,28},{28,24},{1,5},{5... | collective-permute-start | bytes 294920 | tf_op jit(solution)/shard_map/ppermute | solution.py:20
  258.2 19.7 %collective-permute-start.50 = (s32[2,16384]{1,0:T(2,128)S(1)}, s32[2,16384]{1,0:T(2,128)S(1)}, u32[]{:S(2)}, u32[]{:S(2)}) collective-permute-start(s32[2,16384]{1,0:T(2,128)S(1)} %pad_add_fusion.2), channel_id=1, source_target_pairs={{0,8},{4,12},{8,0},{12,4},{16,24},{20,28},{24,16},{28,20},{1,9},{5... | collective-permute-start | bytes 393224 | tf_op jit(solution)/shard_map/ppermute | solution.py:20
  258.8 25.8 %collective-permute-start.48 = (bf16[24,3840]{1,0:T(8,128)(2,1)S(1)}, bf16[24,3840]{1,0:T(8,128)(2,1)S(1)}, u32[]{:S(2)}, u32[]{:S(2)}) collective-permute-start(bf16[24,3840]{1,0:T(8,128)(2,1)S(1)} %get-tuple-element.227), channel_id=1, source_target_pairs={{0,3},{1,2},{2,1},{3,0},{4,7},{5,6},{6,5},{7,4},{8,11},{9,10},{10,... | collective-permute-start | bytes 552968 | tf_op jit(solution)/shard_map/ppermute | solution.py:24
  260.1 9.2 %collective-permute-start.45 = (bf16[24,2304]{1,0:T(8,128)(2,1)S(1)}, bf16[24,2304]{1,0:T(8,128)(2,1)S(1)}, u32[]{:S(2)}, u32[]{:S(2)}) collective-permute-start(bf16[24,2304]{1,0:T(8,128)(2,1)S(1)} %get-tuple-element.278), channel_id=1, source_target_pairs={{0,1},{1,0},{2,3},{3,2},{4,5},{5,4},{6,7},{7,6},{8,9},{9,8},{10,11... | collective-permute-start | bytes 331784 | tf_op jit(solution)/shard_map/ppermute | solution.py:24
  260.2 16.9 %collective-permute-start.46 = (bf16[24,2304]{1,0:T(8,128)(2,1)S(1)}, bf16[24,2304]{1,0:T(8,128)(2,1)S(1)}, u32[]{:S(2)}, u32[]{:S(2)}) collective-permute-start(bf16[24,2304]{1,0:T(8,128)(2,1)S(1)} %get-tuple-element.279), channel_id=1, source_target_pairs={{0,2},{1,3},{2,0},{3,1},{4,6},{5,7},{6,4},{7,5},{8,10},{9,11},{10,... | collective-permute-start | bytes 331784 | tf_op jit(solution)/shard_map/ppermute | solution.py:24
  263.6 13.6 %collective-permute-start.47 = (bf16[24,2304]{1,0:T(8,128)(2,1)S(1)}, bf16[24,2304]{1,0:T(8,128)(2,1)S(1)}, u32[]{:S(2)}, u32[]{:S(2)}) collective-permute-start(bf16[24,2304]{1,0:T(8,128)(2,1)S(1)} %get-tuple-element.280), channel_id=1, source_target_pairs={{0,3},{1,2},{2,1},{3,0},{4,7},{5,6},{6,5},{7,4},{8,11},{9,10},{10,... | collective-permute-start | bytes 331784 | tf_op jit(solution)/shard_map/ppermute | solution.py:24
  277.9 4.0 %collective-permute-start.51 = (bf16[96,128]{1,0:T(8,128)(2,1)S(1)}, bf16[96,128]{1,0:T(8,128)(2,1)S(1)}, u32[]{:S(2)}, u32[]{:S(2)}) collective-permute-start(bf16[96,128]{1,0:T(8,128)(2,1)S(1)} %get-tuple-element.235), channel_id=1, source_target_pairs={{0,8},{4,12},{8,0},{12,4},{16,24},{20,28},{24,16},{28,20},{1,9},{5... | collective-permute-start | bytes 73736 | tf_op jit(solution)/shard_map/ppermute | solution.py:20
  279.4 3.8 %collective-permute-start.52 = (bf16[96,128]{1,0:T(8,128)(2,1)S(1)}, bf16[96,128]{1,0:T(8,128)(2,1)S(1)}, u32[]{:S(2)}, u32[]{:S(2)}) collective-permute-start(bf16[96,128]{1,0:T(8,128)(2,1)S(1)} %get-tuple-element.236), channel_id=1, source_target_pairs={{0,16},{4,20},{8,24},{12,28},{16,0},{20,4},{24,8},{28,12},{1,17},{... | collective-permute-start | bytes 73736 | tf_op jit(solution)/shard_map/ppermute | solution.py:20
  279.8 4.7 %collective-permute-start.53 = (bf16[96,128]{1,0:T(8,128)(2,1)S(1)}, bf16[96,128]{1,0:T(8,128)(2,1)S(1)}, u32[]{:S(2)}, u32[]{:S(2)}) collective-permute-start(bf16[96,128]{1,0:T(8,128)(2,1)S(1)} %get-tuple-element.237), channel_id=1, source_target_pairs={{0,24},{4,28},{8,16},{12,20},{16,8},{20,12},{24,0},{28,4},{1,25},{... | collective-permute-start | bytes 73736 | tf_op jit(solution)/shard_map/ppermute | solution.py:20
  281.6 4.4 %collective-permute-start.54 = (s32[4,16384]{1,0:T(4,128)S(1)}, s32[4,16384]{1,0:T(4,128)S(1)}, u32[]{:S(2)}, u32[]{:S(2)}) collective-permute-start(s32[4,16384]{1,0:T(4,128)S(1)} %pad_add_fusion.1), channel_id=1, source_target_pairs={{0,4},{4,0},{8,12},{12,8},{16,20},{20,16},{24,28},{28,24},{1,5},{5... | collective-permute-start | bytes 786440 | tf_op jit(solution)/shard_map/ppermute | solution.py:20
  286.2 5.6 %collective-permute-start.55 = (bf16[24,128]{1,0:T(8,128)(2,1)S(1)}, bf16[24,128]{1,0:T(8,128)(2,1)S(1)}, u32[]{:S(2)}, u32[]{:S(2)}) collective-permute-start(bf16[24,128]{1,0:T(8,128)(2,1)S(1)} %get-tuple-element.289), channel_id=1, source_target_pairs={{0,1},{1,0},{2,3},{3,2},{4,5},{5,4},{6,7},{7,6},{8,9},{9,8},{10,11... | collective-permute-start | bytes 18440 | tf_op jit(solution)/shard_map/ppermute | solution.py:24
  288.5 4.5 %collective-permute-start.56 = (bf16[24,128]{1,0:T(8,128)(2,1)S(1)}, bf16[24,128]{1,0:T(8,128)(2,1)S(1)}, u32[]{:S(2)}, u32[]{:S(2)}) collective-permute-start(bf16[24,128]{1,0:T(8,128)(2,1)S(1)} %get-tuple-element.290), channel_id=1, source_target_pairs={{0,2},{1,3},{2,0},{3,1},{4,6},{5,7},{6,4},{7,5},{8,10},{9,11},{10,... | collective-permute-start | bytes 18440 | tf_op jit(solution)/shard_map/ppermute | solution.py:24
  288.5 5.4 %collective-permute-start.57 = (bf16[24,128]{1,0:T(8,128)(2,1)S(1)}, bf16[24,128]{1,0:T(8,128)(2,1)S(1)}, u32[]{:S(2)}, u32[]{:S(2)}) collective-permute-start(bf16[24,128]{1,0:T(8,128)(2,1)S(1)} %get-tuple-element.291), channel_id=1, source_target_pairs={{0,3},{1,2},{2,1},{3,0},{4,7},{5,6},{6,5},{7,4},{8,11},{9,10},{10,... | collective-permute-start | bytes 18440 | tf_op jit(solution)/shard_map/ppermute | solution.py:24
  (9 other events, 23.0 us)

commit v2 on v1

--- a/solution.py
+++ b/solution.py
@@ -775,28 +775,29 @@
         early_parts, down_inner = values[:4], values[4 : 3 + inner]
         up_pieces = values[3 + inner :]
         counts = double_tables(counts, other, NEAR_Y)
+        other = swap(counts, NEAR_X)
+        dqkv, other = together([dqkv, other])
+        counts = double_tables(counts, other, NEAR_X)
         down_sum = sum_parts(pieces[:1] + down_inner)
         early_received = scatter_sides(early_parts)
         up_inner = [swap_inner(up_pieces[k], k, inner) for k in range(1, inner - 1)]
     tokens_grad, *late = finish(grad_y, tokens, dqkv, vec, ffn_sums, me, *first)
     if near:
-        *values, tokens_grad, late[1], piece, counts = together(
-            [*early_received, *up_inner, tokens_grad, late[1], up_pieces[-1], counts]
+        *up_inner, tokens_grad, late[1], piece, counts = together(
+            [*up_inner, tokens_grad, late[1], up_pieces[-1], counts]
         )
-        early_received, up_inner = values[:3], values[3:]
         late_parts = scatter_core(*late)
-        other = swap(counts, NEAR_X)
+        other = swap(counts, CORE)
         *late_parts, other = together([*late_parts, other])
-        counts = double_tables(counts, other, NEAR_X)
-        other = swap(counts, CORE)
+        counts = double_tables(counts, other, CORE)
+        late_received = scatter_sides(late_parts)
+        *values, piece = together([*early_received, *late_received, piece])
+        early_received, late_received = values[:3], values[3:]
+        early_mine = add(early_parts[0], *early_received)
         up_inner.append(swap_inner(piece, inner - 1, inner))
-        early_mine = add(early_parts[0], *early_received)
         early_sum = sum_parts(scatter_inner(early_mine, inner))
-        late_received = scatter_sides(late_parts)
         up_sum = sum_parts(up_pieces[:1] + up_inner)
-        late_mine, other = together([add(late_parts[0], *late_received), other])
-        late_sum = sum_parts(scatter_inner(late_mine, inner))
-        counts = double_tables(counts, other, CORE)
+        late_sum = sum_parts(scatter_inner(add(late_parts[0], *late_received), inner))
     else:
         up_sum, down_sum, early_sum, late_sum = [
             scatter_whole(*v) for v in (up_parts, down_parts, early, late)

time: 299 us -> 290 us (0.970)
  waiting for transfers between devices: 68.9 us -> 56.6 us
    ppermute x34, waiting for transfers between devices: 29.3 us -> 22.7 us  [swap(): return lax.ppermute(value, 'dp', [(i, i ^ bit) for i in range(BLOCKS)])]
    ppermute x24, waiting for transfers between devices: 39.6 us -> 33.9 us  [swap_inner(): return lax.ppermute(value, 'fsdp', [(i, i ^ bit) for i in range(size)])]
    unnamed x31 -> x29, local copies, waits for them, and re-layouts: 8.58 us -> 8.57 us
  transfers between devices with their start and end apart: 58 -> 58, of which waited for: 21 -> 19; matrix products, arithmetic and copies ran while one was open for 5% -> 5% of each run, Pallas kernels for 44% -> 46%
where the time goes in v2:
time: 290 us; the launch traced here: 287 us
  Pallas kernels  131 us (45%)
  starting transfers between devices  70.1 us (24%)
  waiting for transfers between devices  56.6 us (20%)
  other arithmetic  15.6 us (5%)
  local copies, waits for them, and re-layouts  11.8 us (4%)
    ppermute x24, starting transfers between devices, swap_inner(): return lax.ppermute(value, 'fsdp', [(i, i ^ bit) for i in range(size)])  39.8 us
    pallas_call x1, Pallas kernels, feed_return(): pl.pallas_call(functools.partial(return_kernel, plan, len(pieces), plan_d...  37.2 us
    ppermute x24, waiting for transfers between devices, swap_inner(): return lax.ppermute(value, 'fsdp', [(i, i ^ bit) for i in range(size)])  33.9 us
    ppermute x34, starting transfers between devices, swap(): return lax.ppermute(value, 'dp', [(i, i ^ bit) for i in range(BLOCKS)])  30.4 us
    pallas_call x1, Pallas kernels, backward(): pl.pallas_call(functools.partial(backward_kernel, plan, len(pieces), grou...  27.6 us
    pallas_call x1, Pallas kernels, feed_forward(): pl.pallas_call(functools.partial(forward_kernel, plan, len(pieces)), grid...  27 us
    pallas_call x1, Pallas kernels, attend(): pl.pallas_call(functools.partial(attend_kernel, plan, len(pieces)), grid=...  24.7 us
    ppermute x34, waiting for transfers between devices, swap(): return lax.ppermute(value, 'dp', [(i, i ^ bit) for i in range(BLOCKS)])  22.7 us
  transfers between devices with their start and end apart: 58, of which 19 were waited for; matrix products, arithmetic and copies ran while one was open for 5% of the time, Pallas kernels for 46%

profile of v2, /device:TPU:0, one launch (start us, length us, event | category | flops | bytes accessed | tf_op | source)
XLA Modules:
  0.0 286.8 jit_solution(16463372366067097252)
XLA Ops:
  2.4 3.1 %collective-permute-start.2 = (bf16[24,2432]{1,0:T(8,128)(2,1)S(1)}, bf16[24,2432]{1,0:T(8,128)(2,1)S(1)}, u32[]{:S(2)}, u32[]{:S(2)}) collective-permute-start(bf16[24,2432]{1,0:T(8,128)(2,1)S(1)} %fusion.13), channel_id=1, source_target_pairs={{0,1},{1,0},{2,3},{3,2},{4,5},{5,4},{6,7},{7,6},{8,9},{9,8},{10,11... | collective-permute-start | bytes 350216 | tf_op jit(solution)/shard_map/ppermute | solution.py:24
  5.5 2.6 collective-permute-start.1
  8.1 0.9 pad_maximum_fusion.6
  9.0 3.0 %shard_map.203 = s32[8,64,256]{2,1,0:T(8,128)} custom-call(s32[8,1024]{1,0:T(8,128)} %bitcast.87), custom_call_target="tpu_custom_call" | custom-call | flops 3000000000 | bytes 1000000 | tf_op jit(solution)/shard_map/pallas_call | solution.py:187
  12.0 1.3 copy.34
  13.4 3.9 %collective-permute-done.1 = bf16[24,2432]{1,0:T(8,128)(2,1)S(1)} collective-permute-done((bf16[24,2432]{1,0:T(8,128)(2,1)S(1)}, bf16[24,2432]{1,0:T(8,128)(2,1)S(1)}, u32[]{:S(2)}, u32[]{:S(2)}) %collective-permute-start.1) | collective-permute-done | bytes 116768 | tf_op jit(solution)/shard_map/ppermute | solution.py:24
  17.5 2.5 collective-permute-start.5
  21.0 2.5 collective-permute-start.8
  24.3 4.8 %collective-permute-done.8 = bf16[24,3840]{1,0:T(8,128)(2,1)S(1)} collective-permute-done((bf16[24,3840]{1,0:T(8,128)(2,1)S(1)}, bf16[24,3840]{1,0:T(8,128)(2,1)S(1)}, u32[]{:S(2)}, u32[]{:S(2)}) %collective-permute-start.8) | collective-permute-done | bytes 184352 | tf_op jit(solution)/shard_map/ppermute | solution.py:24
  29.1 6.5 %collective-permute-start.6 = (bf16[24,3840]{1,0:T(8,128)(2,1)S(1)}, bf16[24,3840]{1,0:T(8,128)(2,1)S(1)}, u32[]{:S(2)}, u32[]{:S(2)}) collective-permute-start(bf16[24,3840]{1,0:T(8,128)(2,1)S(1)} %pad_maximum_fusion.6), channel_id=1, source_target_pairs={{0,1},{1,0},{2,3},{3,2},{4,5},{5,4},{6,7},{7,6},{8,9},{9,8},{10,11... | collective-permute-start | bytes 552968 | tf_op jit(solution)/shard_map/ppermute | solution.py:24
  35.7 2.3 collective-permute-done.7
  38.0 3.4 %collective-permute-done.6 = bf16[24,3840]{1,0:T(8,128)(2,1)S(1)} collective-permute-done((bf16[24,3840]{1,0:T(8,128)(2,1)S(1)}, bf16[24,3840]{1,0:T(8,128)(2,1)S(1)}, u32[]{:S(2)}, u32[]{:S(2)}) %collective-permute-start.6) | collective-permute-done | bytes 184352 | tf_op jit(solution)/shard_map/ppermute | solution.py:24
  43.0 3.0 %collective-permute-done.9 = s32[4,16384]{1,0:T(4,128)S(1)} collective-permute-done((s32[4,16384]{1,0:T(4,128)S(1)}, s32[4,16384]{1,0:T(4,128)S(1)}, u32[]{:S(2)}, u32[]{:S(2)}) %collective-permute-start.9) | collective-permute-done | bytes 262176 | tf_op jit(solution)/shard_map/ppermute | solution.py:20
  46.1 1.3 copy-done.4
  47.3 2.4 collective-permute-start.13
  50.8 1.3 collective-permute-start.15
  52.9 1.0 copy.33.seg_ref
  54.0 24.7 %shard_map.204 = (bf16[2,512,2304]{2,1,0:T(8,128)(2,1)}, bf16[2,12,512,512]{3,2,1,0:T(8,128)(2,1)}, f32[2,12,1,512]{3,2,1,0:T(1,128)}, bf16[2,768,512]{2,1,0:T(8...) custom-call(s32[1]{0:T(128)} %bitcast.me_ref, ...), custom_call_target="tpu_custom_call" | custom-call | flops 1000000000 | bytes 1000000 | tf_op jit(solution)/shard_map/pallas_call | solution.py:292
  78.7 3.9 %collective-permute-done.12 = bf16[96,3840]{1,0:T(8,128)(2,1)S(1)} collective-permute-done((bf16[96,3840]{1,0:T(8,128)(2,1)S(1)}, bf16[96,3840]{1,0:T(8,128)(2,1)S(1)}, u32[]{:S(2)}, u32[]{:S(2)}) %collective-permute-start.12) | collective-permute-done | bytes 737312 | tf_op jit(solution)/shard_map/ppermute | solution.py:20
  82.7 1.5 collective-permute-start.16
  85.2 5.2 %collective-permute-done.16 = bf16[96,768]{1,0:T(8,128)(2,1)S(1)} collective-permute-done((bf16[96,768]{1,0:T(8,128)(2,1)}, bf16[96,768]{1,0:T(8,128)(2,1)S(1)}, u32[]{:S(2)}, u32[]{:S(2)}) %collective-permute-start.16) | collective-permute-done | bytes 147488 | tf_op jit(solution)/shard_map/ppermute | solution.py:24
  90.5 1.1 broadcast_select_fusion.30
  91.7 1.6 copy-done.1
  93.2 1.1 collective-permute-start.20
  94.3 1.9 collective-permute-start.19
  96.8 1.6 collective-permute-start.21
  98.3 27.0 %shard_map.205 = (f32[1024,768]{1,0:T(8,128)}, bf16[768,1024]{1,0:T(8,128)(2,1)}, bf16[4,384,768]{2,1,0:T(8,128)(2,1)}, bf16[4,384,768]{2,1,0:T(8,128)(2,1)}, bf...) custom-call(s32[1]{0:T(128)} %bitcast.me_ref, bf16[1024,768]{1,0:T(8,128)(2,1)} %bitcast.60, ...), custom_call_target="tpu_custom_call" | custom-call | flops 1000000000 | bytes 1000000 | tf_op jit(solution)/shard_map/pallas_call | solution.py:379
  125.8 2.1 copy-done.13
  128.1 5.7 %collective-permute-done.22 = bf16[4,384,768]{2,1,0:T(8,128)(2,1)S(1)} collective-permute-done((bf16[4,384,768]{2,1,0:T(8,128)(2,1)S(1)}, bf16[4,384,768]{2,1,0:T(8,128)(2,1)S(1)}, u32[]{:S(2)}, u32[]{:S(2)}) %collective-permute-start.22) | collective-permute-done | bytes 2359328 | tf_op jit(solution)/shard_map/ppermute | solution.py:20
  133.7 1.6 fusion.7
  135.8 1.4 collective-permute-start.25
  137.3 1.6 collective-permute-start.26
  139.1 1.4 copy-done.6
  140.5 37.2 %shard_map.206 = (f32[1024,768]{1,0:T(8,128)}, bf16[1024,768]{1,0:T(8,128)(2,1)}, bf16[4,96,3840]{2,1,0:T(8,128)(2,1)}, bf16[4,96,3840]{2,1,0:T(8,128)(2,1)}, f32[8,768]{1,0:T(8,128)}) custom-call(s32[1]{0:T(128)} %bitcast.me_ref, f32[1024,768]{1,0:T(8,128)} %get-tuple-element.163.y_ref, bf16[1024,768]{1,0:T(8,128)(2,1)} %bitcast.64, ...), custom_call_target="tpu_custom_call" | custom-call | flops 1000000000 | bytes 1000000 | tf_op jit(solution)/shard_map/pallas_call | solution.py:487
  177.9 1.6 collective-permute-start.31
  179.5 1.9 collective-permute-start.30
  181.4 0.9 collective-permute-start.29
  182.4 1.7 add_convert_fusion.5
  184.8 3.3 %collective-permute-done.30 = s32[1,16384]{1,0:T(1,128)S(1)} collective-permute-done((s32[1,16384]{1,0:T(1,128)S(1)}, s32[1,16384]{1,0:T(1,128)S(1)}, u32[]{:S(2)}, u32[]{:S(2)}) %collective-permute-start.30) | collective-permute-done | bytes 65568 | tf_op jit(solution)/shard_map/ppermute | solution.py:24
  188.9 2.5 collective-permute-start.36
  191.4 1.8 collective-permute-start.32
  193.8 1.1 collective-permute-start.34
  195.0 27.6 %shard_map.207 = (bf16[2,512,2304]{2,1,0:T(8,128)(2,1)}, bf16[4,96,2304]{2,1,0:T(8,128)(2,1)}, bf16[4,96,2304]{2,1,0:T(8,128)(2,1)}) custom-call(s32[1]{0:T(128)} %bitcast.me_ref, f32[2,512,768]{2,1,0:T(8,128)} %bitcast.61, bf16[2,512,2304]{2,1,0:T(8,128)(2,1)} %get-tuple-element.188.q_ref.k_ref.v_ref, ...), custom_call_target="tpu_custom_call" | custom-call | flops 1000000000 | bytes 1000000 | tf_op jit(solution)/shard_map/pallas_call | solution.py:637
  222.7 3.9 %collective-permute-done.33 = bf16[96,3840]{1,0:T(8,128)(2,1)S(1)} collective-permute-done((bf16[96,3840]{1,0:T(8,128)(2,1)S(1)}, bf16[96,3840]{1,0:T(8,128)(2,1)S(1)}, u32[]{:S(2)}, u32[]{:S(2)}) %collective-permute-start.33) | collective-permute-done | bytes 737312 | tf_op jit(solution)/shard_map/ppermute | solution.py:20
  227.2 1.0 collective-permute-start.38
  228.7 3.5 %collective-permute-done.37 = bf16[4,96,2304]{2,1,0:T(8,128)(2,1)S(1)} collective-permute-done((bf16[4,96,2304]{2,1,0:T(8,128)(2,1)}, bf16[4,96,2304]{2,1,0:T(8,128)(2,1)S(1)}, u32[]{:S(2)}, u32[]{:S(2)}) %collective-permute-start.37) | collective-permute-done | bytes 1769504 | tf_op jit(solution)/shard_map/ppermute | solution.py:20
  232.6 1.8 collective-permute-done.38
  234.6 1.6 collective-permute-start.42
  236.9 1.0 collective-permute-start.41
  238.3 1.4 collective-permute-start.44
  239.8 1.5 collective-permute-start.45
  241.6 11.6 %shard_map.208 = (bf16[2,512,768]{2,1,0:T(8,128)(2,1)}, bf16[4,96,128]{2,1,0:T(8,128)(2,1)}, bf16[4,96,128]{2,1,0:T(8,128)(2,1)}) custom-call(s32[1]{0:T(128)} %bitcast.me_ref, f32[2,512,768]{2,1,0:T(8,128)} %bitcast.62, bf16[2,512,768]{2,1,0:T(8,128)(2,1)} %x_ref.3, bf16[2,512,2304]{2,1,0:T(8,128)(2,1)} %get-tuple-element.216.dqkv_ref, ...), custom_call_target="tpu_custom_call" | custom-call | flops 1000000000 | bytes 1000000 | tf_op jit(solution)/shard_map/pallas_call | solution.py:693
  255.7 2.5 collective-permute-start.48
  258.3 1.5 collective-permute-start.50
  260.7 1.5 collective-permute-done.49
  262.2 0.9 collective-permute-done.50
  263.2 1.0 collective-permute-start.55
  264.2 1.8 collective-permute-start.56
  266.0 1.6 collective-permute-start.57
  267.6 2.2 collective-permute-start.54
  270.2 2.2 collective-permute-start.52
  272.4 2.2 collective-permute-start.53
  275.3 3.4 %collective-permute-done.51 = bf16[24,2304]{1,0:T(8,128)(2,1)S(1)} collective-permute-done((bf16[24,2304]{1,0:T(8,128)(2,1)S(1)}, bf16[24,2304]{1,0:T(8,128)(2,1)S(1)}, u32[]{:S(2)}, u32[]{:S(2)}) %collective-permute-start.51) | collective-permute-done | bytes 110624 | tf_op jit(solution)/shard_map/ppermute | solution.py:24
  278.7 5.6 %collective-permute-done.52 = bf16[24,2304]{1,0:T(8,128)(2,1)S(1)} collective-permute-done((bf16[24,2304]{1,0:T(8,128)(2,1)S(1)}, bf16[24,2304]{1,0:T(8,128)(2,1)S(1)}, u32[]{:S(2)}, u32[]{:S(2)}) %collective-permute-start.52) | collective-permute-done | bytes 110624 | tf_op jit(solution)/shard_map/ppermute | solution.py:24
  (133 shorter events, 22.5 us)
Async XLA Ops:
  2.4 11.0 %collective-permute-start.2 = (bf16[24,2432]{1,0:T(8,128)(2,1)S(1)}, bf16[24,2432]{1,0:T(8,128)(2,1)S(1)}, u32[]{:S(2)}, u32[]{:S(2)}) collective-permute-start(bf16[24,2432]{1,0:T(8,128)(2,1)S(1)} %fusion.13), channel_id=1, source_target_pairs={{0,1},{1,0},{2,3},{3,2},{4,5},{5,4},{6,7},{7,6},{8,9},{9,8},{10,11... | collective-permute-start | bytes 350216 | tf_op jit(solution)/shard_map/ppermute | solution.py:24
  5.5 11.9 %collective-permute-start.1 = (bf16[24,2432]{1,0:T(8,128)(2,1)S(1)}, bf16[24,2432]{1,0:T(8,128)(2,1)S(1)}, u32[]{:S(2)}, u32[]{:S(2)}) collective-permute-start(bf16[24,2432]{1,0:T(8,128)(2,1)S(1)} %fusion.13), channel_id=1, source_target_pairs={{0,2},{1,3},{2,0},{3,1},{4,6},{5,7},{6,4},{7,5},{8,10},{9,11},{10,... | collective-permute-start | bytes 350216 | tf_op jit(solution)/shard_map/ppermute | solution.py:24
  8.0 9.3 %collective-permute-start = (bf16[24,2432]{1,0:T(8,128)(2,1)S(1)}, bf16[24,2432]{1,0:T(8,128)(2,1)S(1)}, u32[]{:S(2)}, u32[]{:S(2)}) collective-permute-start(bf16[24,2432]{1,0:T(8,128)(2,1)S(1)} %fusion.13), channel_id=1, source_target_pairs={{0,3},{1,2},{2,1},{3,0},{4,7},{5,6},{6,5},{7,4},{8,11},{9,10},{10,... | collective-permute-start | bytes 350216 | tf_op jit(solution)/shard_map/ppermute | solution.py:24
  9.0 8.3 %copy-start.9 = (bf16[24,2304]{1,0:T(8,128)(2,1)S(1)}, bf16[24,2304]{1,0:T(8,128)(2,1)}, u32[]{:S(2)}) copy-start(bf16[24,2304]{1,0:T(8,128)(2,1)} %param.16) | copy-start | bytes 331780
  17.5 24.0 %collective-permute-start.5 = (bf16[96,2432]{1,0:T(8,128)(2,1)S(1)}, bf16[96,2432]{1,0:T(8,128)(2,1)S(1)}, u32[]{:S(2)}, u32[]{:S(2)}) collective-permute-start(bf16[96,2432]{1,0:T(8,128)(2,1)S(1)} %pad_maximum_fusion.5), channel_id=1, source_target_pairs={{0,24},{4,28},{8,16},{12,20},{16,8},{20,12},{24,0},{28,4},{1,25},{... | collective-permute-start | bytes 1400840 | tf_op jit(solution)/shard_map/ppermute | solution.py:20
  20.0 21.5 %collective-permute-start.4 = (bf16[96,2432]{1,0:T(8,128)(2,1)S(1)}, bf16[96,2432]{1,0:T(8,128)(2,1)S(1)}, u32[]{:S(2)}, u32[]{:S(2)}) collective-permute-start(bf16[96,2432]{1,0:T(8,128)(2,1)S(1)} %pad_maximum_fusion.5), channel_id=1, source_target_pairs={{0,16},{4,20},{8,24},{12,28},{16,0},{20,4},{24,8},{28,12},{1,17},{... | collective-permute-start | bytes 1400840 | tf_op jit(solution)/shard_map/ppermute | solution.py:20
  20.5 21.0 %collective-permute-start.3 = (bf16[96,2432]{1,0:T(8,128)(2,1)S(1)}, bf16[96,2432]{1,0:T(8,128)(2,1)S(1)}, u32[]{:S(2)}, u32[]{:S(2)}) collective-permute-start(bf16[96,2432]{1,0:T(8,128)(2,1)S(1)} %pad_maximum_fusion.5), channel_id=1, source_target_pairs={{0,8},{4,12},{8,0},{12,4},{16,24},{20,28},{24,16},{28,20},{1,9},{5... | collective-permute-start | bytes 1400840 | tf_op jit(solution)/shard_map/ppermute | solution.py:20
  21.0 8.1 %collective-permute-start.8 = (bf16[24,3840]{1,0:T(8,128)(2,1)S(1)}, bf16[24,3840]{1,0:T(8,128)(2,1)S(1)}, u32[]{:S(2)}, u32[]{:S(2)}) collective-permute-start(bf16[24,3840]{1,0:T(8,128)(2,1)S(1)} %pad_maximum_fusion.6), channel_id=1, source_target_pairs={{0,3},{1,2},{2,1},{3,0},{4,7},{5,6},{6,5},{7,4},{8,11},{9,10},{10,... | collective-permute-start | bytes 552968 | tf_op jit(solution)/shard_map/ppermute | solution.py:24
  23.5 14.5 %collective-permute-start.7 = (bf16[24,3840]{1,0:T(8,128)(2,1)S(1)}, bf16[24,3840]{1,0:T(8,128)(2,1)S(1)}, u32[]{:S(2)}, u32[]{:S(2)}) collective-permute-start(bf16[24,3840]{1,0:T(8,128)(2,1)S(1)} %pad_maximum_fusion.6), channel_id=1, source_target_pairs={{0,2},{1,3},{2,0},{3,1},{4,6},{5,7},{6,4},{7,5},{8,10},{9,11},{10,... | collective-permute-start | bytes 552968 | tf_op jit(solution)/shard_map/ppermute | solution.py:24
  29.1 12.3 %collective-permute-start.6 = (bf16[24,3840]{1,0:T(8,128)(2,1)S(1)}, bf16[24,3840]{1,0:T(8,128)(2,1)S(1)}, u32[]{:S(2)}, u32[]{:S(2)}) collective-permute-start(bf16[24,3840]{1,0:T(8,128)(2,1)S(1)} %pad_maximum_fusion.6), channel_id=1, source_target_pairs={{0,1},{1,0},{2,3},{3,2},{4,5},{5,4},{6,7},{7,6},{8,9},{9,8},{10,11... | collective-permute-start | bytes 552968 | tf_op jit(solution)/shard_map/ppermute | solution.py:24
  41.8 4.3 %collective-permute-start.10 = (bf16[4,96,2432]{2,1,0:T(8,128)(2,1)S(1)}, bf16[4,96,2432]{2,1,0:T(8,128)(2,1)S(1)}, u32[]{:S(2)}, u32[]{:S(2)}) collective-permute-start(bf16[4,96,2432]{2,1,0:T(8,128)(2,1)S(1)} %pad_maximum_fusion.2.rest_0_), channel_id=1, source_target_pairs={{0,4},{4,0},{8,12},{12,8},{16,20},{20,16},{24,28},{28,24},{1,5},{5... | collective-permute-start | bytes 5603336 | tf_op jit(solution)/shard_map/ppermute | solution.py:20
  41.9 11.0 %copy-start.12 = (s32[2,512]{1,0:T(2,128)S(1)}, s32[2,512]{1,0:T(2,128)}, u32[]{:S(2)}) copy-start(s32[2,512]{1,0:T(2,128)} %param.13) | copy-start | bytes 12292
  42.0 4.1 %collective-permute-start.9 = (s32[4,16384]{1,0:T(4,128)S(1)}, s32[4,16384]{1,0:T(4,128)S(1)}, u32[]{:S(2)}, u32[]{:S(2)}) collective-permute-start(s32[4,16384]{1,0:T(4,128)S(1)} %slice_select_fusion), channel_id=1, source_target_pairs={{0,4},{4,0},{8,12},{12,8},{16,20},{20,16},{24,28},{28,24},{1,5},{5... | collective-permute-start | bytes 786440 | tf_op jit(solution)/shard_map/ppermute | solution.py:20
  47.3 31.4 %collective-permute-start.13 = (bf16[96,3840]{1,0:T(8,128)(2,1)S(1)}, bf16[96,3840]{1,0:T(8,128)(2,1)S(1)}, u32[]{:S(2)}, u32[]{:S(2)}) collective-permute-start(bf16[96,3840]{1,0:T(8,128)(2,1)S(1)} %pad_maximum_fusion.3), channel_id=1, source_target_pairs={{0,24},{4,28},{8,16},{12,20},{16,8},{20,12},{24,0},{28,4},{1,25},{... | collective-permute-start | bytes 2211848 | tf_op jit(solution)/shard_map/ppermute | solution.py:20
  49.8 32.8 %collective-permute-start.12 = (bf16[96,3840]{1,0:T(8,128)(2,1)S(1)}, bf16[96,3840]{1,0:T(8,128)(2,1)S(1)}, u32[]{:S(2)}, u32[]{:S(2)}) collective-permute-start(bf16[96,3840]{1,0:T(8,128)(2,1)S(1)} %pad_maximum_fusion.3), channel_id=1, source_target_pairs={{0,16},{4,20},{8,24},{12,28},{16,0},{20,4},{24,8},{28,12},{1,17},{... | collective-permute-start | bytes 2211848 | tf_op jit(solution)/shard_map/ppermute | solution.py:20
  50.3 32.4 %collective-permute-start.11 = (bf16[96,3840]{1,0:T(8,128)(2,1)S(1)}, bf16[96,3840]{1,0:T(8,128)(2,1)S(1)}, u32[]{:S(2)}, u32[]{:S(2)}) collective-permute-start(bf16[96,3840]{1,0:T(8,128)(2,1)S(1)} %pad_maximum_fusion.3), channel_id=1, source_target_pairs={{0,8},{4,12},{8,0},{12,4},{16,24},{20,28},{24,16},{28,20},{1,9},{5... | collective-permute-start | bytes 2211848 | tf_op jit(solution)/shard_map/ppermute | solution.py:20
  50.8 27.9 %collective-permute-start.15 = (bf16[96,768]{1,0:T(8,128)(2,1)}, bf16[96,768]{1,0:T(8,128)(2,1)}, u32[]{:S(2)}, u32[]{:S(2)}) collective-permute-start(bf16[96,768]{1,0:T(8,128)(2,1)} %param.19), channel_id=1, source_target_pairs={{0,2},{1,3},{2,0},{3,1},{4,6},{5,7},{6,4},{7,5},{8,10},{9,11},{10,... | collective-permute-start | bytes 442376 | tf_op jit(solution)/shard_map/ppermute | solution.py:24
  52.2 26.5 %collective-permute-start.14 = (bf16[96,768]{1,0:T(8,128)(2,1)}, bf16[96,768]{1,0:T(8,128)(2,1)}, u32[]{:S(2)}, u32[]{:S(2)}) collective-permute-start(bf16[96,768]{1,0:T(8,128)(2,1)} %param.19), channel_id=1, source_target_pairs={{0,1},{1,0},{2,3},{3,2},{4,5},{5,4},{6,7},{7,6},{8,9},{9,8},{10,11... | collective-permute-start | bytes 442376 | tf_op jit(solution)/shard_map/ppermute | solution.py:24
  82.7 7.8 %collective-permute-start.16 = (bf16[96,768]{1,0:T(8,128)(2,1)}, bf16[96,768]{1,0:T(8,128)(2,1)S(1)}, u32[]{:S(2)}, u32[]{:S(2)}) collective-permute-start(bf16[96,768]{1,0:T(8,128)(2,1)} %param.19), channel_id=1, source_target_pairs={{0,3},{1,2},{2,1},{3,0},{4,7},{5,6},{6,5},{7,4},{8,11},{9,10},{10,... | collective-permute-start | bytes 442376 | tf_op jit(solution)/shard_map/ppermute | solution.py:24
  84.6 7.0 %copy-start = (bf16[4,96,3840]{2,1,0:T(8,128)(2,1)}, bf16[4,96,3840]{2,1,0:T(8,128)(2,1)S(1)}, u32[]{:S(2)}) copy-start(bf16[4,96,3840]{2,1,0:T(8,128)(2,1)S(1)} %pad_maximum_fusion.rest_0_) | copy-start | bytes 8847364
  84.6 7.0 %collective-permute-start.17 = (bf16[4,96,3840]{2,1,0:T(8,128)(2,1)S(1)}, bf16[4,96,3840]{2,1,0:T(8,128)(2,1)S(1)}, u32[]{:S(2)}, u32[]{:S(2)}) collective-permute-start(bf16[4,96,3840]{2,1,0:T(8,128)(2,1)S(1)} %pad_maximum_fusion.rest_0_), channel_id=1, source_target_pairs={{0,4},{4,0},{8,12},{12,8},{16,20},{20,16},{24,28},{28,24},{1,5},{5... | collective-permute-start | bytes 8847368 | tf_op jit(solution)/shard_map/ppermute | solution.py:20
  93.2 32.2 %collective-permute-start.20 = (bf16[384,768]{1,0:T(8,128)(2,1)S(1)}, bf16[384,768]{1,0:T(8,128)(2,1)S(1)}, u32[]{:S(2)}, u32[]{:S(2)}) collective-permute-start(bf16[384,768]{1,0:T(8,128)(2,1)S(1)} %pad_maximum_fusion.4), channel_id=1, source_target_pairs={{0,24},{4,28},{8,16},{12,20},{16,8},{20,12},{24,0},{28,4},{1,25},{... | collective-permute-start | bytes 1769480 | tf_op jit(solution)/shard_map/ppermute | solution.py:20
  94.3 31.1 %collective-permute-start.19 = (bf16[384,768]{1,0:T(8,128)(2,1)S(1)}, bf16[384,768]{1,0:T(8,128)(2,1)S(1)}, u32[]{:S(2)}, u32[]{:S(2)}) collective-permute-start(bf16[384,768]{1,0:T(8,128)(2,1)S(1)} %pad_maximum_fusion.4), channel_id=1, source_target_pairs={{0,16},{4,20},{8,24},{12,28},{16,0},{20,4},{24,8},{28,12},{1,17},{... | collective-permute-start | bytes 1769480 | tf_op jit(solution)/shard_map/ppermute | solution.py:20
  96.2 29.2 %collective-permute-start.18 = (bf16[384,768]{1,0:T(8,128)(2,1)S(1)}, bf16[384,768]{1,0:T(8,128)(2,1)S(1)}, u32[]{:S(2)}, u32[]{:S(2)}) collective-permute-start(bf16[384,768]{1,0:T(8,128)(2,1)S(1)} %pad_maximum_fusion.4), channel_id=1, source_target_pairs={{0,8},{4,12},{8,0},{12,4},{16,24},{20,28},{24,16},{28,20},{1,9},{5... | collective-permute-start | bytes 1769480 | tf_op jit(solution)/shard_map/ppermute | solution.py:20
  96.8 28.6 %collective-permute-start.21 = (s32[2,16384]{1,0:T(2,128)S(1)}, s32[2,16384]{1,0:T(2,128)S(1)}, u32[]{:S(2)}, u32[]{:S(2)}) collective-permute-start(s32[2,16384]{1,0:T(2,128)S(1)} %broadcast_select_fusion.37), channel_id=1, source_target_pairs={{0,8},{4,12},{8,0},{12,4},{16,24},{20,28},{24,16},{28,20},{1,9},{5... | collective-permute-start | bytes 393224 | tf_op jit(solution)/shard_map/ppermute | solution.py:20
  125.4 8.3 %copy-start.7 = (bf16[4,384,768]{2,1,0:T(8,128)(2,1)S(1)}, bf16[4,384,768]{2,1,0:T(8,128)(2,1)}, u32[]{:S(2)}) copy-start(bf16[4,384,768]{2,1,0:T(8,128)(2,1)} %get-tuple-element.161) | copy-start | bytes 7077892
  125.8 9.6 %copy-start.3 = (bf16[4,384,768]{2,1,0:T(8,128)(2,1)}, bf16[4,384,768]{2,1,0:T(8,128)(2,1)S(1)}, u32[]{:S(2)}) copy-start(bf16[4,384,768]{2,1,0:T(8,128)(2,1)S(1)} %pad_maximum_fusion.1.rest_2_) | copy-start | bytes 7077892
  125.8 13.3 %collective-permute-start.23 = (bf16[4,384,768]{2,1,0:T(8,128)(2,1)S(1)}, bf16[4,384,768]{2,1,0:T(8,128)(2,1)S(1)}, u32[]{:S(2)}, u32[]{:S(2)}) collective-permute-start(bf16[4,384,768]{2,1,0:T(8,128)(2,1)S(1)} %pad_maximum_fusion.1.rest_2_), channel_id=1, source_target_pairs={{0,4},{4,0},{8,12},{12,8},{16,20},{20,16},{24,28},{28,24},{1,5},{5... | collective-permute-start | bytes 7077896 | tf_op jit(solution)/shard_map/ppermute | solution.py:20
  127.9 5.8 %collective-permute-start.22 = (bf16[4,384,768]{2,1,0:T(8,128)(2,1)S(1)}, bf16[4,384,768]{2,1,0:T(8,128)(2,1)S(1)}, u32[]{:S(2)}, u32[]{:S(2)}) collective-permute-start(bf16[4,384,768]{2,1,0:T(8,128)(2,1)S(1)} %copy-done.13), channel_id=1, source_target_pairs={{0,4},{4,0},{8,12},{12,8},{16,20},{20,16},{24,28},{28,24},{1,5},{5... | collective-permute-start | bytes 7077896 | tf_op jit(solution)/shard_map/ppermute | solution.py:20
  135.4 42.3 %collective-permute-start.24 = (bf16[384,768]{1,0:T(8,128)(2,1)}, bf16[384,768]{1,0:T(8,128)(2,1)}, u32[]{:S(2)}, u32[]{:S(2)}) collective-permute-start(bf16[384,768]{1,0:T(8,128)(2,1)} %get-tuple-element.174), channel_id=1, source_target_pairs={{0,8},{4,12},{8,0},{12,4},{16,24},{20,28},{24,16},{28,20},{1,9},{5... | collective-permute-start | bytes 1769480 | tf_op jit(solution)/shard_map/ppermute | solution.py:20
  135.8 41.8 %collective-permute-start.25 = (bf16[384,768]{1,0:T(8,128)(2,1)}, bf16[384,768]{1,0:T(8,128)(2,1)}, u32[]{:S(2)}, u32[]{:S(2)}) collective-permute-start(bf16[384,768]{1,0:T(8,128)(2,1)} %get-tuple-element.175), channel_id=1, source_target_pairs={{0,16},{4,20},{8,24},{12,28},{16,0},{20,4},{24,8},{28,12},{1,17},{... | collective-permute-start | bytes 1769480 | tf_op jit(solution)/shard_map/ppermute | solution.py:20
  137.3 40.4 %collective-permute-start.26 = (bf16[384,768]{1,0:T(8,128)(2,1)S(1)}, bf16[384,768]{1,0:T(8,128)(2,1)}, u32[]{:S(2)}, u32[]{:S(2)}) collective-permute-start(bf16[384,768]{1,0:T(8,128)(2,1)S(1)} %get-tuple-element.176), channel_id=1, source_target_pairs={{0,24},{4,28},{8,16},{12,20},{16,8},{20,12},{24,0},{28,4},{1,25},{... | collective-permute-start | bytes 1769480 | tf_op jit(solution)/shard_map/ppermute | solution.py:20
  138.9 38.7 %collective-permute-start.27 = (s32[1,16384]{1,0:T(1,128)S(1)}, s32[1,16384]{1,0:T(1,128)S(1)}, u32[]{:S(2)}, u32[]{:S(2)}) collective-permute-start(s32[1,16384]{1,0:T(1,128)S(1)} %broadcast_select_fusion.34), channel_id=1, source_target_pairs={{0,16},{4,20},{8,24},{12,28},{16,0},{20,4},{24,8},{28,12},{1,17},{... | collective-permute-start | bytes 196616 | tf_op jit(solution)/shard_map/ppermute | solution.py:20
  177.7 6.4 %copy-start.5 = (bf16[4,96,3840]{2,1,0:T(8,128)(2,1)S(1)}, bf16[4,96,3840]{2,1,0:T(8,128)(2,1)}, u32[]{:S(2)}) copy-start(bf16[4,96,3840]{2,1,0:T(8,128)(2,1)} %get-tuple-element.173) | copy-start | bytes 8847364
  177.7 6.4 %collective-permute-start.28 = (bf16[4,96,3840]{2,1,0:T(8,128)(2,1)}, bf16[4,96,3840]{2,1,0:T(8,128)(2,1)S(1)}, u32[]{:S(2)}, u32[]{:S(2)}) collective-permute-start(bf16[4,96,3840]{2,1,0:T(8,128)(2,1)} %get-tuple-element.180), channel_id=1, source_target_pairs={{0,4},{4,0},{8,12},{12,8},{16,20},{20,16},{24,28},{28,24},{1,5},{5... | collective-permute-start | bytes 8847368 | tf_op jit(solution)/shard_map/ppermute | solution.py:20
  177.9 6.9 %collective-permute-start.31 = (s32[1,16384]{1,0:T(1,128)S(1)}, s32[1,16384]{1,0:T(1,128)S(1)}, u32[]{:S(2)}, u32[]{:S(2)}) collective-permute-start(s32[1,16384]{1,0:T(1,128)S(1)} %fusion.14), channel_id=1, source_target_pairs={{0,3},{1,2},{2,1},{3,0},{4,7},{5,6},{6,5},{7,4},{8,11},{9,10},{10,... | collective-permute-start | bytes 196616 | tf_op jit(solution)/shard_map/ppermute | solution.py:24
  179.5 8.6 %collective-permute-start.30 = (s32[1,16384]{1,0:T(1,128)S(1)}, s32[1,16384]{1,0:T(1,128)S(1)}, u32[]{:S(2)}, u32[]{:S(2)}) collective-permute-start(s32[1,16384]{1,0:T(1,128)S(1)} %fusion.14), channel_id=1, source_target_pairs={{0,2},{1,3},{2,0},{3,1},{4,6},{5,7},{6,4},{7,5},{8,10},{9,11},{10,... | collective-permute-start | bytes 196616 | tf_op jit(solution)/shard_map/ppermute | solution.py:24
  181.4 6.7 %collective-permute-start.29 = (s32[1,16384]{1,0:T(1,128)S(1)}, s32[1,16384]{1,0:T(1,128)S(1)}, u32[]{:S(2)}, u32[]{:S(2)}) collective-permute-start(s32[1,16384]{1,0:T(1,128)S(1)} %fusion.14), channel_id=1, source_target_pairs={{0,1},{1,0},{2,3},{3,2},{4,5},{5,4},{6,7},{7,6},{8,9},{9,8},{10,11... | collective-permute-start | bytes 196616 | tf_op jit(solution)/shard_map/ppermute | solution.py:24
  188.9 33.7 %collective-permute-start.35 = (bf16[96,768]{1,0:T(8,128)(2,1)}, bf16[96,768]{1,0:T(8,128)(2,1)S(1)}, u32[]{:S(2)}, u32[]{:S(2)}) collective-permute-start(bf16[96,768]{1,0:T(8,128)(2,1)} %get-tuple-element.274), channel_id=1, source_target_pairs={{0,1},{1,0},{2,3},{3,2},{4,5},{5,4},{6,7},{7,6},{8,9},{9,8},{10,11... | collective-permute-start | bytes 442376 | tf_op jit(solution)/shard_map/ppermute | solution.py:24
  188.9 33.7 %collective-permute-start.36 = (bf16[96,768]{1,0:T(8,128)(2,1)}, bf16[96,768]{1,0:T(8,128)(2,1)S(1)}, u32[]{:S(2)}, u32[]{:S(2)}) collective-permute-start(bf16[96,768]{1,0:T(8,128)(2,1)} %get-tuple-element.275), channel_id=1, source_target_pairs={{0,2},{1,3},{2,0},{3,1},{4,6},{5,7},{6,4},{7,5},{8,10},{9,11},{10,... | collective-permute-start | bytes 442376 | tf_op jit(solution)/shard_map/ppermute | solution.py:24
  191.4 31.3 %collective-permute-start.32 = (bf16[96,3840]{1,0:T(8,128)(2,1)S(1)}, bf16[96,3840]{1,0:T(8,128)(2,1)S(1)}, u32[]{:S(2)}, u32[]{:S(2)}) collective-permute-start(bf16[96,3840]{1,0:T(8,128)(2,1)S(1)} %get-tuple-element.193), channel_id=1, source_target_pairs={{0,8},{4,12},{8,0},{12,4},{16,24},{20,28},{24,16},{28,20},{1,9},{5... | collective-permute-start | bytes 2211848 | tf_op jit(solution)/shard_map/ppermute | solution.py:20
  193.2 33.4 %collective-permute-start.33 = (bf16[96,3840]{1,0:T(8,128)(2,1)S(1)}, bf16[96,3840]{1,0:T(8,128)(2,1)S(1)}, u32[]{:S(2)}, u32[]{:S(2)}) collective-permute-start(bf16[96,3840]{1,0:T(8,128)(2,1)S(1)} %get-tuple-element.194), channel_id=1, source_target_pairs={{0,16},{4,20},{8,24},{12,28},{16,0},{20,4},{24,8},{28,12},{1,17},{... | collective-permute-start | bytes 2211848 | tf_op jit(solution)/shard_map/ppermute | solution.py:20
  193.8 32.8 %collective-permute-start.34 = (bf16[96,3840]{1,0:T(8,128)(2,1)S(1)}, bf16[96,3840]{1,0:T(8,128)(2,1)S(1)}, u32[]{:S(2)}, u32[]{:S(2)}) collective-permute-start(bf16[96,3840]{1,0:T(8,128)(2,1)S(1)} %get-tuple-element.195), channel_id=1, source_target_pairs={{0,24},{4,28},{8,16},{12,20},{16,8},{20,12},{24,0},{28,4},{1,25},{... | collective-permute-start | bytes 2211848 | tf_op jit(solution)/shard_map/ppermute | solution.py:20
  226.6 6.0 %collective-permute-start.39 = (s32[1,16384]{1,0:T(1,128)S(1)}, s32[1,16384]{1,0:T(1,128)S(1)}, u32[]{:S(2)}, u32[]{:S(2)}) collective-permute-start(s32[1,16384]{1,0:T(1,128)S(1)} %add_add_fusion), channel_id=1, source_target_pairs={{0,16},{4,20},{8,24},{12,28},{16,0},{20,4},{24,8},{28,12},{1,17},{... | collective-permute-start | bytes 196616 | tf_op jit(solution)/shard_map/ppermute | solution.py:20
  227.2 7.2 %collective-permute-start.38 = (bf16[96,768]{1,0:T(8,128)(2,1)}, bf16[96,768]{1,0:T(8,128)(2,1)S(1)}, u32[]{:S(2)}, u32[]{:S(2)}) collective-permute-start(bf16[96,768]{1,0:T(8,128)(2,1)} %get-tuple-element.205), channel_id=1, source_target_pairs={{0,3},{1,2},{2,1},{3,0},{4,7},{5,6},{6,5},{7,4},{8,11},{9,10},{10,... | collective-permute-start | bytes 442376 | tf_op jit(solution)/shard_map/ppermute | solution.py:24
  228.2 3.9 %collective-permute-start.37 = (bf16[4,96,2304]{2,1,0:T(8,128)(2,1)}, bf16[4,96,2304]{2,1,0:T(8,128)(2,1)S(1)}, u32[]{:S(2)}, u32[]{:S(2)}) collective-permute-start(bf16[4,96,2304]{2,1,0:T(8,128)(2,1)} %get-tuple-element.202), channel_id=1, source_target_pairs={{0,4},{4,0},{8,12},{12,8},{16,20},{20,16},{24,28},{28,24},{1,5},{5... | collective-permute-start | bytes 5308424 | tf_op jit(solution)/shard_map/ppermute | solution.py:20
  234.6 5.2 %collective-permute-start.42 = (s32[2,16384]{1,0:T(2,128)S(1)}, s32[2,16384]{1,0:T(2,128)S(1)}, u32[]{:S(2)}, u32[]{:S(2)}) collective-permute-start(s32[2,16384]{1,0:T(2,128)S(1)} %pad_add_fusion.2), channel_id=1, source_target_pairs={{0,8},{4,12},{8,0},{12,4},{16,24},{20,28},{24,16},{28,20},{1,9},{5... | collective-permute-start | bytes 393224 | tf_op jit(solution)/shard_map/ppermute | solution.py:20
  236.3 17.0 %collective-permute-start.40 = (bf16[24,3840]{1,0:T(8,128)(2,1)S(1)}, bf16[24,3840]{1,0:T(8,128)(2,1)S(1)}, u32[]{:S(2)}, u32[]{:S(2)}) collective-permute-start(bf16[24,3840]{1,0:T(8,128)(2,1)S(1)} %get-tuple-element.212), channel_id=1, source_target_pairs={{0,1},{1,0},{2,3},{3,2},{4,5},{5,4},{6,7},{7,6},{8,9},{9,8},{10,11... | collective-permute-start | bytes 552968 | tf_op jit(solution)/shard_map/ppermute | solution.py:24
  236.9 16.4 %collective-permute-start.41 = (bf16[24,3840]{1,0:T(8,128)(2,1)S(1)}, bf16[24,3840]{1,0:T(8,128)(2,1)S(1)}, u32[]{:S(2)}, u32[]{:S(2)}) collective-permute-start(bf16[24,3840]{1,0:T(8,128)(2,1)S(1)} %get-tuple-element.213), channel_id=1, source_target_pairs={{0,2},{1,3},{2,0},{3,1},{4,6},{5,7},{6,4},{7,5},{8,10},{9,11},{10,... | collective-permute-start | bytes 552968 | tf_op jit(solution)/shard_map/ppermute | solution.py:24
  237.9 20.5 %collective-permute-start.43 = (bf16[96,2304]{1,0:T(8,128)(2,1)S(1)}, bf16[96,2304]{1,0:T(8,128)(2,1)S(1)}, u32[]{:S(2)}, u32[]{:S(2)}) collective-permute-start(bf16[96,2304]{1,0:T(8,128)(2,1)S(1)} %get-tuple-element.224), channel_id=1, source_target_pairs={{0,8},{4,12},{8,0},{12,4},{16,24},{20,28},{24,16},{28,20},{1,9},{5... | collective-permute-start | bytes 1327112 | tf_op jit(solution)/shard_map/ppermute | solution.py:20
  238.3 22.4 %collective-permute-start.44 = (bf16[96,2304]{1,0:T(8,128)(2,1)S(1)}, bf16[96,2304]{1,0:T(8,128)(2,1)S(1)}, u32[]{:S(2)}, u32[]{:S(2)}) collective-permute-start(bf16[96,2304]{1,0:T(8,128)(2,1)S(1)} %get-tuple-element.225), channel_id=1, source_target_pairs={{0,16},{4,20},{8,24},{12,28},{16,0},{20,4},{24,8},{28,12},{1,17},{... | collective-permute-start | bytes 1327112 | tf_op jit(solution)/shard_map/ppermute | solution.py:20
  239.8 20.9 %collective-permute-start.45 = (bf16[96,2304]{1,0:T(8,128)(2,1)S(1)}, bf16[96,2304]{1,0:T(8,128)(2,1)S(1)}, u32[]{:S(2)}, u32[]{:S(2)}) collective-permute-start(bf16[96,2304]{1,0:T(8,128)(2,1)S(1)} %get-tuple-element.226), channel_id=1, source_target_pairs={{0,24},{4,28},{8,16},{12,20},{16,8},{20,12},{24,0},{28,4},{1,25},{... | collective-permute-start | bytes 1327112 | tf_op jit(solution)/shard_map/ppermute | solution.py:20
  253.3 1.6 collective-permute-start.46
  253.3 2.3 collective-permute-start.47
  255.7 5.1 %collective-permute-start.48 = (bf16[96,128]{1,0:T(8,128)(2,1)S(1)}, bf16[96,128]{1,0:T(8,128)(2,1)S(1)}, u32[]{:S(2)}, u32[]{:S(2)}) collective-permute-start(bf16[96,128]{1,0:T(8,128)(2,1)S(1)} %get-tuple-element.230), channel_id=1, source_target_pairs={{0,8},{4,12},{8,0},{12,4},{16,24},{20,28},{24,16},{28,20},{1,9},{5... | collective-permute-start | bytes 73736 | tf_op jit(solution)/shard_map/ppermute | solution.py:20
  258.1 4.1 %collective-permute-start.49 = (bf16[96,128]{1,0:T(8,128)(2,1)S(1)}, bf16[96,128]{1,0:T(8,128)(2,1)S(1)}, u32[]{:S(2)}, u32[]{:S(2)}) collective-permute-start(bf16[96,128]{1,0:T(8,128)(2,1)S(1)} %get-tuple-element.231), channel_id=1, source_target_pairs={{0,16},{4,20},{8,24},{12,28},{16,0},{20,4},{24,8},{28,12},{1,17},{... | collective-permute-start | bytes 73736 | tf_op jit(solution)/shard_map/ppermute | solution.py:20
  258.3 4.8 %collective-permute-start.50 = (bf16[96,128]{1,0:T(8,128)(2,1)S(1)}, bf16[96,128]{1,0:T(8,128)(2,1)S(1)}, u32[]{:S(2)}, u32[]{:S(2)}) collective-permute-start(bf16[96,128]{1,0:T(8,128)(2,1)S(1)} %get-tuple-element.232), channel_id=1, source_target_pairs={{0,24},{4,28},{8,16},{12,20},{16,8},{20,12},{24,0},{28,4},{1,25},{... | collective-permute-start | bytes 73736 | tf_op jit(solution)/shard_map/ppermute | solution.py:20
  263.2 7.0 %collective-permute-start.55 = (bf16[24,128]{1,0:T(8,128)(2,1)S(1)}, bf16[24,128]{1,0:T(8,128)(2,1)S(1)}, u32[]{:S(2)}, u32[]{:S(2)}) collective-permute-start(bf16[24,128]{1,0:T(8,128)(2,1)S(1)} %get-tuple-element.297), channel_id=1, source_target_pairs={{0,1},{1,0},{2,3},{3,2},{4,5},{5,4},{6,7},{7,6},{8,9},{9,8},{10,11... | collective-permute-start | bytes 18440 | tf_op jit(solution)/shard_map/ppermute | solution.py:24
  264.2 8.2 %collective-permute-start.56 = (bf16[24,128]{1,0:T(8,128)(2,1)S(1)}, bf16[24,128]{1,0:T(8,128)(2,1)S(1)}, u32[]{:S(2)}, u32[]{:S(2)}) collective-permute-start(bf16[24,128]{1,0:T(8,128)(2,1)S(1)} %get-tuple-element.298), channel_id=1, source_target_pairs={{0,2},{1,3},{2,0},{3,1},{4,6},{5,7},{6,4},{7,5},{8,10},{9,11},{10,... | collective-permute-start | bytes 18440 | tf_op jit(solution)/shard_map/ppermute | solution.py:24
  266.0 8.6 %collective-permute-start.57 = (bf16[24,128]{1,0:T(8,128)(2,1)S(1)}, bf16[24,128]{1,0:T(8,128)(2,1)S(1)}, u32[]{:S(2)}, u32[]{:S(2)}) collective-permute-start(bf16[24,128]{1,0:T(8,128)(2,1)S(1)} %get-tuple-element.299), channel_id=1, source_target_pairs={{0,3},{1,2},{2,1},{3,0},{4,7},{5,6},{6,5},{7,4},{8,11},{9,10},{10,... | collective-permute-start | bytes 18440 | tf_op jit(solution)/shard_map/ppermute | solution.py:24
  267.6 17.5 %collective-permute-start.54 = (bf16[24,3840]{1,0:T(8,128)(2,1)S(1)}, bf16[24,3840]{1,0:T(8,128)(2,1)S(1)}, u32[]{:S(2)}, u32[]{:S(2)}) collective-permute-start(bf16[24,3840]{1,0:T(8,128)(2,1)S(1)} %get-tuple-element.240), channel_id=1, source_target_pairs={{0,3},{1,2},{2,1},{3,0},{4,7},{5,6},{6,5},{7,4},{8,11},{9,10},{10,... | collective-permute-start | bytes 552968 | tf_op jit(solution)/shard_map/ppermute | solution.py:24
  270.1 8.6 %collective-permute-start.51 = (bf16[24,2304]{1,0:T(8,128)(2,1)S(1)}, bf16[24,2304]{1,0:T(8,128)(2,1)S(1)}, u32[]{:S(2)}, u32[]{:S(2)}) collective-permute-start(bf16[24,2304]{1,0:T(8,128)(2,1)S(1)} %get-tuple-element.286), channel_id=1, source_target_pairs={{0,1},{1,0},{2,3},{3,2},{4,5},{5,4},{6,7},{7,6},{8,9},{9,8},{10,11... | collective-permute-start | bytes 331784 | tf_op jit(solution)/shard_map/ppermute | solution.py:24
  270.2 14.1 %collective-permute-start.52 = (bf16[24,2304]{1,0:T(8,128)(2,1)S(1)}, bf16[24,2304]{1,0:T(8,128)(2,1)S(1)}, u32[]{:S(2)}, u32[]{:S(2)}) collective-permute-start(bf16[24,2304]{1,0:T(8,128)(2,1)S(1)} %get-tuple-element.287), channel_id=1, source_target_pairs={{0,2},{1,3},{2,0},{3,1},{4,6},{5,7},{6,4},{7,5},{8,10},{9,11},{10,... | collective-permute-start | bytes 331784 | tf_op jit(solution)/shard_map/ppermute | solution.py:24
  272.4 11.9 %collective-permute-start.53 = (bf16[24,2304]{1,0:T(8,128)(2,1)S(1)}, bf16[24,2304]{1,0:T(8,128)(2,1)S(1)}, u32[]{:S(2)}, u32[]{:S(2)}) collective-permute-start(bf16[24,2304]{1,0:T(8,128)(2,1)S(1)} %get-tuple-element.288), channel_id=1, source_target_pairs={{0,3},{1,2},{2,1},{3,0},{4,7},{5,6},{6,5},{7,4},{8,11},{9,10},{10,... | collective-permute-start | bytes 331784 | tf_op jit(solution)/shard_map/ppermute | solution.py:24
  (8 other events, 16.6 us)

commit v3 on v2

--- a/solution.py
+++ b/solution.py
@@ -232,7 +232,7 @@
     qkv_ref[0, :, :width] = qkv[:, :width] * (1.0 / head_dim**0.5)
     qkv_ref[0, :, width:] = qkv[:, width:]
     lane = lax.broadcasted_iota(jnp.int32, (length, 128), 1)
-    seg = seg_ref[0]
+    seg = jnp.broadcast_to(seg_ref[0], (128, length)).T.astype(jnp.int32)
     key_seg = jnp.where(seg == lane, 1.0, 0.0).astype(jnp.bfloat16)
     query_seg = jnp.where(seg == lane, 0.0, -1e30).astype(jnp.bfloat16)
     for pair in range(H // 2):
@@ -408,23 +408,26 @@
 
 
 def return_kernel(
-    plan, count, plan_down, count_down, me_ref, y_ref, cot_ref, vec_ref, ht_ref, mixed_ref,
+    plan, count, plan_down, count_down, me_ref, y_hbm, cot_ref, vec_ref, ht_ref, mixed_hbm,
     rise_ref, act_ref, *rest
 ):
     pieces = rest[:count]
     down_pieces = rest[count : count + count_down]
     (
         grad_ref, out_ref, keep_ref, send_ref, sums_ref,
-        acc_ref, du_ref, w_ref, wd_ref, part_ref, out_grad_ref, sems, down_sems,
+        acc_ref, du_ref, w_ref, wd_ref, part_ref, out_grad_ref, y_ref, mixed_ref,
+        sems, down_sems, late_sems,
     ) = rest[count + count_down :]
     step = pl.program_id(0)
-    width = y_ref.shape[1]
+    width = cot_ref.shape[1]
     chunk = act_ref.shape[1]
     block = width // BLOCKS
     copies = [
         pltpu.make_async_copy(*pair)
         for pair in piece_pairs(pieces, plan, me_ref[0], block, w_ref, sems)
     ]
+    copies.append(pltpu.make_async_copy(y_hbm, y_ref, late_sems.at[0]))
+    copies.append(pltpu.make_async_copy(mixed_hbm, mixed_ref, late_sems.at[1]))
 
     @pl.when(step == 0)
     def _():
@@ -433,7 +436,7 @@
         )
         for copy in copies:
             copy.start()
-        acc_ref[...] = y_ref[...]
+        acc_ref[...] = jnp.zeros_like(acc_ref)
         out_grad_ref[...] = jnp.zeros_like(out_grad_ref)
         sums_ref[...] = jnp.zeros_like(sums_ref)
         for copy in down_copies:
@@ -453,9 +456,9 @@
 
     @pl.when(step == pl.num_programs(0) - 1)
     def _():
-        out_ref[...] = acc_ref[...].astype(jnp.bfloat16)
         for copy in copies:
             copy.wait()
+        out_ref[...] = (y_ref[...] + acc_ref[...]).astype(jnp.bfloat16)
         size = mixed_ref.shape[2]
 
         def body(place, carry):
@@ -490,7 +493,9 @@
         ),
         grid=(hidden // chunk + 1,),
         in_specs=[pl.BlockSpec(memory_space=pltpu.SMEM)]
-        + [whole_spec(v.shape) for v in (y_one, cotangent, vec, h_t, mixed)]
+        + any_specs([y_one])
+        + [whole_spec(v.shape) for v in (cotangent, vec, h_t)]
+        + any_specs([mixed])
         + [
             pl.BlockSpec((count, chunk), lambda j: (0, jnp.minimum(j, 3))),
             pl.BlockSpec((count, chunk), lambda j: (0, jnp.minimum(j, 3))),
@@ -508,8 +513,11 @@
             pltpu.VMEM((hidden, width), jnp.bfloat16),
             pltpu.VMEM((width, chunk), jnp.float32),
             pltpu.VMEM((width, width), jnp.float32),
+            pltpu.VMEM((count, width), jnp.float32),
+            pltpu.VMEM(mixed.shape, jnp.bfloat16),
             pltpu.SemaphoreType.DMA((BLOCKS,)),
             pltpu.SemaphoreType.DMA((BLOCKS,)),
+            pltpu.SemaphoreType.DMA((2,)),
         ],
         compiler_params=kernel_params(60),
         cost_estimate=pl.CostEstimate(
@@ -793,11 +801,13 @@
         late_received = scatter_sides(late_parts)
         *values, piece = together([*early_received, *late_received, piece])
         early_received, late_received = values[:3], values[3:]
+        up_inner.append(swap_inner(piece, inner - 1, inner))
         early_mine = add(early_parts[0], *early_received)
-        up_inner.append(swap_inner(piece, inner - 1, inner))
-        early_sum = sum_parts(scatter_inner(early_mine, inner))
+        late_mine = add(late_parts[0], *late_received)
+        both = jnp.concatenate([early_mine, late_mine], axis=1)
+        both = sum_parts(scatter_inner(both, inner))
         up_sum = sum_parts(up_pieces[:1] + up_inner)
-        late_sum = sum_parts(scatter_inner(add(late_parts[0], *late_received), inner))
+        early_sum, late_sum = both[:, : 3 * width], both[:, 3 * width :]
     else:
         up_sum, down_sum, early_sum, late_sum = [
             scatter_whole(*v) for v in (up_parts, down_parts, early, late)
@@ -835,7 +845,7 @@
     vectors = jnp.pad(vectors, ((0, 0), (0, 124)))
     ids = bucket_ids.reshape(-1, bucket_ids.shape[2]).T
     counts = count_buckets(ids)
-    segments = segment_ids[:, :, None]
+    segments = segment_ids.astype(jnp.float32)[:, None, :]
     shards = (
         jnp.concatenate([qkv_weight, vectors], axis=1),
         jnp.concatenate([up_weight, out_weight], axis=1),

time: 290 us -> 287 us (0.990)
    ppermute x24 -> x21, waiting for transfers between devices: 33.9 us -> 31.6 us  [swap_inner(): return lax.ppermute(value, 'fsdp', [(i, i ^ bit) for i in range(size)])]
    ppermute x24 -> x21, starting transfers between devices: 39.8 us -> 38.3 us  [swap_inner(): return lax.ppermute(value, 'fsdp', [(i, i ^ bit) for i in range(size)])]
  transfers between devices with their start and end apart: 58 -> 55, of which waited for: 19 -> 18; matrix products, arithmetic and copies ran while one was open for 5% -> 5% of each run, Pallas kernels for 46% -> 46%
where the time goes in v3:
time: 287 us; the launch traced here: 282 us
  Pallas kernels  131 us (46%)
  starting transfers between devices  68.7 us (24%)
  waiting for transfers between devices  53.8 us (19%)
  other arithmetic  15 us (5%)
  local copies, waits for them, and re-layouts  12.1 us (4%)
    ppermute x21, starting transfers between devices, swap_inner(): return lax.ppermute(value, 'fsdp', [(i, i ^ bit) for i in range(size)])  38.3 us
    pallas_call x1, Pallas kernels, feed_return(): pl.pallas_call(functools.partial(return_kernel, plan, len(pieces), plan_d...  37.2 us
    ppermute x21, waiting for transfers between devices, swap_inner(): return lax.ppermute(value, 'fsdp', [(i, i ^ bit) for i in range(size)])  31.6 us
    ppermute x34, starting transfers between devices, swap(): return lax.ppermute(value, 'dp', [(i, i ^ bit) for i in range(BLOCKS)])  30.3 us
    pallas_call x1, Pallas kernels, backward(): pl.pallas_call(functools.partial(backward_kernel, plan, len(pieces), grou...  27.6 us
    pallas_call x1, Pallas kernels, feed_forward(): pl.pallas_call(functools.partial(forward_kernel, plan, len(pieces)), grid...  27 us
    pallas_call x1, Pallas kernels, attend(): pl.pallas_call(functools.partial(attend_kernel, plan, len(pieces)), grid=...  24.7 us
    ppermute x34, waiting for transfers between devices, swap(): return lax.ppermute(value, 'dp', [(i, i ^ bit) for i in range(BLOCKS)])  22.2 us
  transfers between devices with their start and end apart: 55, of which 18 were waited for; matrix products, arithmetic and copies ran while one was open for 5% of the time, Pallas kernels for 46%

profile of v3, /device:TPU:0, one launch (start us, length us, event | category | flops | bytes accessed | tf_op | source)
XLA Modules:
  0.0 282.3 jit_solution(1336054727219845860)
XLA Ops:
  1.5 0.9 fusion.13
  2.4 3.1 %collective-permute-start.2 = (bf16[24,2432]{1,0:T(8,128)(2,1)S(1)}, bf16[24,2432]{1,0:T(8,128)(2,1)S(1)}, u32[]{:S(2)}, u32[]{:S(2)}) collective-permute-start(bf16[24,2432]{1,0:T(8,128)(2,1)S(1)} %fusion.13), channel_id=1, source_target_pairs={{0,1},{1,0},{2,3},{3,2},{4,5},{5,4},{6,7},{7,6},{8,9},{9,8},{10,11... | collective-permute-start | bytes 350216 | tf_op jit(solution)/shard_map/ppermute | solution.py:24
  5.5 2.6 collective-permute-start.1
  8.1 0.9 pad_maximum_fusion.6
  9.0 3.0 %shard_map.203 = s32[8,64,256]{2,1,0:T(8,128)} custom-call(s32[8,1024]{1,0:T(8,128)} %bitcast.85), custom_call_target="tpu_custom_call" | custom-call | flops 3000000000 | bytes 1000000 | tf_op jit(solution)/shard_map/pallas_call | solution.py:187
  12.6 1.3 copy.32
  14.0 3.3 %collective-permute-done.1 = bf16[24,2432]{1,0:T(8,128)(2,1)S(1)} collective-permute-done((bf16[24,2432]{1,0:T(8,128)(2,1)S(1)}, bf16[24,2432]{1,0:T(8,128)(2,1)S(1)}, u32[]{:S(2)}, u32[]{:S(2)}) %collective-permute-start.1) | collective-permute-done | bytes 116768 | tf_op jit(solution)/shard_map/ppermute | solution.py:24
  17.5 2.5 collective-permute-start.5
  21.0 2.5 collective-permute-start.8
  24.3 4.8 %collective-permute-done.8 = bf16[24,3840]{1,0:T(8,128)(2,1)S(1)} collective-permute-done((bf16[24,3840]{1,0:T(8,128)(2,1)S(1)}, bf16[24,3840]{1,0:T(8,128)(2,1)S(1)}, u32[]{:S(2)}, u32[]{:S(2)}) %collective-permute-start.8) | collective-permute-done | bytes 184352 | tf_op jit(solution)/shard_map/ppermute | solution.py:24
  29.1 6.5 %collective-permute-start.6 = (bf16[24,3840]{1,0:T(8,128)(2,1)S(1)}, bf16[24,3840]{1,0:T(8,128)(2,1)S(1)}, u32[]{:S(2)}, u32[]{:S(2)}) collective-permute-start(bf16[24,3840]{1,0:T(8,128)(2,1)S(1)} %pad_maximum_fusion.6), channel_id=1, source_target_pairs={{0,1},{1,0},{2,3},{3,2},{4,5},{5,4},{6,7},{7,6},{8,9},{9,8},{10,11... | collective-permute-start | bytes 552968 | tf_op jit(solution)/shard_map/ppermute | solution.py:24
  35.7 2.3 collective-permute-done.7
  38.0 3.4 %collective-permute-done.6 = bf16[24,3840]{1,0:T(8,128)(2,1)S(1)} collective-permute-done((bf16[24,3840]{1,0:T(8,128)(2,1)S(1)}, bf16[24,3840]{1,0:T(8,128)(2,1)S(1)}, u32[]{:S(2)}, u32[]{:S(2)}) %collective-permute-start.6) | collective-permute-done | bytes 184352 | tf_op jit(solution)/shard_map/ppermute | solution.py:24
  43.0 3.0 %collective-permute-done.9 = s32[4,16384]{1,0:T(4,128)S(1)} collective-permute-done((s32[4,16384]{1,0:T(4,128)S(1)}, s32[4,16384]{1,0:T(4,128)S(1)}, u32[]{:S(2)}, u32[]{:S(2)}) %collective-permute-start.9) | collective-permute-done | bytes 262176 | tf_op jit(solution)/shard_map/ppermute | solution.py:20
  46.1 1.3 copy-done.4
  47.4 2.4 collective-permute-start.13
  50.8 1.3 collective-permute-start.15
  52.2 1.6 collective-permute-start.14
  53.8 24.7 %shard_map.204 = (bf16[2,512,2304]{2,1,0:T(8,128)(2,1)}, bf16[2,12,512,512]{3,2,1,0:T(8,128)(2,1)}, f32[2,12,1,512]{3,2,1,0:T(1,128)}, bf16[2,768,512]{2,1,0:T(8...) custom-call(s32[1]{0:T(128)} %bitcast.me_ref, ...), custom_call_target="tpu_custom_call" | custom-call | flops 1000000000 | bytes 1000000 | tf_op jit(solution)/shard_map/pallas_call | solution.py:292
  78.5 4.1 %collective-permute-done.12 = bf16[96,3840]{1,0:T(8,128)(2,1)S(1)} collective-permute-done((bf16[96,3840]{1,0:T(8,128)(2,1)S(1)}, bf16[96,3840]{1,0:T(8,128)(2,1)S(1)}, u32[]{:S(2)}, u32[]{:S(2)}) %collective-permute-start.12) | collective-permute-done | bytes 737312 | tf_op jit(solution)/shard_map/ppermute | solution.py:20
  82.7 2.4 collective-permute-start.16
  86.1 4.4 %collective-permute-done.16 = bf16[96,768]{1,0:T(8,128)(2,1)S(1)} collective-permute-done((bf16[96,768]{1,0:T(8,128)(2,1)}, bf16[96,768]{1,0:T(8,128)(2,1)S(1)}, u32[]{:S(2)}, u32[]{:S(2)}) %collective-permute-start.16) | collective-permute-done | bytes 147488 | tf_op jit(solution)/shard_map/ppermute | solution.py:24
  90.5 1.1 broadcast_select_fusion.30
  91.7 1.6 copy-done.1
  93.2 1.1 collective-permute-start.20
  94.3 1.9 collective-permute-start.19
  96.8 1.6 collective-permute-start.21
  98.4 27.0 %shard_map.205 = (f32[1024,768]{1,0:T(8,128)}, bf16[768,1024]{1,0:T(8,128)(2,1)}, bf16[4,384,768]{2,1,0:T(8,128)(2,1)}, bf16[4,384,768]{2,1,0:T(8,128)(2,1)}, bf...) custom-call(s32[1]{0:T(128)} %bitcast.me_ref, bf16[1024,768]{1,0:T(8,128)(2,1)} %bitcast.59, ...), custom_call_target="tpu_custom_call" | custom-call | flops 1000000000 | bytes 1000000 | tf_op jit(solution)/shard_map/pallas_call | solution.py:379
  125.8 2.1 copy-done.13
  128.1 5.7 %collective-permute-done.22 = bf16[4,384,768]{2,1,0:T(8,128)(2,1)S(1)} collective-permute-done((bf16[4,384,768]{2,1,0:T(8,128)(2,1)S(1)}, bf16[4,384,768]{2,1,0:T(8,128)(2,1)S(1)}, u32[]{:S(2)}, u32[]{:S(2)}) %collective-permute-start.22) | collective-permute-done | bytes 2359328 | tf_op jit(solution)/shard_map/ppermute | solution.py:20
  133.7 1.6 fusion.7
  135.9 1.4 collective-permute-start.25
  137.3 1.6 collective-permute-start.26
  139.1 1.4 copy-done.6
  140.5 37.2 %shard_map.206 = (f32[1024,768]{1,0:T(8,128)}, bf16[1024,768]{1,0:T(8,128)(2,1)}, bf16[4,96,3840]{2,1,0:T(8,128)(2,1)}, bf16[4,96,3840]{2,1,0:T(8,128)(2,1)}, f32[8,768]{1,0:T(8,128)}) custom-call(s32[1]{0:T(128)} %bitcast.me_ref, f32[1024,768]{1,0:T(8,128)} %get-tuple-element.163.y_hbm, bf16[1024,768]{1,0:T(8,128)(2,1)} %bitcast.63, ...), custom_call_target="tpu_custom_call" | custom-call | flops 1000000000 | bytes 1000000 | tf_op jit(solution)/shard_map/pallas_call | solution.py:490
  178.0 2.4 collective-permute-start.31
  180.4 1.1 collective-permute-start.30
  181.5 0.9 collective-permute-start.29
  182.4 1.7 add_convert_fusion.5
  184.9 3.3 %collective-permute-done.30 = s32[1,16384]{1,0:T(1,128)S(1)} collective-permute-done((s32[1,16384]{1,0:T(1,128)S(1)}, s32[1,16384]{1,0:T(1,128)S(1)}, u32[]{:S(2)}, u32[]{:S(2)}) %collective-permute-start.30) | collective-permute-done | bytes 65568 | tf_op jit(solution)/shard_map/ppermute | solution.py:24
  189.0 3.2 %collective-permute-start.36 = (bf16[96,768]{1,0:T(8,128)(2,1)}, bf16[96,768]{1,0:T(8,128)(2,1)S(1)}, u32[]{:S(2)}, u32[]{:S(2)}) collective-permute-start(bf16[96,768]{1,0:T(8,128)(2,1)} %get-tuple-element.280), channel_id=1, source_target_pairs={{0,2},{1,3},{2,0},{3,1},{4,6},{5,7},{6,4},{7,5},{8,10},{9,11},{10,... | collective-permute-start | bytes 442376 | tf_op jit(solution)/shard_map/ppermute | solution.py:24
  192.2 1.2 collective-permute-start.32
  194.1 1.6 collective-permute-start.34
  195.8 27.6 %shard_map.207 = (bf16[2,512,2304]{2,1,0:T(8,128)(2,1)}, bf16[4,96,2304]{2,1,0:T(8,128)(2,1)}, bf16[4,96,2304]{2,1,0:T(8,128)(2,1)}) custom-call(s32[1]{0:T(128)} %bitcast.me_ref, f32[2,512,768]{2,1,0:T(8,128)} %bitcast.60, bf16[2,512,2304]{2,1,0:T(8,128)(2,1)} %get-tuple-element.188.q_ref.k_ref.v_ref, ...), custom_call_target="tpu_custom_call" | custom-call | flops 1000000000 | bytes 1000000 | tf_op jit(solution)/shard_map/pallas_call | solution.py:645
  223.5 2.9 %collective-permute-done.34 = bf16[96,3840]{1,0:T(8,128)(2,1)S(1)} collective-permute-done((bf16[96,3840]{1,0:T(8,128)(2,1)S(1)}, bf16[96,3840]{1,0:T(8,128)(2,1)S(1)}, u32[]{:S(2)}, u32[]{:S(2)}) %collective-permute-start.34) | collective-permute-done | bytes 737312 | tf_op jit(solution)/shard_map/ppermute | solution.py:20
  227.2 1.1 collective-permute-start.38
  228.8 3.5 %collective-permute-done.37 = bf16[4,96,2304]{2,1,0:T(8,128)(2,1)S(1)} collective-permute-done((bf16[4,96,2304]{2,1,0:T(8,128)(2,1)}, bf16[4,96,2304]{2,1,0:T(8,128)(2,1)S(1)}, u32[]{:S(2)}, u32[]{:S(2)}) %collective-permute-start.37) | collective-permute-done | bytes 1769504 | tf_op jit(solution)/shard_map/ppermute | solution.py:20
  232.7 1.7 collective-permute-done.38
  234.7 1.4 collective-permute-start.42
  236.1 1.8 collective-permute-start.41
  238.5 1.4 collective-permute-start.44
  239.8 2.0 collective-permute-start.45
  242.1 11.6 %shard_map.208 = (bf16[2,512,768]{2,1,0:T(8,128)(2,1)}, bf16[4,96,128]{2,1,0:T(8,128)(2,1)}, bf16[4,96,128]{2,1,0:T(8,128)(2,1)}) custom-call(s32[1]{0:T(128)} %bitcast.me_ref, f32[2,512,768]{2,1,0:T(8,128)} %bitcast.61, bf16[2,512,768]{2,1,0:T(8,128)(2,1)} %x_ref.3, bf16[2,512,2304]{2,1,0:T(8,128)(2,1)} %get-tuple-element.216.dqkv_ref, ...), custom_call_target="tpu_custom_call" | custom-call | flops 1000000000 | bytes 1000000 | tf_op jit(solution)/shard_map/pallas_call | solution.py:701
  254.3 0.8 convert_add_fusion.1
  256.2 1.0 collective-permute-start.48
  257.9 1.9 collective-permute-start.50
  260.1 1.0 collective-permute-done.49
  261.1 1.6 collective-permute-done.50
  263.0 1.3 collective-permute-start.51
  264.3 1.8 collective-permute-start.52
  266.1 1.5 collective-permute-start.53
  267.5 0.9 pad_add_fusion
  268.4 2.4 collective-permute-start.54
  270.8 8.2 %collective-permute-done.52 = bf16[24,2432]{1,0:T(8,128)(2,1)S(1)} collective-permute-done((bf16[24,2432]{1,0:T(8,128)(2,1)S(1)}, bf16[24,2432]{1,0:T(8,128)(2,1)S(1)}, u32[]{:S(2)}, u32[]{:S(2)}) %collective-permute-start.52) | collective-permute-done | bytes 116768 | tf_op jit(solution)/shard_map/ppermute | solution.py:24
  (128 shorter events, 20.2 us)
Async XLA Ops:
  2.4 11.6 %collective-permute-start.2 = (bf16[24,2432]{1,0:T(8,128)(2,1)S(1)}, bf16[24,2432]{1,0:T(8,128)(2,1)S(1)}, u32[]{:S(2)}, u32[]{:S(2)}) collective-permute-start(bf16[24,2432]{1,0:T(8,128)(2,1)S(1)} %fusion.13), channel_id=1, source_target_pairs={{0,1},{1,0},{2,3},{3,2},{4,5},{5,4},{6,7},{7,6},{8,9},{9,8},{10,11... | collective-permute-start | bytes 350216 | tf_op jit(solution)/shard_map/ppermute | solution.py:24
  5.5 11.9 %collective-permute-start.1 = (bf16[24,2432]{1,0:T(8,128)(2,1)S(1)}, bf16[24,2432]{1,0:T(8,128)(2,1)S(1)}, u32[]{:S(2)}, u32[]{:S(2)}) collective-permute-start(bf16[24,2432]{1,0:T(8,128)(2,1)S(1)} %fusion.13), channel_id=1, source_target_pairs={{0,2},{1,3},{2,0},{3,1},{4,6},{5,7},{6,4},{7,5},{8,10},{9,11},{10,... | collective-permute-start | bytes 350216 | tf_op jit(solution)/shard_map/ppermute | solution.py:24
  8.0 9.3 %collective-permute-start = (bf16[24,2432]{1,0:T(8,128)(2,1)S(1)}, bf16[24,2432]{1,0:T(8,128)(2,1)S(1)}, u32[]{:S(2)}, u32[]{:S(2)}) collective-permute-start(bf16[24,2432]{1,0:T(8,128)(2,1)S(1)} %fusion.13), channel_id=1, source_target_pairs={{0,3},{1,2},{2,1},{3,0},{4,7},{5,6},{6,5},{7,4},{8,11},{9,10},{10,... | collective-permute-start | bytes 350216 | tf_op jit(solution)/shard_map/ppermute | solution.py:24
  9.0 3.0 %copy-start.12 = (s32[2,512]{1,0:T(2,128)S(1)}, s32[2,512]{1,0:T(2,128)}, u32[]{:S(2)}) copy-start(s32[2,512]{1,0:T(2,128)} %param.13) | copy-start | bytes 12292
  9.0 8.3 %copy-start.9 = (bf16[24,2304]{1,0:T(8,128)(2,1)S(1)}, bf16[24,2304]{1,0:T(8,128)(2,1)}, u32[]{:S(2)}) copy-start(bf16[24,2304]{1,0:T(8,128)(2,1)} %param.16) | copy-start | bytes 331780
  17.5 24.0 %collective-permute-start.5 = (bf16[96,2432]{1,0:T(8,128)(2,1)S(1)}, bf16[96,2432]{1,0:T(8,128)(2,1)S(1)}, u32[]{:S(2)}, u32[]{:S(2)}) collective-permute-start(bf16[96,2432]{1,0:T(8,128)(2,1)S(1)} %pad_maximum_fusion.5), channel_id=1, source_target_pairs={{0,24},{4,28},{8,16},{12,20},{16,8},{20,12},{24,0},{28,4},{1,25},{... | collective-permute-start | bytes 1400840 | tf_op jit(solution)/shard_map/ppermute | solution.py:20
  20.0 21.5 %collective-permute-start.4 = (bf16[96,2432]{1,0:T(8,128)(2,1)S(1)}, bf16[96,2432]{1,0:T(8,128)(2,1)S(1)}, u32[]{:S(2)}, u32[]{:S(2)}) collective-permute-start(bf16[96,2432]{1,0:T(8,128)(2,1)S(1)} %pad_maximum_fusion.5), channel_id=1, source_target_pairs={{0,16},{4,20},{8,24},{12,28},{16,0},{20,4},{24,8},{28,12},{1,17},{... | collective-permute-start | bytes 1400840 | tf_op jit(solution)/shard_map/ppermute | solution.py:20
  20.5 21.0 %collective-permute-start.3 = (bf16[96,2432]{1,0:T(8,128)(2,1)S(1)}, bf16[96,2432]{1,0:T(8,128)(2,1)S(1)}, u32[]{:S(2)}, u32[]{:S(2)}) collective-permute-start(bf16[96,2432]{1,0:T(8,128)(2,1)S(1)} %pad_maximum_fusion.5), channel_id=1, source_target_pairs={{0,8},{4,12},{8,0},{12,4},{16,24},{20,28},{24,16},{28,20},{1,9},{5... | collective-permute-start | bytes 1400840 | tf_op jit(solution)/shard_map/ppermute | solution.py:20
  21.0 8.1 %collective-permute-start.8 = (bf16[24,3840]{1,0:T(8,128)(2,1)S(1)}, bf16[24,3840]{1,0:T(8,128)(2,1)S(1)}, u32[]{:S(2)}, u32[]{:S(2)}) collective-permute-start(bf16[24,3840]{1,0:T(8,128)(2,1)S(1)} %pad_maximum_fusion.6), channel_id=1, source_target_pairs={{0,3},{1,2},{2,1},{3,0},{4,7},{5,6},{6,5},{7,4},{8,11},{9,10},{10,... | collective-permute-start | bytes 552968 | tf_op jit(solution)/shard_map/ppermute | solution.py:24
  23.5 14.5 %collective-permute-start.7 = (bf16[24,3840]{1,0:T(8,128)(2,1)S(1)}, bf16[24,3840]{1,0:T(8,128)(2,1)S(1)}, u32[]{:S(2)}, u32[]{:S(2)}) collective-permute-start(bf16[24,3840]{1,0:T(8,128)(2,1)S(1)} %pad_maximum_fusion.6), channel_id=1, source_target_pairs={{0,2},{1,3},{2,0},{3,1},{4,6},{5,7},{6,4},{7,5},{8,10},{9,11},{10,... | collective-permute-start | bytes 552968 | tf_op jit(solution)/shard_map/ppermute | solution.py:24
  29.1 12.3 %collective-permute-start.6 = (bf16[24,3840]{1,0:T(8,128)(2,1)S(1)}, bf16[24,3840]{1,0:T(8,128)(2,1)S(1)}, u32[]{:S(2)}, u32[]{:S(2)}) collective-permute-start(bf16[24,3840]{1,0:T(8,128)(2,1)S(1)} %pad_maximum_fusion.6), channel_id=1, source_target_pairs={{0,1},{1,0},{2,3},{3,2},{4,5},{5,4},{6,7},{7,6},{8,9},{9,8},{10,11... | collective-permute-start | bytes 552968 | tf_op jit(solution)/shard_map/ppermute | solution.py:24
  41.8 4.3 %collective-permute-start.10 = (bf16[4,96,2432]{2,1,0:T(8,128)(2,1)S(1)}, bf16[4,96,2432]{2,1,0:T(8,128)(2,1)S(1)}, u32[]{:S(2)}, u32[]{:S(2)}) collective-permute-start(bf16[4,96,2432]{2,1,0:T(8,128)(2,1)S(1)} %pad_maximum_fusion.2.rest_0_), channel_id=1, source_target_pairs={{0,4},{4,0},{8,12},{12,8},{16,20},{20,16},{24,28},{28,24},{1,5},{5... | collective-permute-start | bytes 5603336 | tf_op jit(solution)/shard_map/ppermute | solution.py:20
  41.9 4.1 %collective-permute-start.9 = (s32[4,16384]{1,0:T(4,128)S(1)}, s32[4,16384]{1,0:T(4,128)S(1)}, u32[]{:S(2)}, u32[]{:S(2)}) collective-permute-start(s32[4,16384]{1,0:T(4,128)S(1)} %slice_select_fusion), channel_id=1, source_target_pairs={{0,4},{4,0},{8,12},{12,8},{16,20},{20,16},{24,28},{28,24},{1,5},{5... | collective-permute-start | bytes 786440 | tf_op jit(solution)/shard_map/ppermute | solution.py:20
  46.1 3.7 %copy-start.10 = (s32[4,16384]{1,0:T(4,128)}, s32[4,16384]{1,0:T(4,128)S(1)}, u32[]{:S(2)}) copy-start(s32[4,16384]{1,0:T(4,128)S(1)} %collective-permute-done.9) | copy-start | bytes 786436
  47.4 31.1 %collective-permute-start.13 = (bf16[96,3840]{1,0:T(8,128)(2,1)S(1)}, bf16[96,3840]{1,0:T(8,128)(2,1)S(1)}, u32[]{:S(2)}, u32[]{:S(2)}) collective-permute-start(bf16[96,3840]{1,0:T(8,128)(2,1)S(1)} %pad_maximum_fusion.3), channel_id=1, source_target_pairs={{0,24},{4,28},{8,16},{12,20},{16,8},{20,12},{24,0},{28,4},{1,25},{... | collective-permute-start | bytes 2211848 | tf_op jit(solution)/shard_map/ppermute | solution.py:20
  49.8 32.8 %collective-permute-start.12 = (bf16[96,3840]{1,0:T(8,128)(2,1)S(1)}, bf16[96,3840]{1,0:T(8,128)(2,1)S(1)}, u32[]{:S(2)}, u32[]{:S(2)}) collective-permute-start(bf16[96,3840]{1,0:T(8,128)(2,1)S(1)} %pad_maximum_fusion.3), channel_id=1, source_target_pairs={{0,16},{4,20},{8,24},{12,28},{16,0},{20,4},{24,8},{28,12},{1,17},{... | collective-permute-start | bytes 2211848 | tf_op jit(solution)/shard_map/ppermute | solution.py:20
  50.3 32.4 %collective-permute-start.11 = (bf16[96,3840]{1,0:T(8,128)(2,1)S(1)}, bf16[96,3840]{1,0:T(8,128)(2,1)S(1)}, u32[]{:S(2)}, u32[]{:S(2)}) collective-permute-start(bf16[96,3840]{1,0:T(8,128)(2,1)S(1)} %pad_maximum_fusion.3), channel_id=1, source_target_pairs={{0,8},{4,12},{8,0},{12,4},{16,24},{20,28},{24,16},{28,20},{1,9},{5... | collective-permute-start | bytes 2211848 | tf_op jit(solution)/shard_map/ppermute | solution.py:20
  50.8 27.6 %collective-permute-start.15 = (bf16[96,768]{1,0:T(8,128)(2,1)}, bf16[96,768]{1,0:T(8,128)(2,1)}, u32[]{:S(2)}, u32[]{:S(2)}) collective-permute-start(bf16[96,768]{1,0:T(8,128)(2,1)} %param.19), channel_id=1, source_target_pairs={{0,2},{1,3},{2,0},{3,1},{4,6},{5,7},{6,4},{7,5},{8,10},{9,11},{10,... | collective-permute-start | bytes 442376 | tf_op jit(solution)/shard_map/ppermute | solution.py:24
  52.2 26.3 %collective-permute-start.14 = (bf16[96,768]{1,0:T(8,128)(2,1)}, bf16[96,768]{1,0:T(8,128)(2,1)}, u32[]{:S(2)}, u32[]{:S(2)}) collective-permute-start(bf16[96,768]{1,0:T(8,128)(2,1)} %param.19), channel_id=1, source_target_pairs={{0,1},{1,0},{2,3},{3,2},{4,5},{5,4},{6,7},{7,6},{8,9},{9,8},{10,11... | collective-permute-start | bytes 442376 | tf_op jit(solution)/shard_map/ppermute | solution.py:24
  82.7 7.8 %collective-permute-start.16 = (bf16[96,768]{1,0:T(8,128)(2,1)}, bf16[96,768]{1,0:T(8,128)(2,1)S(1)}, u32[]{:S(2)}, u32[]{:S(2)}) collective-permute-start(bf16[96,768]{1,0:T(8,128)(2,1)} %param.19), channel_id=1, source_target_pairs={{0,3},{1,2},{2,1},{3,0},{4,7},{5,6},{6,5},{7,4},{8,11},{9,10},{10,... | collective-permute-start | bytes 442376 | tf_op jit(solution)/shard_map/ppermute | solution.py:24
  85.5 6.2 %copy-start = (bf16[4,96,3840]{2,1,0:T(8,128)(2,1)}, bf16[4,96,3840]{2,1,0:T(8,128)(2,1)S(1)}, u32[]{:S(2)}) copy-start(bf16[4,96,3840]{2,1,0:T(8,128)(2,1)S(1)} %pad_maximum_fusion.rest_0_) | copy-start | bytes 8847364
  85.5 6.2 %collective-permute-start.17 = (bf16[4,96,3840]{2,1,0:T(8,128)(2,1)S(1)}, bf16[4,96,3840]{2,1,0:T(8,128)(2,1)S(1)}, u32[]{:S(2)}, u32[]{:S(2)}) collective-permute-start(bf16[4,96,3840]{2,1,0:T(8,128)(2,1)S(1)} %pad_maximum_fusion.rest_0_), channel_id=1, source_target_pairs={{0,4},{4,0},{8,12},{12,8},{16,20},{20,16},{24,28},{28,24},{1,5},{5... | collective-permute-start | bytes 8847368 | tf_op jit(solution)/shard_map/ppermute | solution.py:20
  93.2 32.2 %collective-permute-start.20 = (bf16[384,768]{1,0:T(8,128)(2,1)S(1)}, bf16[384,768]{1,0:T(8,128)(2,1)S(1)}, u32[]{:S(2)}, u32[]{:S(2)}) collective-permute-start(bf16[384,768]{1,0:T(8,128)(2,1)S(1)} %pad_maximum_fusion.4), channel_id=1, source_target_pairs={{0,24},{4,28},{8,16},{12,20},{16,8},{20,12},{24,0},{28,4},{1,25},{... | collective-permute-start | bytes 1769480 | tf_op jit(solution)/shard_map/ppermute | solution.py:20
  94.3 31.1 %collective-permute-start.19 = (bf16[384,768]{1,0:T(8,128)(2,1)S(1)}, bf16[384,768]{1,0:T(8,128)(2,1)S(1)}, u32[]{:S(2)}, u32[]{:S(2)}) collective-permute-start(bf16[384,768]{1,0:T(8,128)(2,1)S(1)} %pad_maximum_fusion.4), channel_id=1, source_target_pairs={{0,16},{4,20},{8,24},{12,28},{16,0},{20,4},{24,8},{28,12},{1,17},{... | collective-permute-start | bytes 1769480 | tf_op jit(solution)/shard_map/ppermute | solution.py:20
  96.2 29.2 %collective-permute-start.18 = (bf16[384,768]{1,0:T(8,128)(2,1)S(1)}, bf16[384,768]{1,0:T(8,128)(2,1)S(1)}, u32[]{:S(2)}, u32[]{:S(2)}) collective-permute-start(bf16[384,768]{1,0:T(8,128)(2,1)S(1)} %pad_maximum_fusion.4), channel_id=1, source_target_pairs={{0,8},{4,12},{8,0},{12,4},{16,24},{20,28},{24,16},{28,20},{1,9},{5... | collective-permute-start | bytes 1769480 | tf_op jit(solution)/shard_map/ppermute | solution.py:20
  96.8 28.6 %collective-permute-start.21 = (s32[2,16384]{1,0:T(2,128)S(1)}, s32[2,16384]{1,0:T(2,128)S(1)}, u32[]{:S(2)}, u32[]{:S(2)}) collective-permute-start(s32[2,16384]{1,0:T(2,128)S(1)} %broadcast_select_fusion.37), channel_id=1, source_target_pairs={{0,8},{4,12},{8,0},{12,4},{16,24},{20,28},{24,16},{28,20},{1,9},{5... | collective-permute-start | bytes 393224 | tf_op jit(solution)/shard_map/ppermute | solution.py:20
  125.4 2.5 copy-start.13
  125.4 8.3 %copy-start.7 = (bf16[4,384,768]{2,1,0:T(8,128)(2,1)S(1)}, bf16[4,384,768]{2,1,0:T(8,128)(2,1)}, u32[]{:S(2)}) copy-start(bf16[4,384,768]{2,1,0:T(8,128)(2,1)} %get-tuple-element.161) | copy-start | bytes 7077892
  125.8 9.6 %copy-start.3 = (bf16[4,384,768]{2,1,0:T(8,128)(2,1)}, bf16[4,384,768]{2,1,0:T(8,128)(2,1)S(1)}, u32[]{:S(2)}) copy-start(bf16[4,384,768]{2,1,0:T(8,128)(2,1)S(1)} %pad_maximum_fusion.1.rest_2_) | copy-start | bytes 7077892
  125.8 13.3 %collective-permute-start.23 = (bf16[4,384,768]{2,1,0:T(8,128)(2,1)S(1)}, bf16[4,384,768]{2,1,0:T(8,128)(2,1)S(1)}, u32[]{:S(2)}, u32[]{:S(2)}) collective-permute-start(bf16[4,384,768]{2,1,0:T(8,128)(2,1)S(1)} %pad_maximum_fusion.1.rest_2_), channel_id=1, source_target_pairs={{0,4},{4,0},{8,12},{12,8},{16,20},{20,16},{24,28},{28,24},{1,5},{5... | collective-permute-start | bytes 7077896 | tf_op jit(solution)/shard_map/ppermute | solution.py:20
  128.0 5.8 %collective-permute-start.22 = (bf16[4,384,768]{2,1,0:T(8,128)(2,1)S(1)}, bf16[4,384,768]{2,1,0:T(8,128)(2,1)S(1)}, u32[]{:S(2)}, u32[]{:S(2)}) collective-permute-start(bf16[4,384,768]{2,1,0:T(8,128)(2,1)S(1)} %copy-done.13), channel_id=1, source_target_pairs={{0,4},{4,0},{8,12},{12,8},{16,20},{20,16},{24,28},{28,24},{1,5},{5... | collective-permute-start | bytes 7077896 | tf_op jit(solution)/shard_map/ppermute | solution.py:20
  135.4 42.4 %collective-permute-start.24 = (bf16[384,768]{1,0:T(8,128)(2,1)}, bf16[384,768]{1,0:T(8,128)(2,1)}, u32[]{:S(2)}, u32[]{:S(2)}) collective-permute-start(bf16[384,768]{1,0:T(8,128)(2,1)} %get-tuple-element.174), channel_id=1, source_target_pairs={{0,8},{4,12},{8,0},{12,4},{16,24},{20,28},{24,16},{28,20},{1,9},{5... | collective-permute-start | bytes 1769480 | tf_op jit(solution)/shard_map/ppermute | solution.py:20
  135.9 41.9 %collective-permute-start.25 = (bf16[384,768]{1,0:T(8,128)(2,1)}, bf16[384,768]{1,0:T(8,128)(2,1)}, u32[]{:S(2)}, u32[]{:S(2)}) collective-permute-start(bf16[384,768]{1,0:T(8,128)(2,1)} %get-tuple-element.175), channel_id=1, source_target_pairs={{0,16},{4,20},{8,24},{12,28},{16,0},{20,4},{24,8},{28,12},{1,17},{... | collective-permute-start | bytes 1769480 | tf_op jit(solution)/shard_map/ppermute | solution.py:20
  137.3 40.5 %collective-permute-start.26 = (bf16[384,768]{1,0:T(8,128)(2,1)S(1)}, bf16[384,768]{1,0:T(8,128)(2,1)}, u32[]{:S(2)}, u32[]{:S(2)}) collective-permute-start(bf16[384,768]{1,0:T(8,128)(2,1)S(1)} %get-tuple-element.176), channel_id=1, source_target_pairs={{0,24},{4,28},{8,16},{12,20},{16,8},{20,12},{24,0},{28,4},{1,25},{... | collective-permute-start | bytes 1769480 | tf_op jit(solution)/shard_map/ppermute | solution.py:20
  138.9 38.8 %collective-permute-start.27 = (s32[1,16384]{1,0:T(1,128)S(1)}, s32[1,16384]{1,0:T(1,128)S(1)}, u32[]{:S(2)}, u32[]{:S(2)}) collective-permute-start(s32[1,16384]{1,0:T(1,128)S(1)} %broadcast_select_fusion.34), channel_id=1, source_target_pairs={{0,16},{4,20},{8,24},{12,28},{16,0},{20,4},{24,8},{28,12},{1,17},{... | collective-permute-start | bytes 196616 | tf_op jit(solution)/shard_map/ppermute | solution.py:20
  177.8 6.4 %copy-start.5 = (bf16[4,96,3840]{2,1,0:T(8,128)(2,1)S(1)}, bf16[4,96,3840]{2,1,0:T(8,128)(2,1)}, u32[]{:S(2)}) copy-start(bf16[4,96,3840]{2,1,0:T(8,128)(2,1)} %get-tuple-element.173) | copy-start | bytes 8847364
  177.8 6.4 %collective-permute-start.28 = (bf16[4,96,3840]{2,1,0:T(8,128)(2,1)}, bf16[4,96,3840]{2,1,0:T(8,128)(2,1)S(1)}, u32[]{:S(2)}, u32[]{:S(2)}) collective-permute-start(bf16[4,96,3840]{2,1,0:T(8,128)(2,1)} %get-tuple-element.180), channel_id=1, source_target_pairs={{0,4},{4,0},{8,12},{12,8},{16,20},{20,16},{24,28},{28,24},{1,5},{5... | collective-permute-start | bytes 8847368 | tf_op jit(solution)/shard_map/ppermute | solution.py:20
  178.0 6.9 %collective-permute-start.31 = (s32[1,16384]{1,0:T(1,128)S(1)}, s32[1,16384]{1,0:T(1,128)S(1)}, u32[]{:S(2)}, u32[]{:S(2)}) collective-permute-start(s32[1,16384]{1,0:T(1,128)S(1)} %fusion.17), channel_id=1, source_target_pairs={{0,3},{1,2},{2,1},{3,0},{4,7},{5,6},{6,5},{7,4},{8,11},{9,10},{10,... | collective-permute-start | bytes 196616 | tf_op jit(solution)/shard_map/ppermute | solution.py:24
  180.4 7.8 %collective-permute-start.30 = (s32[1,16384]{1,0:T(1,128)S(1)}, s32[1,16384]{1,0:T(1,128)S(1)}, u32[]{:S(2)}, u32[]{:S(2)}) collective-permute-start(s32[1,16384]{1,0:T(1,128)S(1)} %fusion.17), channel_id=1, source_target_pairs={{0,2},{1,3},{2,0},{3,1},{4,6},{5,7},{6,4},{7,5},{8,10},{9,11},{10,... | collective-permute-start | bytes 196616 | tf_op jit(solution)/shard_map/ppermute | solution.py:24
  181.5 6.7 %collective-permute-start.29 = (s32[1,16384]{1,0:T(1,128)S(1)}, s32[1,16384]{1,0:T(1,128)S(1)}, u32[]{:S(2)}, u32[]{:S(2)}) collective-permute-start(s32[1,16384]{1,0:T(1,128)S(1)} %fusion.17), channel_id=1, source_target_pairs={{0,1},{1,0},{2,3},{3,2},{4,5},{5,4},{6,7},{7,6},{8,9},{9,8},{10,11... | collective-permute-start | bytes 196616 | tf_op jit(solution)/shard_map/ppermute | solution.py:24
  189.0 34.5 %collective-permute-start.35 = (bf16[96,768]{1,0:T(8,128)(2,1)}, bf16[96,768]{1,0:T(8,128)(2,1)S(1)}, u32[]{:S(2)}, u32[]{:S(2)}) collective-permute-start(bf16[96,768]{1,0:T(8,128)(2,1)} %get-tuple-element.279), channel_id=1, source_target_pairs={{0,1},{1,0},{2,3},{3,2},{4,5},{5,4},{6,7},{7,6},{8,9},{9,8},{10,11... | collective-permute-start | bytes 442376 | tf_op jit(solution)/shard_map/ppermute | solution.py:24
  189.0 34.5 %collective-permute-start.36 = (bf16[96,768]{1,0:T(8,128)(2,1)}, bf16[96,768]{1,0:T(8,128)(2,1)S(1)}, u32[]{:S(2)}, u32[]{:S(2)}) collective-permute-start(bf16[96,768]{1,0:T(8,128)(2,1)} %get-tuple-element.280), channel_id=1, source_target_pairs={{0,2},{1,3},{2,0},{3,1},{4,6},{5,7},{6,4},{7,5},{8,10},{9,11},{10,... | collective-permute-start | bytes 442376 | tf_op jit(solution)/shard_map/ppermute | solution.py:24
  192.2 31.3 %collective-permute-start.32 = (bf16[96,3840]{1,0:T(8,128)(2,1)S(1)}, bf16[96,3840]{1,0:T(8,128)(2,1)S(1)}, u32[]{:S(2)}, u32[]{:S(2)}) collective-permute-start(bf16[96,3840]{1,0:T(8,128)(2,1)S(1)} %get-tuple-element.193), channel_id=1, source_target_pairs={{0,8},{4,12},{8,0},{12,4},{16,24},{20,28},{24,16},{28,20},{1,9},{5... | collective-permute-start | bytes 2211848 | tf_op jit(solution)/shard_map/ppermute | solution.py:20
  193.4 30.1 %collective-permute-start.33 = (bf16[96,3840]{1,0:T(8,128)(2,1)S(1)}, bf16[96,3840]{1,0:T(8,128)(2,1)S(1)}, u32[]{:S(2)}, u32[]{:S(2)}) collective-permute-start(bf16[96,3840]{1,0:T(8,128)(2,1)S(1)} %get-tuple-element.194), channel_id=1, source_target_pairs={{0,16},{4,20},{8,24},{12,28},{16,0},{20,4},{24,8},{28,12},{1,17},{... | collective-permute-start | bytes 2211848 | tf_op jit(solution)/shard_map/ppermute | solution.py:20
  194.1 32.4 %collective-permute-start.34 = (bf16[96,3840]{1,0:T(8,128)(2,1)S(1)}, bf16[96,3840]{1,0:T(8,128)(2,1)S(1)}, u32[]{:S(2)}, u32[]{:S(2)}) collective-permute-start(bf16[96,3840]{1,0:T(8,128)(2,1)S(1)} %get-tuple-element.195), channel_id=1, source_target_pairs={{0,24},{4,28},{8,16},{12,20},{16,8},{20,12},{24,0},{28,4},{1,25},{... | collective-permute-start | bytes 2211848 | tf_op jit(solution)/shard_map/ppermute | solution.py:20
  226.4 6.3 %collective-permute-start.39 = (s32[1,16384]{1,0:T(1,128)S(1)}, s32[1,16384]{1,0:T(1,128)S(1)}, u32[]{:S(2)}, u32[]{:S(2)}) collective-permute-start(s32[1,16384]{1,0:T(1,128)S(1)} %add_add_fusion), channel_id=1, source_target_pairs={{0,16},{4,20},{8,24},{12,28},{16,0},{20,4},{24,8},{28,12},{1,17},{... | collective-permute-start | bytes 196616 | tf_op jit(solution)/shard_map/ppermute | solution.py:20
  227.2 7.3 %collective-permute-start.38 = (bf16[96,768]{1,0:T(8,128)(2,1)}, bf16[96,768]{1,0:T(8,128)(2,1)S(1)}, u32[]{:S(2)}, u32[]{:S(2)}) collective-permute-start(bf16[96,768]{1,0:T(8,128)(2,1)} %get-tuple-element.205), channel_id=1, source_target_pairs={{0,3},{1,2},{2,1},{3,0},{4,7},{5,6},{6,5},{7,4},{8,11},{9,10},{10,... | collective-permute-start | bytes 442376 | tf_op jit(solution)/shard_map/ppermute | solution.py:24
  228.4 3.9 %collective-permute-start.37 = (bf16[4,96,2304]{2,1,0:T(8,128)(2,1)}, bf16[4,96,2304]{2,1,0:T(8,128)(2,1)S(1)}, u32[]{:S(2)}, u32[]{:S(2)}) collective-permute-start(bf16[4,96,2304]{2,1,0:T(8,128)(2,1)} %get-tuple-element.202), channel_id=1, source_target_pairs={{0,4},{4,0},{8,12},{12,8},{16,20},{20,16},{24,28},{28,24},{1,5},{5... | collective-permute-start | bytes 5308424 | tf_op jit(solution)/shard_map/ppermute | solution.py:20
  228.4 3.9 %copy-start.8 = (bf16[4,96,2304]{2,1,0:T(8,128)(2,1)S(1)}, bf16[4,96,2304]{2,1,0:T(8,128)(2,1)}, u32[]{:S(2)}) copy-start(bf16[4,96,2304]{2,1,0:T(8,128)(2,1)} %get-tuple-element.192) | copy-start | bytes 5308420
  234.7 5.2 %collective-permute-start.42 = (s32[2,16384]{1,0:T(2,128)S(1)}, s32[2,16384]{1,0:T(2,128)S(1)}, u32[]{:S(2)}, u32[]{:S(2)}) collective-permute-start(s32[2,16384]{1,0:T(2,128)S(1)} %pad_add_fusion.2), channel_id=1, source_target_pairs={{0,8},{4,12},{8,0},{12,4},{16,24},{20,28},{24,16},{28,20},{1,9},{5... | collective-permute-start | bytes 393224 | tf_op jit(solution)/shard_map/ppermute | solution.py:20
  236.1 17.7 %collective-permute-start.40 = (bf16[24,3840]{1,0:T(8,128)(2,1)S(1)}, bf16[24,3840]{1,0:T(8,128)(2,1)S(1)}, u32[]{:S(2)}, u32[]{:S(2)}) collective-permute-start(bf16[24,3840]{1,0:T(8,128)(2,1)S(1)} %get-tuple-element.212), channel_id=1, source_target_pairs={{0,1},{1,0},{2,3},{3,2},{4,5},{5,4},{6,7},{7,6},{8,9},{9,8},{10,11... | collective-permute-start | bytes 552968 | tf_op jit(solution)/shard_map/ppermute | solution.py:24
  236.1 17.7 %collective-permute-start.41 = (bf16[24,3840]{1,0:T(8,128)(2,1)S(1)}, bf16[24,3840]{1,0:T(8,128)(2,1)S(1)}, u32[]{:S(2)}, u32[]{:S(2)}) collective-permute-start(bf16[24,3840]{1,0:T(8,128)(2,1)S(1)} %get-tuple-element.213), channel_id=1, source_target_pairs={{0,2},{1,3},{2,0},{3,1},{4,6},{5,7},{6,4},{7,5},{8,10},{9,11},{10,... | collective-permute-start | bytes 552968 | tf_op jit(solution)/shard_map/ppermute | solution.py:24
  237.9 20.0 %collective-permute-start.43 = (bf16[96,2304]{1,0:T(8,128)(2,1)S(1)}, bf16[96,2304]{1,0:T(8,128)(2,1)S(1)}, u32[]{:S(2)}, u32[]{:S(2)}) collective-permute-start(bf16[96,2304]{1,0:T(8,128)(2,1)S(1)} %get-tuple-element.224), channel_id=1, source_target_pairs={{0,8},{4,12},{8,0},{12,4},{16,24},{20,28},{24,16},{28,20},{1,9},{5... | collective-permute-start | bytes 1327112 | tf_op jit(solution)/shard_map/ppermute | solution.py:20
  238.5 21.4 %collective-permute-start.44 = (bf16[96,2304]{1,0:T(8,128)(2,1)S(1)}, bf16[96,2304]{1,0:T(8,128)(2,1)S(1)}, u32[]{:S(2)}, u32[]{:S(2)}) collective-permute-start(bf16[96,2304]{1,0:T(8,128)(2,1)S(1)} %get-tuple-element.225), channel_id=1, source_target_pairs={{0,16},{4,20},{8,24},{12,28},{16,0},{20,4},{24,8},{28,12},{1,17},{... | collective-permute-start | bytes 1327112 | tf_op jit(solution)/shard_map/ppermute | solution.py:20
  239.8 20.0 %collective-permute-start.45 = (bf16[96,2304]{1,0:T(8,128)(2,1)S(1)}, bf16[96,2304]{1,0:T(8,128)(2,1)S(1)}, u32[]{:S(2)}, u32[]{:S(2)}) collective-permute-start(bf16[96,2304]{1,0:T(8,128)(2,1)S(1)} %get-tuple-element.226), channel_id=1, source_target_pairs={{0,24},{4,28},{8,16},{12,20},{16,8},{20,12},{24,0},{28,4},{1,25},{... | collective-permute-start | bytes 1327112 | tf_op jit(solution)/shard_map/ppermute | solution.py:20
  253.8 1.6 collective-permute-start.46
  253.8 2.3 collective-permute-start.47
  256.2 3.9 %collective-permute-start.48 = (bf16[96,128]{1,0:T(8,128)(2,1)S(1)}, bf16[96,128]{1,0:T(8,128)(2,1)S(1)}, u32[]{:S(2)}, u32[]{:S(2)}) collective-permute-start(bf16[96,128]{1,0:T(8,128)(2,1)S(1)} %get-tuple-element.230), channel_id=1, source_target_pairs={{0,8},{4,12},{8,0},{12,4},{16,24},{20,28},{24,16},{28,20},{1,9},{5... | collective-permute-start | bytes 73736 | tf_op jit(solution)/shard_map/ppermute | solution.py:20
  257.2 3.8 %collective-permute-start.49 = (bf16[96,128]{1,0:T(8,128)(2,1)S(1)}, bf16[96,128]{1,0:T(8,128)(2,1)S(1)}, u32[]{:S(2)}, u32[]{:S(2)}) collective-permute-start(bf16[96,128]{1,0:T(8,128)(2,1)S(1)} %get-tuple-element.231), channel_id=1, source_target_pairs={{0,16},{4,20},{8,24},{12,28},{16,0},{20,4},{24,8},{28,12},{1,17},{... | collective-permute-start | bytes 73736 | tf_op jit(solution)/shard_map/ppermute | solution.py:20
  257.9 4.7 %collective-permute-start.50 = (bf16[96,128]{1,0:T(8,128)(2,1)S(1)}, bf16[96,128]{1,0:T(8,128)(2,1)S(1)}, u32[]{:S(2)}, u32[]{:S(2)}) collective-permute-start(bf16[96,128]{1,0:T(8,128)(2,1)S(1)} %get-tuple-element.232), channel_id=1, source_target_pairs={{0,24},{4,28},{8,16},{12,20},{16,8},{20,12},{24,0},{28,4},{1,25},{... | collective-permute-start | bytes 73736 | tf_op jit(solution)/shard_map/ppermute | solution.py:20
  263.0 7.8 %collective-permute-start.51 = (bf16[24,2432]{1,0:T(8,128)(2,1)S(1)}, bf16[24,2432]{1,0:T(8,128)(2,1)S(1)}, u32[]{:S(2)}, u32[]{:S(2)}) collective-permute-start(bf16[24,2432]{1,0:T(8,128)(2,1)S(1)} %get-tuple-element.253), channel_id=1, source_target_pairs={{0,1},{1,0},{2,3},{3,2},{4,5},{5,4},{6,7},{7,6},{8,9},{9,8},{10,11... | collective-permute-start | bytes 350216 | tf_op jit(solution)/shard_map/ppermute | solution.py:24
  264.3 14.8 %collective-permute-start.52 = (bf16[24,2432]{1,0:T(8,128)(2,1)S(1)}, bf16[24,2432]{1,0:T(8,128)(2,1)S(1)}, u32[]{:S(2)}, u32[]{:S(2)}) collective-permute-start(bf16[24,2432]{1,0:T(8,128)(2,1)S(1)} %get-tuple-element.287), channel_id=1, source_target_pairs={{0,2},{1,3},{2,0},{3,1},{4,6},{5,7},{6,4},{7,5},{8,10},{9,11},{10,... | collective-permute-start | bytes 350216 | tf_op jit(solution)/shard_map/ppermute | solution.py:24
  266.1 12.9 %collective-permute-start.53 = (bf16[24,2432]{1,0:T(8,128)(2,1)S(1)}, bf16[24,2432]{1,0:T(8,128)(2,1)S(1)}, u32[]{:S(2)}, u32[]{:S(2)}) collective-permute-start(bf16[24,2432]{1,0:T(8,128)(2,1)S(1)} %get-tuple-element.288), channel_id=1, source_target_pairs={{0,3},{1,2},{2,1},{3,0},{4,7},{5,6},{6,5},{7,4},{8,11},{9,10},{10,... | collective-permute-start | bytes 350216 | tf_op jit(solution)/shard_map/ppermute | solution.py:24
  268.4 12.2 %collective-permute-start.54 = (bf16[24,3840]{1,0:T(8,128)(2,1)S(1)}, bf16[24,3840]{1,0:T(8,128)(2,1)S(1)}, u32[]{:S(2)}, u32[]{:S(2)}) collective-permute-start(bf16[24,3840]{1,0:T(8,128)(2,1)S(1)} %get-tuple-element.244), channel_id=1, source_target_pairs={{0,3},{1,2},{2,1},{3,0},{4,7},{5,6},{6,5},{7,4},{8,11},{9,10},{10,... | collective-permute-start | bytes 552968 | tf_op jit(solution)/shard_map/ppermute | solution.py:24
  (5 other events, 6.5 us)

commit v4 on v3

--- a/solution.py
+++ b/solution.py
@@ -409,18 +409,18 @@
 
 def return_kernel(
     plan, count, plan_down, count_down, me_ref, y_hbm, cot_ref, vec_ref, ht_ref, mixed_hbm,
-    rise_ref, act_ref, *rest
+    rise_ref, act_hbm, *rest
 ):
     pieces = rest[:count]
     down_pieces = rest[count : count + count_down]
     (
         grad_ref, out_ref, keep_ref, send_ref, sums_ref,
-        acc_ref, du_ref, w_ref, wd_ref, part_ref, out_grad_ref, y_ref, mixed_ref,
+        act_ref, du_ref, w_ref, wd_ref, part_ref, out_grad_ref, y_ref, mixed_ref,
         sems, down_sems, late_sems,
     ) = rest[count + count_down :]
     step = pl.program_id(0)
     width = cot_ref.shape[1]
-    chunk = act_ref.shape[1]
+    chunk = rise_ref.shape[1]
     block = width // BLOCKS
     copies = [
         pltpu.make_async_copy(*pair)
@@ -428,6 +428,7 @@
     ]
     copies.append(pltpu.make_async_copy(y_hbm, y_ref, late_sems.at[0]))
     copies.append(pltpu.make_async_copy(mixed_hbm, mixed_ref, late_sems.at[1]))
+    copies.append(pltpu.make_async_copy(act_hbm, act_ref, late_sems.at[2]))
 
     @pl.when(step == 0)
     def _():
@@ -436,7 +437,6 @@
         )
         for copy in copies:
             copy.start()
-        acc_ref[...] = jnp.zeros_like(acc_ref)
         out_grad_ref[...] = jnp.zeros_like(out_grad_ref)
         sums_ref[...] = jnp.zeros_like(sums_ref)
         for copy in down_copies:
@@ -450,7 +450,6 @@
             dot_nt(cot_ref[...], down) * rise_ref[...].astype(jnp.float32)
         ).astype(jnp.bfloat16)
         du_ref[:, pl.ds(start, chunk)] = grad_upper
-        acc_ref[...] += dot_nn(act_ref[...], down)
         part_ref[...] = dot_nn(ht_ref[...], grad_upper)
         split_blocks(part_ref, me_ref[0], block, keep_ref, send_ref)
 
@@ -458,11 +457,12 @@
     def _():
         for copy in copies:
             copy.wait()
-        out_ref[...] = (y_ref[...] + acc_ref[...]).astype(jnp.bfloat16)
         size = mixed_ref.shape[2]
 
         def body(place, carry):
             rows = pl.ds(pl.multiple_of(place * size, size), size)
+            total = y_ref[rows, :] + dot_nn(act_ref[rows, :], wd_ref[...])
+            out_ref[rows, :] = total.astype(jnp.bfloat16)
             back = dot_nt(du_ref[rows, :], w_ref[...])
             normed, factor = norm_parts(y_ref[rows, :])
             through, gain_grad, bias_grad = norm_back(back, normed, factor, vec_ref[2:3])
@@ -498,7 +498,7 @@
         + any_specs([mixed])
         + [
             pl.BlockSpec((count, chunk), lambda j: (0, jnp.minimum(j, 3))),
-            pl.BlockSpec((count, chunk), lambda j: (0, jnp.minimum(j, 3))),
+            pl.BlockSpec(memory_space=pl.ANY),
         ]
         + any_specs(pieces)
         + any_specs(down_pieces),
@@ -507,7 +507,7 @@
         + [whole_spec((8, width))],
         out_shape=shapes,
         scratch_shapes=[
-            pltpu.VMEM((count, width), jnp.float32),
+            pltpu.VMEM((count, hidden), jnp.bfloat16),
             pltpu.VMEM((count, hidden), jnp.bfloat16),
             pltpu.VMEM((width, hidden), jnp.bfloat16),
             pltpu.VMEM((hidden, width), jnp.bfloat16),
@@ -517,7 +517,7 @@
             pltpu.VMEM(mixed.shape, jnp.bfloat16),
             pltpu.SemaphoreType.DMA((BLOCKS,)),
             pltpu.SemaphoreType.DMA((BLOCKS,)),
-            pltpu.SemaphoreType.DMA((2,)),
+            pltpu.SemaphoreType.DMA((3,)),
         ],
         compiler_params=kernel_params(60),
         cost_estimate=pl.CostEstimate(
@@ -796,12 +796,12 @@
         )
         late_parts = scatter_core(*late)
         other = swap(counts, CORE)
-        *late_parts, other = together([*late_parts, other])
+        *late_parts, other, piece = together([*late_parts, other, piece])
+        up_inner.append(swap_inner(piece, inner - 1, inner))
         counts = double_tables(counts, other, CORE)
         late_received = scatter_sides(late_parts)
-        *values, piece = together([*early_received, *late_received, piece])
+        values = together([*early_received, *late_received])
         early_received, late_received = values[:3], values[3:]
-        up_inner.append(swap_inner(piece, inner - 1, inner))
         early_mine = add(early_parts[0], *early_received)
         late_mine = add(late_parts[0], *late_received)
         both = jnp.concatenate([early_mine, late_mine], axis=1)

time: 287 us -> 282 us (0.983)
  transfers between devices with their start and end apart: 55 -> 55, of which waited for: 18 -> 17; matrix products, arithmetic and copies ran while one was open for 5% -> 5% of each run, Pallas kernels for 46% -> 46%
where the time goes in v4:
time: 282 us; the launch traced here: 278 us
  Pallas kernels  129 us (46%)
  starting transfers between devices  68.4 us (24%)
  waiting for transfers between devices  52.6 us (19%)
  other arithmetic  15 us (5%)
  local copies, waits for them, and re-layouts  12.1 us (4%)
    ppermute x21, starting transfers between devices, swap_inner(): return lax.ppermute(value, 'fsdp', [(i, i ^ bit) for i in range(size)])  38.1 us
    pallas_call x1, Pallas kernels, feed_return(): pl.pallas_call(functools.partial(return_kernel, plan, len(pieces), plan_d...  34.7 us
    ppermute x21, waiting for transfers between devices, swap_inner(): return lax.ppermute(value, 'fsdp', [(i, i ^ bit) for i in range(size)])  32.5 us
    ppermute x34, starting transfers between devices, swap(): return lax.ppermute(value, 'dp', [(i, i ^ bit) for i in range(BLOCKS)])  30.3 us
    pallas_call x1, Pallas kernels, backward(): pl.pallas_call(functools.partial(backward_kernel, plan, len(pieces), grou...  27.6 us
    pallas_call x1, Pallas kernels, feed_forward(): pl.pallas_call(functools.partial(forward_kernel, plan, len(pieces)), grid...  27 us
    pallas_call x1, Pallas kernels, attend(): pl.pallas_call(functools.partial(attend_kernel, plan, len(pieces)), grid=...  24.7 us
    ppermute x34, waiting for transfers between devices, swap(): return lax.ppermute(value, 'dp', [(i, i ^ bit) for i in range(BLOCKS)])  20.1 us
  transfers between devices with their start and end apart: 55, of which 17 were waited for; matrix products, arithmetic and copies ran while one was open for 5% of the time, Pallas kernels for 46%

profile of v4, /device:TPU:0, one launch (start us, length us, event | category | flops | bytes accessed | tf_op | source)
XLA Modules:
  0.0 278.2 jit_solution(2310785906848665759)
XLA Ops:
  1.5 0.9 fusion.13
  2.4 3.1 %collective-permute-start.2 = (bf16[24,2432]{1,0:T(8,128)(2,1)S(1)}, bf16[24,2432]{1,0:T(8,128)(2,1)S(1)}, u32[]{:S(2)}, u32[]{:S(2)}) collective-permute-start(bf16[24,2432]{1,0:T(8,128)(2,1)S(1)} %fusion.13), channel_id=1, source_target_pairs={{0,1},{1,0},{2,3},{3,2},{4,5},{5,4},{6,7},{7,6},{8,9},{9,8},{10,11... | collective-permute-start | bytes 350216 | tf_op jit(solution)/shard_map/ppermute | solution.py:24
  5.5 2.6 collective-permute-start.1
  8.1 0.9 pad_maximum_fusion.6
  9.0 3.0 %shard_map.203 = s32[8,64,256]{2,1,0:T(8,128)} custom-call(s32[8,1024]{1,0:T(8,128)} %bitcast.85), custom_call_target="tpu_custom_call" | custom-call | flops 3000000000 | bytes 1000000 | tf_op jit(solution)/shard_map/pallas_call | solution.py:187
  12.6 1.3 copy.32
  14.0 3.3 %collective-permute-done.1 = bf16[24,2432]{1,0:T(8,128)(2,1)S(1)} collective-permute-done((bf16[24,2432]{1,0:T(8,128)(2,1)S(1)}, bf16[24,2432]{1,0:T(8,128)(2,1)S(1)}, u32[]{:S(2)}, u32[]{:S(2)}) %collective-permute-start.1) | collective-permute-done | bytes 116768 | tf_op jit(solution)/shard_map/ppermute | solution.py:24
  17.5 2.5 collective-permute-start.5
  21.0 2.5 collective-permute-start.8
  24.3 4.8 %collective-permute-done.8 = bf16[24,3840]{1,0:T(8,128)(2,1)S(1)} collective-permute-done((bf16[24,3840]{1,0:T(8,128)(2,1)S(1)}, bf16[24,3840]{1,0:T(8,128)(2,1)S(1)}, u32[]{:S(2)}, u32[]{:S(2)}) %collective-permute-start.8) | collective-permute-done | bytes 184352 | tf_op jit(solution)/shard_map/ppermute | solution.py:24
  29.1 6.5 %collective-permute-start.6 = (bf16[24,3840]{1,0:T(8,128)(2,1)S(1)}, bf16[24,3840]{1,0:T(8,128)(2,1)S(1)}, u32[]{:S(2)}, u32[]{:S(2)}) collective-permute-start(bf16[24,3840]{1,0:T(8,128)(2,1)S(1)} %pad_maximum_fusion.6), channel_id=1, source_target_pairs={{0,1},{1,0},{2,3},{3,2},{4,5},{5,4},{6,7},{7,6},{8,9},{9,8},{10,11... | collective-permute-start | bytes 552968 | tf_op jit(solution)/shard_map/ppermute | solution.py:24
  35.7 2.3 collective-permute-done.7
  38.0 3.4 %collective-permute-done.6 = bf16[24,3840]{1,0:T(8,128)(2,1)S(1)} collective-permute-done((bf16[24,3840]{1,0:T(8,128)(2,1)S(1)}, bf16[24,3840]{1,0:T(8,128)(2,1)S(1)}, u32[]{:S(2)}, u32[]{:S(2)}) %collective-permute-start.6) | collective-permute-done | bytes 184352 | tf_op jit(solution)/shard_map/ppermute | solution.py:24
  43.0 3.0 %collective-permute-done.9 = s32[4,16384]{1,0:T(4,128)S(1)} collective-permute-done((s32[4,16384]{1,0:T(4,128)S(1)}, s32[4,16384]{1,0:T(4,128)S(1)}, u32[]{:S(2)}, u32[]{:S(2)}) %collective-permute-start.9) | collective-permute-done | bytes 262176 | tf_op jit(solution)/shard_map/ppermute | solution.py:20
  46.1 1.3 copy-done.4
  47.4 2.4 collective-permute-start.13
  50.8 1.3 collective-permute-start.15
  52.2 1.6 collective-permute-start.14
  53.8 24.7 %shard_map.204 = (bf16[2,512,2304]{2,1,0:T(8,128)(2,1)}, bf16[2,12,512,512]{3,2,1,0:T(8,128)(2,1)}, f32[2,12,1,512]{3,2,1,0:T(1,128)}, bf16[2,768,512]{2,1,0:T(8...) custom-call(s32[1]{0:T(128)} %bitcast.me_ref, ...), custom_call_target="tpu_custom_call" | custom-call | flops 1000000000 | bytes 1000000 | tf_op jit(solution)/shard_map/pallas_call | solution.py:292
  78.5 4.1 %collective-permute-done.12 = bf16[96,3840]{1,0:T(8,128)(2,1)S(1)} collective-permute-done((bf16[96,3840]{1,0:T(8,128)(2,1)S(1)}, bf16[96,3840]{1,0:T(8,128)(2,1)S(1)}, u32[]{:S(2)}, u32[]{:S(2)}) %collective-permute-start.12) | collective-permute-done | bytes 737312 | tf_op jit(solution)/shard_map/ppermute | solution.py:20
  82.7 2.4 collective-permute-start.16
  86.1 4.4 %collective-permute-done.16 = bf16[96,768]{1,0:T(8,128)(2,1)S(1)} collective-permute-done((bf16[96,768]{1,0:T(8,128)(2,1)}, bf16[96,768]{1,0:T(8,128)(2,1)S(1)}, u32[]{:S(2)}, u32[]{:S(2)}) %collective-permute-start.16) | collective-permute-done | bytes 147488 | tf_op jit(solution)/shard_map/ppermute | solution.py:24
  90.5 1.1 broadcast_select_fusion.30
  91.7 1.6 copy-done.1
  93.2 1.1 collective-permute-start.20
  94.3 1.9 collective-permute-start.19
  96.8 1.6 collective-permute-start.21
  98.4 27.0 %shard_map.205 = (f32[1024,768]{1,0:T(8,128)}, bf16[768,1024]{1,0:T(8,128)(2,1)}, bf16[4,384,768]{2,1,0:T(8,128)(2,1)}, bf16[4,384,768]{2,1,0:T(8,128)(2,1)}, bf...) custom-call(s32[1]{0:T(128)} %bitcast.me_ref, bf16[1024,768]{1,0:T(8,128)(2,1)} %bitcast.59, ...), custom_call_target="tpu_custom_call" | custom-call | flops 1000000000 | bytes 1000000 | tf_op jit(solution)/shard_map/pallas_call | solution.py:379
  125.8 2.1 copy-done.13
  128.1 5.7 %collective-permute-done.22 = bf16[4,384,768]{2,1,0:T(8,128)(2,1)S(1)} collective-permute-done((bf16[4,384,768]{2,1,0:T(8,128)(2,1)S(1)}, bf16[4,384,768]{2,1,0:T(8,128)(2,1)S(1)}, u32[]{:S(2)}, u32[]{:S(2)}) %collective-permute-start.22) | collective-permute-done | bytes 2359328 | tf_op jit(solution)/shard_map/ppermute | solution.py:20
  133.7 1.6 fusion.7
  135.9 1.4 collective-permute-start.25
  137.3 1.6 collective-permute-start.26
  139.1 1.4 copy-done.6
  140.5 34.7 %shard_map.206 = (f32[1024,768]{1,0:T(8,128)}, bf16[1024,768]{1,0:T(8,128)(2,1)}, bf16[4,96,3840]{2,1,0:T(8,128)(2,1)}, bf16[4,96,3840]{2,1,0:T(8,128)(2,1)}, f32[8,768]{1,0:T(8,128)}) custom-call(s32[1]{0:T(128)} %bitcast.me_ref, f32[1024,768]{1,0:T(8,128)} %get-tuple-element.163.y_hbm, bf16[1024,768]{1,0:T(8,128)(2,1)} %bitcast.63, ...), custom_call_target="tpu_custom_call" | custom-call | flops 1000000000 | bytes 1000000 | tf_op jit(solution)/shard_map/pallas_call | solution.py:490
  175.4 2.4 collective-permute-start.31
  177.8 1.1 collective-permute-start.30
  178.9 0.9 collective-permute-start.29
  179.8 1.7 add_convert_fusion.5
  182.3 3.3 %collective-permute-done.30 = s32[1,16384]{1,0:T(1,128)S(1)} collective-permute-done((s32[1,16384]{1,0:T(1,128)S(1)}, s32[1,16384]{1,0:T(1,128)S(1)}, u32[]{:S(2)}, u32[]{:S(2)}) %collective-permute-start.30) | collective-permute-done | bytes 65568 | tf_op jit(solution)/shard_map/ppermute | solution.py:24
  186.4 3.2 %collective-permute-start.36 = (bf16[96,768]{1,0:T(8,128)(2,1)}, bf16[96,768]{1,0:T(8,128)(2,1)S(1)}, u32[]{:S(2)}, u32[]{:S(2)}) collective-permute-start(bf16[96,768]{1,0:T(8,128)(2,1)} %get-tuple-element.280), channel_id=1, source_target_pairs={{0,2},{1,3},{2,0},{3,1},{4,6},{5,7},{6,4},{7,5},{8,10},{9,11},{10,... | collective-permute-start | bytes 442376 | tf_op jit(solution)/shard_map/ppermute | solution.py:24
  189.6 1.2 collective-permute-start.32
  191.5 1.6 collective-permute-start.34
  193.2 27.6 %shard_map.207 = (bf16[2,512,2304]{2,1,0:T(8,128)(2,1)}, bf16[4,96,2304]{2,1,0:T(8,128)(2,1)}, bf16[4,96,2304]{2,1,0:T(8,128)(2,1)}) custom-call(s32[1]{0:T(128)} %bitcast.me_ref, f32[2,512,768]{2,1,0:T(8,128)} %bitcast.60, bf16[2,512,2304]{2,1,0:T(8,128)(2,1)} %get-tuple-element.188.q_ref.k_ref.v_ref, ...), custom_call_target="tpu_custom_call" | custom-call | flops 1000000000 | bytes 1000000 | tf_op jit(solution)/shard_map/pallas_call | solution.py:645
  220.9 2.9 %collective-permute-done.34 = bf16[96,3840]{1,0:T(8,128)(2,1)S(1)} collective-permute-done((bf16[96,3840]{1,0:T(8,128)(2,1)S(1)}, bf16[96,3840]{1,0:T(8,128)(2,1)S(1)}, u32[]{:S(2)}, u32[]{:S(2)}) %collective-permute-start.34) | collective-permute-done | bytes 737312 | tf_op jit(solution)/shard_map/ppermute | solution.py:20
  224.6 1.2 collective-permute-start.38
  226.2 3.5 %collective-permute-done.37 = bf16[4,96,2304]{2,1,0:T(8,128)(2,1)S(1)} collective-permute-done((bf16[4,96,2304]{2,1,0:T(8,128)(2,1)}, bf16[4,96,2304]{2,1,0:T(8,128)(2,1)S(1)}, u32[]{:S(2)}, u32[]{:S(2)}) %collective-permute-start.37) | collective-permute-done | bytes 1769504 | tf_op jit(solution)/shard_map/ppermute | solution.py:20
  230.2 1.7 collective-permute-done.38
  232.1 1.4 collective-permute-start.42
  233.5 1.8 collective-permute-start.41
  235.9 1.4 collective-permute-start.44
  237.3 2.0 collective-permute-start.45
  239.5 11.6 %shard_map.208 = (bf16[2,512,768]{2,1,0:T(8,128)(2,1)}, bf16[4,96,128]{2,1,0:T(8,128)(2,1)}, bf16[4,96,128]{2,1,0:T(8,128)(2,1)}) custom-call(s32[1]{0:T(128)} %bitcast.me_ref, f32[2,512,768]{2,1,0:T(8,128)} %bitcast.61, bf16[2,512,768]{2,1,0:T(8,128)(2,1)} %x_ref.3, bf16[2,512,2304]{2,1,0:T(8,128)(2,1)} %get-tuple-element.216.dqkv_ref, ...), custom_call_target="tpu_custom_call" | custom-call | flops 1000000000 | bytes 1000000 | tf_op jit(solution)/shard_map/pallas_call | solution.py:701
  251.7 0.8 convert_add_fusion.1
  252.7 0.8 fusion.21
  253.6 1.1 collective-permute-start.48
  255.3 1.8 collective-permute-start.50
  257.2 2.2 collective-permute-start.54
  260.4 1.2 collective-permute-start.51
  261.7 1.8 collective-permute-start.52
  263.5 1.4 collective-permute-start.53
  264.9 0.9 pad_add_fusion
  265.8 3.4 %collective-permute-done.51 = bf16[24,2432]{1,0:T(8,128)(2,1)S(1)} collective-permute-done((bf16[24,2432]{1,0:T(8,128)(2,1)S(1)}, bf16[24,2432]{1,0:T(8,128)(2,1)S(1)}, u32[]{:S(2)}, u32[]{:S(2)}) %collective-permute-start.51) | collective-permute-done | bytes 116768 | tf_op jit(solution)/shard_map/ppermute | solution.py:24
  269.2 5.7 %collective-permute-done.52 = bf16[24,2432]{1,0:T(8,128)(2,1)S(1)} collective-permute-done((bf16[24,2432]{1,0:T(8,128)(2,1)S(1)}, bf16[24,2432]{1,0:T(8,128)(2,1)S(1)}, u32[]{:S(2)}, u32[]{:S(2)}) %collective-permute-start.52) | collective-permute-done | bytes 116768 | tf_op jit(solution)/shard_map/ppermute | solution.py:24
  (128 shorter events, 19.8 us)
Async XLA Ops:
  2.4 11.6 %collective-permute-start.2 = (bf16[24,2432]{1,0:T(8,128)(2,1)S(1)}, bf16[24,2432]{1,0:T(8,128)(2,1)S(1)}, u32[]{:S(2)}, u32[]{:S(2)}) collective-permute-start(bf16[24,2432]{1,0:T(8,128)(2,1)S(1)} %fusion.13), channel_id=1, source_target_pairs={{0,1},{1,0},{2,3},{3,2},{4,5},{5,4},{6,7},{7,6},{8,9},{9,8},{10,11... | collective-permute-start | bytes 350216 | tf_op jit(solution)/shard_map/ppermute | solution.py:24
  5.5 11.9 %collective-permute-start.1 = (bf16[24,2432]{1,0:T(8,128)(2,1)S(1)}, bf16[24,2432]{1,0:T(8,128)(2,1)S(1)}, u32[]{:S(2)}, u32[]{:S(2)}) collective-permute-start(bf16[24,2432]{1,0:T(8,128)(2,1)S(1)} %fusion.13), channel_id=1, source_target_pairs={{0,2},{1,3},{2,0},{3,1},{4,6},{5,7},{6,4},{7,5},{8,10},{9,11},{10,... | collective-permute-start | bytes 350216 | tf_op jit(solution)/shard_map/ppermute | solution.py:24
  8.0 9.3 %collective-permute-start = (bf16[24,2432]{1,0:T(8,128)(2,1)S(1)}, bf16[24,2432]{1,0:T(8,128)(2,1)S(1)}, u32[]{:S(2)}, u32[]{:S(2)}) collective-permute-start(bf16[24,2432]{1,0:T(8,128)(2,1)S(1)} %fusion.13), channel_id=1, source_target_pairs={{0,3},{1,2},{2,1},{3,0},{4,7},{5,6},{6,5},{7,4},{8,11},{9,10},{10,... | collective-permute-start | bytes 350216 | tf_op jit(solution)/shard_map/ppermute | solution.py:24
  9.0 3.0 %copy-start.12 = (s32[2,512]{1,0:T(2,128)S(1)}, s32[2,512]{1,0:T(2,128)}, u32[]{:S(2)}) copy-start(s32[2,512]{1,0:T(2,128)} %param.13) | copy-start | bytes 12292
  9.0 8.3 %copy-start.9 = (bf16[24,2304]{1,0:T(8,128)(2,1)S(1)}, bf16[24,2304]{1,0:T(8,128)(2,1)}, u32[]{:S(2)}) copy-start(bf16[24,2304]{1,0:T(8,128)(2,1)} %param.16) | copy-start | bytes 331780
  17.5 24.0 %collective-permute-start.5 = (bf16[96,2432]{1,0:T(8,128)(2,1)S(1)}, bf16[96,2432]{1,0:T(8,128)(2,1)S(1)}, u32[]{:S(2)}, u32[]{:S(2)}) collective-permute-start(bf16[96,2432]{1,0:T(8,128)(2,1)S(1)} %pad_maximum_fusion.5), channel_id=1, source_target_pairs={{0,24},{4,28},{8,16},{12,20},{16,8},{20,12},{24,0},{28,4},{1,25},{... | collective-permute-start | bytes 1400840 | tf_op jit(solution)/shard_map/ppermute | solution.py:20
  20.0 21.5 %collective-permute-start.4 = (bf16[96,2432]{1,0:T(8,128)(2,1)S(1)}, bf16[96,2432]{1,0:T(8,128)(2,1)S(1)}, u32[]{:S(2)}, u32[]{:S(2)}) collective-permute-start(bf16[96,2432]{1,0:T(8,128)(2,1)S(1)} %pad_maximum_fusion.5), channel_id=1, source_target_pairs={{0,16},{4,20},{8,24},{12,28},{16,0},{20,4},{24,8},{28,12},{1,17},{... | collective-permute-start | bytes 1400840 | tf_op jit(solution)/shard_map/ppermute | solution.py:20
  20.5 21.0 %collective-permute-start.3 = (bf16[96,2432]{1,0:T(8,128)(2,1)S(1)}, bf16[96,2432]{1,0:T(8,128)(2,1)S(1)}, u32[]{:S(2)}, u32[]{:S(2)}) collective-permute-start(bf16[96,2432]{1,0:T(8,128)(2,1)S(1)} %pad_maximum_fusion.5), channel_id=1, source_target_pairs={{0,8},{4,12},{8,0},{12,4},{16,24},{20,28},{24,16},{28,20},{1,9},{5... | collective-permute-start | bytes 1400840 | tf_op jit(solution)/shard_map/ppermute | solution.py:20
  21.0 8.1 %collective-permute-start.8 = (bf16[24,3840]{1,0:T(8,128)(2,1)S(1)}, bf16[24,3840]{1,0:T(8,128)(2,1)S(1)}, u32[]{:S(2)}, u32[]{:S(2)}) collective-permute-start(bf16[24,3840]{1,0:T(8,128)(2,1)S(1)} %pad_maximum_fusion.6), channel_id=1, source_target_pairs={{0,3},{1,2},{2,1},{3,0},{4,7},{5,6},{6,5},{7,4},{8,11},{9,10},{10,... | collective-permute-start | bytes 552968 | tf_op jit(solution)/shard_map/ppermute | solution.py:24
  23.5 14.5 %collective-permute-start.7 = (bf16[24,3840]{1,0:T(8,128)(2,1)S(1)}, bf16[24,3840]{1,0:T(8,128)(2,1)S(1)}, u32[]{:S(2)}, u32[]{:S(2)}) collective-permute-start(bf16[24,3840]{1,0:T(8,128)(2,1)S(1)} %pad_maximum_fusion.6), channel_id=1, source_target_pairs={{0,2},{1,3},{2,0},{3,1},{4,6},{5,7},{6,4},{7,5},{8,10},{9,11},{10,... | collective-permute-start | bytes 552968 | tf_op jit(solution)/shard_map/ppermute | solution.py:24
  29.1 12.3 %collective-permute-start.6 = (bf16[24,3840]{1,0:T(8,128)(2,1)S(1)}, bf16[24,3840]{1,0:T(8,128)(2,1)S(1)}, u32[]{:S(2)}, u32[]{:S(2)}) collective-permute-start(bf16[24,3840]{1,0:T(8,128)(2,1)S(1)} %pad_maximum_fusion.6), channel_id=1, source_target_pairs={{0,1},{1,0},{2,3},{3,2},{4,5},{5,4},{6,7},{7,6},{8,9},{9,8},{10,11... | collective-permute-start | bytes 552968 | tf_op jit(solution)/shard_map/ppermute | solution.py:24
  41.8 4.3 %collective-permute-start.10 = (bf16[4,96,2432]{2,1,0:T(8,128)(2,1)S(1)}, bf16[4,96,2432]{2,1,0:T(8,128)(2,1)S(1)}, u32[]{:S(2)}, u32[]{:S(2)}) collective-permute-start(bf16[4,96,2432]{2,1,0:T(8,128)(2,1)S(1)} %pad_maximum_fusion.2.rest_0_), channel_id=1, source_target_pairs={{0,4},{4,0},{8,12},{12,8},{16,20},{20,16},{24,28},{28,24},{1,5},{5... | collective-permute-start | bytes 5603336 | tf_op jit(solution)/shard_map/ppermute | solution.py:20
  41.9 4.1 %collective-permute-start.9 = (s32[4,16384]{1,0:T(4,128)S(1)}, s32[4,16384]{1,0:T(4,128)S(1)}, u32[]{:S(2)}, u32[]{:S(2)}) collective-permute-start(s32[4,16384]{1,0:T(4,128)S(1)} %slice_select_fusion), channel_id=1, source_target_pairs={{0,4},{4,0},{8,12},{12,8},{16,20},{20,16},{24,28},{28,24},{1,5},{5... | collective-permute-start | bytes 786440 | tf_op jit(solution)/shard_map/ppermute | solution.py:20
  46.1 3.7 %copy-start.10 = (s32[4,16384]{1,0:T(4,128)}, s32[4,16384]{1,0:T(4,128)S(1)}, u32[]{:S(2)}) copy-start(s32[4,16384]{1,0:T(4,128)S(1)} %collective-permute-done.9) | copy-start | bytes 786436
  47.4 31.1 %collective-permute-start.13 = (bf16[96,3840]{1,0:T(8,128)(2,1)S(1)}, bf16[96,3840]{1,0:T(8,128)(2,1)S(1)}, u32[]{:S(2)}, u32[]{:S(2)}) collective-permute-start(bf16[96,3840]{1,0:T(8,128)(2,1)S(1)} %pad_maximum_fusion.3), channel_id=1, source_target_pairs={{0,24},{4,28},{8,16},{12,20},{16,8},{20,12},{24,0},{28,4},{1,25},{... | collective-permute-start | bytes 2211848 | tf_op jit(solution)/shard_map/ppermute | solution.py:20
  49.8 32.8 %collective-permute-start.12 = (bf16[96,3840]{1,0:T(8,128)(2,1)S(1)}, bf16[96,3840]{1,0:T(8,128)(2,1)S(1)}, u32[]{:S(2)}, u32[]{:S(2)}) collective-permute-start(bf16[96,3840]{1,0:T(8,128)(2,1)S(1)} %pad_maximum_fusion.3), channel_id=1, source_target_pairs={{0,16},{4,20},{8,24},{12,28},{16,0},{20,4},{24,8},{28,12},{1,17},{... | collective-permute-start | bytes 2211848 | tf_op jit(solution)/shard_map/ppermute | solution.py:20
  50.3 32.4 %collective-permute-start.11 = (bf16[96,3840]{1,0:T(8,128)(2,1)S(1)}, bf16[96,3840]{1,0:T(8,128)(2,1)S(1)}, u32[]{:S(2)}, u32[]{:S(2)}) collective-permute-start(bf16[96,3840]{1,0:T(8,128)(2,1)S(1)} %pad_maximum_fusion.3), channel_id=1, source_target_pairs={{0,8},{4,12},{8,0},{12,4},{16,24},{20,28},{24,16},{28,20},{1,9},{5... | collective-permute-start | bytes 2211848 | tf_op jit(solution)/shard_map/ppermute | solution.py:20
  50.8 27.6 %collective-permute-start.15 = (bf16[96,768]{1,0:T(8,128)(2,1)}, bf16[96,768]{1,0:T(8,128)(2,1)}, u32[]{:S(2)}, u32[]{:S(2)}) collective-permute-start(bf16[96,768]{1,0:T(8,128)(2,1)} %param.19), channel_id=1, source_target_pairs={{0,2},{1,3},{2,0},{3,1},{4,6},{5,7},{6,4},{7,5},{8,10},{9,11},{10,... | collective-permute-start | bytes 442376 | tf_op jit(solution)/shard_map/ppermute | solution.py:24
  52.2 26.3 %collective-permute-start.14 = (bf16[96,768]{1,0:T(8,128)(2,1)}, bf16[96,768]{1,0:T(8,128)(2,1)}, u32[]{:S(2)}, u32[]{:S(2)}) collective-permute-start(bf16[96,768]{1,0:T(8,128)(2,1)} %param.19), channel_id=1, source_target_pairs={{0,1},{1,0},{2,3},{3,2},{4,5},{5,4},{6,7},{7,6},{8,9},{9,8},{10,11... | collective-permute-start | bytes 442376 | tf_op jit(solution)/shard_map/ppermute | solution.py:24
  82.7 7.8 %collective-permute-start.16 = (bf16[96,768]{1,0:T(8,128)(2,1)}, bf16[96,768]{1,0:T(8,128)(2,1)S(1)}, u32[]{:S(2)}, u32[]{:S(2)}) collective-permute-start(bf16[96,768]{1,0:T(8,128)(2,1)} %param.19), channel_id=1, source_target_pairs={{0,3},{1,2},{2,1},{3,0},{4,7},{5,6},{6,5},{7,4},{8,11},{9,10},{10,... | collective-permute-start | bytes 442376 | tf_op jit(solution)/shard_map/ppermute | solution.py:24
  85.5 6.2 %copy-start = (bf16[4,96,3840]{2,1,0:T(8,128)(2,1)}, bf16[4,96,3840]{2,1,0:T(8,128)(2,1)S(1)}, u32[]{:S(2)}) copy-start(bf16[4,96,3840]{2,1,0:T(8,128)(2,1)S(1)} %pad_maximum_fusion.rest_0_) | copy-start | bytes 8847364
  85.5 6.2 %collective-permute-start.17 = (bf16[4,96,3840]{2,1,0:T(8,128)(2,1)S(1)}, bf16[4,96,3840]{2,1,0:T(8,128)(2,1)S(1)}, u32[]{:S(2)}, u32[]{:S(2)}) collective-permute-start(bf16[4,96,3840]{2,1,0:T(8,128)(2,1)S(1)} %pad_maximum_fusion.rest_0_), channel_id=1, source_target_pairs={{0,4},{4,0},{8,12},{12,8},{16,20},{20,16},{24,28},{28,24},{1,5},{5... | collective-permute-start | bytes 8847368 | tf_op jit(solution)/shard_map/ppermute | solution.py:20
  93.2 32.2 %collective-permute-start.20 = (bf16[384,768]{1,0:T(8,128)(2,1)S(1)}, bf16[384,768]{1,0:T(8,128)(2,1)S(1)}, u32[]{:S(2)}, u32[]{:S(2)}) collective-permute-start(bf16[384,768]{1,0:T(8,128)(2,1)S(1)} %pad_maximum_fusion.4), channel_id=1, source_target_pairs={{0,24},{4,28},{8,16},{12,20},{16,8},{20,12},{24,0},{28,4},{1,25},{... | collective-permute-start | bytes 1769480 | tf_op jit(solution)/shard_map/ppermute | solution.py:20
  94.3 31.1 %collective-permute-start.19 = (bf16[384,768]{1,0:T(8,128)(2,1)S(1)}, bf16[384,768]{1,0:T(8,128)(2,1)S(1)}, u32[]{:S(2)}, u32[]{:S(2)}) collective-permute-start(bf16[384,768]{1,0:T(8,128)(2,1)S(1)} %pad_maximum_fusion.4), channel_id=1, source_target_pairs={{0,16},{4,20},{8,24},{12,28},{16,0},{20,4},{24,8},{28,12},{1,17},{... | collective-permute-start | bytes 1769480 | tf_op jit(solution)/shard_map/ppermute | solution.py:20
  96.2 29.2 %collective-permute-start.18 = (bf16[384,768]{1,0:T(8,128)(2,1)S(1)}, bf16[384,768]{1,0:T(8,128)(2,1)S(1)}, u32[]{:S(2)}, u32[]{:S(2)}) collective-permute-start(bf16[384,768]{1,0:T(8,128)(2,1)S(1)} %pad_maximum_fusion.4), channel_id=1, source_target_pairs={{0,8},{4,12},{8,0},{12,4},{16,24},{20,28},{24,16},{28,20},{1,9},{5... | collective-permute-start | bytes 1769480 | tf_op jit(solution)/shard_map/ppermute | solution.py:20
  96.8 28.6 %collective-permute-start.21 = (s32[2,16384]{1,0:T(2,128)S(1)}, s32[2,16384]{1,0:T(2,128)S(1)}, u32[]{:S(2)}, u32[]{:S(2)}) collective-permute-start(s32[2,16384]{1,0:T(2,128)S(1)} %broadcast_select_fusion.37), channel_id=1, source_target_pairs={{0,8},{4,12},{8,0},{12,4},{16,24},{20,28},{24,16},{28,20},{1,9},{5... | collective-permute-start | bytes 393224 | tf_op jit(solution)/shard_map/ppermute | solution.py:20
  125.4 2.5 copy-start.13
  125.4 8.3 %copy-start.7 = (bf16[4,384,768]{2,1,0:T(8,128)(2,1)S(1)}, bf16[4,384,768]{2,1,0:T(8,128)(2,1)}, u32[]{:S(2)}) copy-start(bf16[4,384,768]{2,1,0:T(8,128)(2,1)} %get-tuple-element.161) | copy-start | bytes 7077892
  125.8 9.6 %copy-start.3 = (bf16[4,384,768]{2,1,0:T(8,128)(2,1)}, bf16[4,384,768]{2,1,0:T(8,128)(2,1)S(1)}, u32[]{:S(2)}) copy-start(bf16[4,384,768]{2,1,0:T(8,128)(2,1)S(1)} %pad_maximum_fusion.1.rest_2_) | copy-start | bytes 7077892
  125.8 13.3 %collective-permute-start.23 = (bf16[4,384,768]{2,1,0:T(8,128)(2,1)S(1)}, bf16[4,384,768]{2,1,0:T(8,128)(2,1)S(1)}, u32[]{:S(2)}, u32[]{:S(2)}) collective-permute-start(bf16[4,384,768]{2,1,0:T(8,128)(2,1)S(1)} %pad_maximum_fusion.1.rest_2_), channel_id=1, source_target_pairs={{0,4},{4,0},{8,12},{12,8},{16,20},{20,16},{24,28},{28,24},{1,5},{5... | collective-permute-start | bytes 7077896 | tf_op jit(solution)/shard_map/ppermute | solution.py:20
  128.0 5.8 %collective-permute-start.22 = (bf16[4,384,768]{2,1,0:T(8,128)(2,1)S(1)}, bf16[4,384,768]{2,1,0:T(8,128)(2,1)S(1)}, u32[]{:S(2)}, u32[]{:S(2)}) collective-permute-start(bf16[4,384,768]{2,1,0:T(8,128)(2,1)S(1)} %copy-done.13), channel_id=1, source_target_pairs={{0,4},{4,0},{8,12},{12,8},{16,20},{20,16},{24,28},{28,24},{1,5},{5... | collective-permute-start | bytes 7077896 | tf_op jit(solution)/shard_map/ppermute | solution.py:20
  135.4 39.8 %collective-permute-start.24 = (bf16[384,768]{1,0:T(8,128)(2,1)}, bf16[384,768]{1,0:T(8,128)(2,1)}, u32[]{:S(2)}, u32[]{:S(2)}) collective-permute-start(bf16[384,768]{1,0:T(8,128)(2,1)} %get-tuple-element.174), channel_id=1, source_target_pairs={{0,8},{4,12},{8,0},{12,4},{16,24},{20,28},{24,16},{28,20},{1,9},{5... | collective-permute-start | bytes 1769480 | tf_op jit(solution)/shard_map/ppermute | solution.py:20
  135.9 39.3 %collective-permute-start.25 = (bf16[384,768]{1,0:T(8,128)(2,1)}, bf16[384,768]{1,0:T(8,128)(2,1)}, u32[]{:S(2)}, u32[]{:S(2)}) collective-permute-start(bf16[384,768]{1,0:T(8,128)(2,1)} %get-tuple-element.175), channel_id=1, source_target_pairs={{0,16},{4,20},{8,24},{12,28},{16,0},{20,4},{24,8},{28,12},{1,17},{... | collective-permute-start | bytes 1769480 | tf_op jit(solution)/shard_map/ppermute | solution.py:20
  137.3 37.9 %collective-permute-start.26 = (bf16[384,768]{1,0:T(8,128)(2,1)S(1)}, bf16[384,768]{1,0:T(8,128)(2,1)}, u32[]{:S(2)}, u32[]{:S(2)}) collective-permute-start(bf16[384,768]{1,0:T(8,128)(2,1)S(1)} %get-tuple-element.176), channel_id=1, source_target_pairs={{0,24},{4,28},{8,16},{12,20},{16,8},{20,12},{24,0},{28,4},{1,25},{... | collective-permute-start | bytes 1769480 | tf_op jit(solution)/shard_map/ppermute | solution.py:20
  138.9 36.2 %collective-permute-start.27 = (s32[1,16384]{1,0:T(1,128)S(1)}, s32[1,16384]{1,0:T(1,128)S(1)}, u32[]{:S(2)}, u32[]{:S(2)}) collective-permute-start(s32[1,16384]{1,0:T(1,128)S(1)} %broadcast_select_fusion.34), channel_id=1, source_target_pairs={{0,16},{4,20},{8,24},{12,28},{16,0},{20,4},{24,8},{28,12},{1,17},{... | collective-permute-start | bytes 196616 | tf_op jit(solution)/shard_map/ppermute | solution.py:20
  175.2 6.4 %copy-start.5 = (bf16[4,96,3840]{2,1,0:T(8,128)(2,1)S(1)}, bf16[4,96,3840]{2,1,0:T(8,128)(2,1)}, u32[]{:S(2)}) copy-start(bf16[4,96,3840]{2,1,0:T(8,128)(2,1)} %get-tuple-element.173) | copy-start | bytes 8847364
  175.2 6.4 %collective-permute-start.28 = (bf16[4,96,3840]{2,1,0:T(8,128)(2,1)}, bf16[4,96,3840]{2,1,0:T(8,128)(2,1)S(1)}, u32[]{:S(2)}, u32[]{:S(2)}) collective-permute-start(bf16[4,96,3840]{2,1,0:T(8,128)(2,1)} %get-tuple-element.180), channel_id=1, source_target_pairs={{0,4},{4,0},{8,12},{12,8},{16,20},{20,16},{24,28},{28,24},{1,5},{5... | collective-permute-start | bytes 8847368 | tf_op jit(solution)/shard_map/ppermute | solution.py:20
  175.4 6.9 %collective-permute-start.31 = (s32[1,16384]{1,0:T(1,128)S(1)}, s32[1,16384]{1,0:T(1,128)S(1)}, u32[]{:S(2)}, u32[]{:S(2)}) collective-permute-start(s32[1,16384]{1,0:T(1,128)S(1)} %fusion.17), channel_id=1, source_target_pairs={{0,3},{1,2},{2,1},{3,0},{4,7},{5,6},{6,5},{7,4},{8,11},{9,10},{10,... | collective-permute-start | bytes 196616 | tf_op jit(solution)/shard_map/ppermute | solution.py:24
  177.8 7.8 %collective-permute-start.30 = (s32[1,16384]{1,0:T(1,128)S(1)}, s32[1,16384]{1,0:T(1,128)S(1)}, u32[]{:S(2)}, u32[]{:S(2)}) collective-permute-start(s32[1,16384]{1,0:T(1,128)S(1)} %fusion.17), channel_id=1, source_target_pairs={{0,2},{1,3},{2,0},{3,1},{4,6},{5,7},{6,4},{7,5},{8,10},{9,11},{10,... | collective-permute-start | bytes 196616 | tf_op jit(solution)/shard_map/ppermute | solution.py:24
  178.9 6.7 %collective-permute-start.29 = (s32[1,16384]{1,0:T(1,128)S(1)}, s32[1,16384]{1,0:T(1,128)S(1)}, u32[]{:S(2)}, u32[]{:S(2)}) collective-permute-start(s32[1,16384]{1,0:T(1,128)S(1)} %fusion.17), channel_id=1, source_target_pairs={{0,1},{1,0},{2,3},{3,2},{4,5},{5,4},{6,7},{7,6},{8,9},{9,8},{10,11... | collective-permute-start | bytes 196616 | tf_op jit(solution)/shard_map/ppermute | solution.py:24
  186.4 34.5 %collective-permute-start.35 = (bf16[96,768]{1,0:T(8,128)(2,1)}, bf16[96,768]{1,0:T(8,128)(2,1)S(1)}, u32[]{:S(2)}, u32[]{:S(2)}) collective-permute-start(bf16[96,768]{1,0:T(8,128)(2,1)} %get-tuple-element.279), channel_id=1, source_target_pairs={{0,1},{1,0},{2,3},{3,2},{4,5},{5,4},{6,7},{7,6},{8,9},{9,8},{10,11... | collective-permute-start | bytes 442376 | tf_op jit(solution)/shard_map/ppermute | solution.py:24
  186.4 34.5 %collective-permute-start.36 = (bf16[96,768]{1,0:T(8,128)(2,1)}, bf16[96,768]{1,0:T(8,128)(2,1)S(1)}, u32[]{:S(2)}, u32[]{:S(2)}) collective-permute-start(bf16[96,768]{1,0:T(8,128)(2,1)} %get-tuple-element.280), channel_id=1, source_target_pairs={{0,2},{1,3},{2,0},{3,1},{4,6},{5,7},{6,4},{7,5},{8,10},{9,11},{10,... | collective-permute-start | bytes 442376 | tf_op jit(solution)/shard_map/ppermute | solution.py:24
  189.6 31.3 %collective-permute-start.32 = (bf16[96,3840]{1,0:T(8,128)(2,1)S(1)}, bf16[96,3840]{1,0:T(8,128)(2,1)S(1)}, u32[]{:S(2)}, u32[]{:S(2)}) collective-permute-start(bf16[96,3840]{1,0:T(8,128)(2,1)S(1)} %get-tuple-element.193), channel_id=1, source_target_pairs={{0,8},{4,12},{8,0},{12,4},{16,24},{20,28},{24,16},{28,20},{1,9},{5... | collective-permute-start | bytes 2211848 | tf_op jit(solution)/shard_map/ppermute | solution.py:20
  190.8 30.1 %collective-permute-start.33 = (bf16[96,3840]{1,0:T(8,128)(2,1)S(1)}, bf16[96,3840]{1,0:T(8,128)(2,1)S(1)}, u32[]{:S(2)}, u32[]{:S(2)}) collective-permute-start(bf16[96,3840]{1,0:T(8,128)(2,1)S(1)} %get-tuple-element.194), channel_id=1, source_target_pairs={{0,16},{4,20},{8,24},{12,28},{16,0},{20,4},{24,8},{28,12},{1,17},{... | collective-permute-start | bytes 2211848 | tf_op jit(solution)/shard_map/ppermute | solution.py:20
  191.5 32.4 %collective-permute-start.34 = (bf16[96,3840]{1,0:T(8,128)(2,1)S(1)}, bf16[96,3840]{1,0:T(8,128)(2,1)S(1)}, u32[]{:S(2)}, u32[]{:S(2)}) collective-permute-start(bf16[96,3840]{1,0:T(8,128)(2,1)S(1)} %get-tuple-element.195), channel_id=1, source_target_pairs={{0,24},{4,28},{8,16},{12,20},{16,8},{20,12},{24,0},{28,4},{1,25},{... | collective-permute-start | bytes 2211848 | tf_op jit(solution)/shard_map/ppermute | solution.py:20
  223.8 6.3 %collective-permute-start.39 = (s32[1,16384]{1,0:T(1,128)S(1)}, s32[1,16384]{1,0:T(1,128)S(1)}, u32[]{:S(2)}, u32[]{:S(2)}) collective-permute-start(s32[1,16384]{1,0:T(1,128)S(1)} %add_add_fusion), channel_id=1, source_target_pairs={{0,16},{4,20},{8,24},{12,28},{16,0},{20,4},{24,8},{28,12},{1,17},{... | collective-permute-start | bytes 196616 | tf_op jit(solution)/shard_map/ppermute | solution.py:20
  224.6 7.3 %collective-permute-start.38 = (bf16[96,768]{1,0:T(8,128)(2,1)}, bf16[96,768]{1,0:T(8,128)(2,1)S(1)}, u32[]{:S(2)}, u32[]{:S(2)}) collective-permute-start(bf16[96,768]{1,0:T(8,128)(2,1)} %get-tuple-element.205), channel_id=1, source_target_pairs={{0,3},{1,2},{2,1},{3,0},{4,7},{5,6},{6,5},{7,4},{8,11},{9,10},{10,... | collective-permute-start | bytes 442376 | tf_op jit(solution)/shard_map/ppermute | solution.py:24
  225.8 3.9 %collective-permute-start.37 = (bf16[4,96,2304]{2,1,0:T(8,128)(2,1)}, bf16[4,96,2304]{2,1,0:T(8,128)(2,1)S(1)}, u32[]{:S(2)}, u32[]{:S(2)}) collective-permute-start(bf16[4,96,2304]{2,1,0:T(8,128)(2,1)} %get-tuple-element.202), channel_id=1, source_target_pairs={{0,4},{4,0},{8,12},{12,8},{16,20},{20,16},{24,28},{28,24},{1,5},{5... | collective-permute-start | bytes 5308424 | tf_op jit(solution)/shard_map/ppermute | solution.py:20
  225.8 3.9 %copy-start.8 = (bf16[4,96,2304]{2,1,0:T(8,128)(2,1)S(1)}, bf16[4,96,2304]{2,1,0:T(8,128)(2,1)}, u32[]{:S(2)}) copy-start(bf16[4,96,2304]{2,1,0:T(8,128)(2,1)} %get-tuple-element.192) | copy-start | bytes 5308420
  232.1 5.2 %collective-permute-start.42 = (s32[2,16384]{1,0:T(2,128)S(1)}, s32[2,16384]{1,0:T(2,128)S(1)}, u32[]{:S(2)}, u32[]{:S(2)}) collective-permute-start(s32[2,16384]{1,0:T(2,128)S(1)} %pad_add_fusion.2), channel_id=1, source_target_pairs={{0,8},{4,12},{8,0},{12,4},{16,24},{20,28},{24,16},{28,20},{1,9},{5... | collective-permute-start | bytes 393224 | tf_op jit(solution)/shard_map/ppermute | solution.py:20
  233.5 17.7 %collective-permute-start.40 = (bf16[24,3840]{1,0:T(8,128)(2,1)S(1)}, bf16[24,3840]{1,0:T(8,128)(2,1)S(1)}, u32[]{:S(2)}, u32[]{:S(2)}) collective-permute-start(bf16[24,3840]{1,0:T(8,128)(2,1)S(1)} %get-tuple-element.212), channel_id=1, source_target_pairs={{0,1},{1,0},{2,3},{3,2},{4,5},{5,4},{6,7},{7,6},{8,9},{9,8},{10,11... | collective-permute-start | bytes 552968 | tf_op jit(solution)/shard_map/ppermute | solution.py:24
  233.5 17.7 %collective-permute-start.41 = (bf16[24,3840]{1,0:T(8,128)(2,1)S(1)}, bf16[24,3840]{1,0:T(8,128)(2,1)S(1)}, u32[]{:S(2)}, u32[]{:S(2)}) collective-permute-start(bf16[24,3840]{1,0:T(8,128)(2,1)S(1)} %get-tuple-element.213), channel_id=1, source_target_pairs={{0,2},{1,3},{2,0},{3,1},{4,6},{5,7},{6,4},{7,5},{8,10},{9,11},{10,... | collective-permute-start | bytes 552968 | tf_op jit(solution)/shard_map/ppermute | solution.py:24
  235.3 20.0 %collective-permute-start.43 = (bf16[96,2304]{1,0:T(8,128)(2,1)S(1)}, bf16[96,2304]{1,0:T(8,128)(2,1)S(1)}, u32[]{:S(2)}, u32[]{:S(2)}) collective-permute-start(bf16[96,2304]{1,0:T(8,128)(2,1)S(1)} %get-tuple-element.224), channel_id=1, source_target_pairs={{0,8},{4,12},{8,0},{12,4},{16,24},{20,28},{24,16},{28,20},{1,9},{5... | collective-permute-start | bytes 1327112 | tf_op jit(solution)/shard_map/ppermute | solution.py:20
  235.9 21.3 %collective-permute-start.44 = (bf16[96,2304]{1,0:T(8,128)(2,1)S(1)}, bf16[96,2304]{1,0:T(8,128)(2,1)S(1)}, u32[]{:S(2)}, u32[]{:S(2)}) collective-permute-start(bf16[96,2304]{1,0:T(8,128)(2,1)S(1)} %get-tuple-element.225), channel_id=1, source_target_pairs={{0,16},{4,20},{8,24},{12,28},{16,0},{20,4},{24,8},{28,12},{1,17},{... | collective-permute-start | bytes 1327112 | tf_op jit(solution)/shard_map/ppermute | solution.py:20
  237.3 22.1 %collective-permute-start.45 = (bf16[96,2304]{1,0:T(8,128)(2,1)S(1)}, bf16[96,2304]{1,0:T(8,128)(2,1)S(1)}, u32[]{:S(2)}, u32[]{:S(2)}) collective-permute-start(bf16[96,2304]{1,0:T(8,128)(2,1)S(1)} %get-tuple-element.226), channel_id=1, source_target_pairs={{0,24},{4,28},{8,16},{12,20},{16,8},{20,12},{24,0},{28,4},{1,25},{... | collective-permute-start | bytes 1327112 | tf_op jit(solution)/shard_map/ppermute | solution.py:20
  251.2 1.6 collective-permute-start.46
  251.2 2.3 collective-permute-start.47
  253.6 5.8 %collective-permute-start.48 = (bf16[96,128]{1,0:T(8,128)(2,1)S(1)}, bf16[96,128]{1,0:T(8,128)(2,1)S(1)}, u32[]{:S(2)}, u32[]{:S(2)}) collective-permute-start(bf16[96,128]{1,0:T(8,128)(2,1)S(1)} %get-tuple-element.231), channel_id=1, source_target_pairs={{0,8},{4,12},{8,0},{12,4},{16,24},{20,28},{24,16},{28,20},{1,9},{5... | collective-permute-start | bytes 73736 | tf_op jit(solution)/shard_map/ppermute | solution.py:20
  254.7 4.8 %collective-permute-start.49 = (bf16[96,128]{1,0:T(8,128)(2,1)S(1)}, bf16[96,128]{1,0:T(8,128)(2,1)S(1)}, u32[]{:S(2)}, u32[]{:S(2)}) collective-permute-start(bf16[96,128]{1,0:T(8,128)(2,1)S(1)} %get-tuple-element.232), channel_id=1, source_target_pairs={{0,16},{4,20},{8,24},{12,28},{16,0},{20,4},{24,8},{28,12},{1,17},{... | collective-permute-start | bytes 73736 | tf_op jit(solution)/shard_map/ppermute | solution.py:20
  255.3 4.7 %collective-permute-start.50 = (bf16[96,128]{1,0:T(8,128)(2,1)S(1)}, bf16[96,128]{1,0:T(8,128)(2,1)S(1)}, u32[]{:S(2)}, u32[]{:S(2)}) collective-permute-start(bf16[96,128]{1,0:T(8,128)(2,1)S(1)} %get-tuple-element.233), channel_id=1, source_target_pairs={{0,24},{4,28},{8,16},{12,20},{16,8},{20,12},{24,0},{28,4},{1,25},{... | collective-permute-start | bytes 73736 | tf_op jit(solution)/shard_map/ppermute | solution.py:20
  257.2 19.2 %collective-permute-start.54 = (bf16[24,3840]{1,0:T(8,128)(2,1)S(1)}, bf16[24,3840]{1,0:T(8,128)(2,1)S(1)}, u32[]{:S(2)}, u32[]{:S(2)}) collective-permute-start(bf16[24,3840]{1,0:T(8,128)(2,1)S(1)} %get-tuple-element.244), channel_id=1, source_target_pairs={{0,3},{1,2},{2,1},{3,0},{4,7},{5,6},{6,5},{7,4},{8,11},{9,10},{10,... | collective-permute-start | bytes 552968 | tf_op jit(solution)/shard_map/ppermute | solution.py:24
  260.4 8.9 %collective-permute-start.51 = (bf16[24,2432]{1,0:T(8,128)(2,1)S(1)}, bf16[24,2432]{1,0:T(8,128)(2,1)S(1)}, u32[]{:S(2)}, u32[]{:S(2)}) collective-permute-start(bf16[24,2432]{1,0:T(8,128)(2,1)S(1)} %get-tuple-element.253), channel_id=1, source_target_pairs={{0,1},{1,0},{2,3},{3,2},{4,5},{5,4},{6,7},{7,6},{8,9},{9,8},{10,11... | collective-permute-start | bytes 350216 | tf_op jit(solution)/shard_map/ppermute | solution.py:24
  261.7 13.3 %collective-permute-start.52 = (bf16[24,2432]{1,0:T(8,128)(2,1)S(1)}, bf16[24,2432]{1,0:T(8,128)(2,1)S(1)}, u32[]{:S(2)}, u32[]{:S(2)}) collective-permute-start(bf16[24,2432]{1,0:T(8,128)(2,1)S(1)} %get-tuple-element.287), channel_id=1, source_target_pairs={{0,2},{1,3},{2,0},{3,1},{4,6},{5,7},{6,4},{7,5},{8,10},{9,11},{10,... | collective-permute-start | bytes 350216 | tf_op jit(solution)/shard_map/ppermute | solution.py:24
  263.5 11.5 %collective-permute-start.53 = (bf16[24,2432]{1,0:T(8,128)(2,1)S(1)}, bf16[24,2432]{1,0:T(8,128)(2,1)S(1)}, u32[]{:S(2)}, u32[]{:S(2)}) collective-permute-start(bf16[24,2432]{1,0:T(8,128)(2,1)S(1)} %get-tuple-element.288), channel_id=1, source_target_pairs={{0,3},{1,2},{2,1},{3,0},{4,7},{5,6},{6,5},{7,4},{8,11},{9,10},{10,... | collective-permute-start | bytes 350216 | tf_op jit(solution)/shard_map/ppermute | solution.py:24
  (5 other events, 6.5 us)
